TPU v7x, 32 devices: a whole 2x2x4 slice. The times are simulated.
32 devices in a mesh: dp: 4 (over x, core), ctx: 2 (over y), tensor: 4 (over z).
Axes of the slice: x: 2, y: 2, z: 4, core: 2. Of those that a mesh axis runs over, the one named last changes fastest.
Arguments:
- tokens: bfloat16 [16, 1024, 1024], P('dp', ('ctx', 'tensor')), may hold values from -6 to 6
- seg_starts: int32 [16, 7], P('dp'), may hold values from 0 to 1024, as said below
- norm_gain: float32 [1024], replicated, may hold values from 0.5 to 1.5
- w_query: bfloat16 [1024, 1024], P(('dp', 'ctx'), 'tensor'), may hold values from -0.1875 to 0.1875
- w_key: bfloat16 [1024, 1024], P(('dp', 'ctx'), 'tensor'), may hold values from -0.1875 to 0.1875
- w_value: bfloat16 [1024, 2048], P(('dp', 'ctx'), 'tensor'), may hold values from -0.1875 to 0.1875
- w_gate: bfloat16 [1024, 2048], P(('dp', 'ctx'), 'tensor'), may hold values from -0.1875 to 0.1875
- w_alpha: bfloat16 [1024, 8], P(('dp', 'ctx'), 'tensor'), may hold values from -0.1875 to 0.1875
- w_beta: bfloat16 [1024, 8], P(('dp', 'ctx'), 'tensor'), may hold values from -0.1875 to 0.1875
- conv_query: float32 [4, 1024], replicated, may hold values from -3 to 3
- conv_key: float32 [4, 1024], replicated, may hold values from -3 to 3
- conv_value: float32 [4, 2048], replicated, may hold values from -3 to 3
- a_log: float32 [8], replicated, may hold values from -9 to -2.5
- dt_bias: float32 [8], replicated, may hold values from -1 to 1
- out_gain: float32 [256], replicated, may hold values from 0.5 to 1.5
- w_out: bfloat16 [2048, 1024], P('tensor', ('dp', 'ctx')), may hold values from -0.125 to 0.125
- ffn_gain: float32 [1024], replicated, may hold values from 0.5 to 1.5
- w_ffn_gate: bfloat16 [1024, 2816], P(('dp', 'ctx'), 'tensor'), may hold values from -0.1875 to 0.1875
- w_ffn_up: bfloat16 [1024, 2816], P(('dp', 'ctx'), 'tensor'), may hold values from -0.1875 to 0.1875
- w_ffn_down: bfloat16 [2816, 1024], P('tensor', ('dp', 'ctx')), may hold values from -0.109375 to 0.109375
- d_mixed: bfloat16 [16, 1024, 1024], P('dp', ('ctx', 'tensor')), may hold values from -6 to 6
Outputs:
- mixed: bfloat16 [16, 1024, 1024], P('dp', ('ctx', 'tensor'))
- grad_tokens: float32 [16, 1024, 1024], P('dp', ('ctx', 'tensor'))
- grad_norm_gain: float32 [1024], replicated
- grad_w_query: float32 [1024, 1024], P(('dp', 'ctx'), 'tensor')
- grad_w_key: float32 [1024, 1024], P(('dp', 'ctx'), 'tensor')
- grad_w_value: float32 [1024, 2048], P(('dp', 'ctx'), 'tensor')
- grad_w_gate: float32 [1024, 2048], P(('dp', 'ctx'), 'tensor')
- grad_w_alpha: float32 [1024, 8], P(('dp', 'ctx'), 'tensor')
- grad_w_beta: float32 [1024, 8], P(('dp', 'ctx'), 'tensor')
- grad_conv_query: float32 [4, 1024], replicated
- grad_conv_key: float32 [4, 1024], replicated
- grad_conv_value: float32 [4, 2048], replicated
- grad_a_log: float32 [8], replicated
- grad_dt_bias: float32 [8], replicated
- grad_out_gain: float32 [256], replicated
- grad_w_out: float32 [2048, 1024], P('tensor', ('dp', 'ctx'))
- grad_ffn_gain: float32 [1024], replicated
- grad_w_ffn_gate: float32 [1024, 2816], P(('dp', 'ctx'), 'tensor')
- grad_w_ffn_up: float32 [1024, 2816], P(('dp', 'ctx'), 'tensor')
- grad_w_ffn_down: float32 [2816, 1024], P('tensor', ('dp', 'ctx'))
Inputs may be any that keep to these rules, and one draw needn't show every extreme that they name: `seg_starts`: each row lists the start positions of the documents packed into one sequence, increasing, the first 0; entries after the last document's start equal 1024, and every row has some. In each aligned group of 4 rows (the sequences of one index of dp) one row, drawn from the seed, holds three documents: a first one of at least one token, a second one that starts within the row's first 512 tokens and ends within its last 512 tokens, and a last one of at least one token. In every other row each document has 200 to 2000 tokens except the last, which the sequence's end may cut.
All inputs are finite; a program needn't handle non-finite values.
Results may differ from a plain program's by a relative error of at most 0.014.
Values may be sent and summed in bfloat16 or wider, within the bound.
No kernel may reach another device: no remote copies, remote signals or barrier semaphores. Data moves between devices by JAX's collectives and lax.ppermute only.
A program may use at most 256 MiB of HBM per device.

v0:
```python
from functools import partial

import jax
import jax.numpy as jnp
from jax import lax
from jax.sharding import PartitionSpec as P

BLK = 64


EPS_NORM = 1e-05
EPS_UNIT = 1e-06
FULL_ACCURACY = lax.Precision.HIGHEST


def passed_along(value, axis, steps):
    count = lax.axis_size(axis)
    first, last = (max(0, -steps), min(count, count - steps))
    return lax.ppermute(value, axis, [(source, source + steps) for source in range(first, last)])


def seg_ids(starts, positions):
    return jnp.sum((starts[None, :] <= positions[:, None]).astype(jnp.int32), axis=1) - 1


def rms_rows(values):
    return values * lax.rsqrt(jnp.mean(values * values, axis=-1, keepdims=True) + EPS_NORM)


def unit_rows(values):
    return values * lax.rsqrt(jnp.sum(values * values, axis=-1, keepdims=True) + EPS_UNIT)


def norm_scaled(values, gain):
    return rms_rows(values) * gain


def matmul(left, right):
    return jnp.dot(left, right, preferred_element_type=jnp.float32)


def matmul_left_t(left, right):
    return lax.dot_general(
        left, right, (((0,), (0,)), ((), ())), preferred_element_type=jnp.float32
    )


def matmul_right_t(left, right):
    return lax.dot_general(
        left, right, (((1,), (1,)), ((), ())), preferred_element_type=jnp.float32
    )


def short_conv(extended, taps, seg_ext):
    count = taps.shape[0]
    length = extended.shape[0] - (count - 1)
    target = seg_ext[count - 1 :]
    total = jnp.zeros((length, extended.shape[1]), extended.dtype)
    for offset in range(count):
        first = count - 1 - offset
        shifted = extended[first : first + length]
        inside = (seg_ext[first : first + length] == target).astype(extended.dtype)
        total = total + taps[offset] * shifted * inside[:, None]
    return total


def prepare(
    ext_query,
    ext_key,
    ext_value,
    pre_alpha,
    pre_beta,
    taps_query,
    taps_key,
    taps_value,
    log_scale,
    decay_bias,
    seg_ext,
):
    length, heads = pre_alpha.shape
    query_rows = jax.nn.silu(short_conv(ext_query, taps_query, seg_ext)).reshape(length, heads, -1)
    key_rows = jax.nn.silu(short_conv(ext_key, taps_key, seg_ext)).reshape(length, heads, -1)
    values = jax.nn.silu(short_conv(ext_value, taps_value, seg_ext)).reshape(length, heads, -1)
    query_rows = unit_rows(query_rows) * query_rows.shape[-1] ** (-0.5)
    key_rows = unit_rows(key_rows)
    decay = jnp.transpose(-jnp.exp(log_scale) * jax.nn.softplus(pre_alpha + decay_bias))
    strength = jnp.transpose(jax.nn.sigmoid(pre_beta))
    return (
        jnp.transpose(query_rows, (1, 0, 2)),
        jnp.transpose(key_rows, (1, 0, 2)),
        jnp.transpose(values, (1, 0, 2)),
        decay,
        strength,
    )


def delta_block(
    running_state, query_rows, key_rows, values, decay, strength, seg, seg_prev, outputs
):
    width = seg.shape[0]
    cumul = jnp.cumsum(decay, axis=1)
    same_doc = seg[:, None] == seg[None, :]
    lower = jnp.tri(width, dtype=bool)
    strict = jnp.tri(width, k=-1, dtype=bool)
    allowed = (lower & same_doc)[None]
    spread = cumul[:, :, None] - cumul[:, None, :]
    within = jnp.exp(jnp.where(allowed, spread, 0.0)) * allowed
    carried = (seg == seg_prev).astype(cumul.dtype)
    opening_state = jnp.exp(cumul) * carried[None, :]
    inner = jnp.einsum("hik,hjk->hij", key_rows, key_rows, precision=FULL_ACCURACY)
    system = (
        jnp.eye(width, dtype=cumul.dtype)[None]
        + strength[:, :, None] * within * inner * strict[None]
    )
    known_state = jnp.einsum("yzd,ydf->yzf", key_rows, running_state, precision=FULL_ACCURACY)
    right_side = strength[:, :, None] * (values - opening_state[:, :, None] * known_state)
    state_update = jax.scipy.linalg.solve_triangular(
        system, right_side, lower=True, unit_diagonal=True
    )
    last_doc = seg == seg[-1]
    closing_state = jnp.exp(jnp.where(last_doc[None, :], cumul[:, -1:] - cumul, 0.0)) * last_doc[
        None, :
    ].astype(cumul.dtype)
    updated_state = opening_state[:, -1][:, None, None] * running_state + jnp.einsum(
        "nqu,nql->nul", closing_state[:, :, None] * key_rows, state_update, precision=FULL_ACCURACY
    )
    scores = jnp.einsum("hik,hjk->hij", query_rows, key_rows, precision=FULL_ACCURACY) * within
    layer_result = opening_state[:, :, None] * jnp.einsum(
        "yzd,ydf->yzf", query_rows, running_state, precision=FULL_ACCURACY
    )
    layer_result = layer_result + jnp.einsum(
        "hij,hjv->hiv", scores, state_update, precision=FULL_ACCURACY
    )
    return (updated_state, layer_result)


def delta_run(running_state, query_rows, key_rows, values, decay, strength, seg, seg_before, block):
    heads, length = decay.shape
    count = length // block

    def split_blocks(array):
        shaped = array.reshape((heads, count, block) + array.shape[2:])
        return jnp.moveaxis(shaped, 1, 0)

    step_block = jax.checkpoint(partial(delta_block, outputs=True))

    def one_block(carry_state, items):
        return step_block(
            carry_state, items[0], items[1], items[2], items[3], items[4], items[5], items[6]
        )

    items = (
        split_blocks(query_rows),
        split_blocks(key_rows),
        split_blocks(values),
        split_blocks(decay),
        split_blocks(strength),
        seg.reshape(count, block),
        seg_before,
    )
    final_state, pieces = lax.scan(one_block, running_state, items)
    return (final_state, jnp.moveaxis(pieces, 0, 1).reshape(heads, length, -1))


def run_all(states, query_rows, key_rows, values, decay, strength, seg, seg_before):

    def one_sequence(
        state, query_part, key_part, value_part, decay_part, strength_part, seg_part, before_part
    ):
        return delta_run(
            state,
            query_part,
            key_part,
            value_part,
            decay_part,
            strength_part,
            seg_part,
            before_part,
            BLK,
        )

    return jax.vmap(one_sequence)(
        states, query_rows, key_rows, values, decay, strength, seg, seg_before
    )


def gate_norm(mixer_out, pre_gate, gain):
    heads, length, width = mixer_out.shape
    normed = rms_rows(mixer_out) * gain
    merged = jnp.transpose(normed, (1, 0, 2)).reshape(length, heads * width)
    return merged * jax.nn.silu(pre_gate)


def apply_map(linear, running_state):
    return jnp.einsum("hij,hjv->hiv", linear, running_state, precision=FULL_ACCURACY)


def shards(
    tokens,
    seg_starts,
    norm_gain,
    w_query,
    w_key,
    w_value,
    w_gate,
    w_alpha,
    w_beta,
    conv_query,
    conv_key,
    conv_value,
    a_log,
    dt_bias,
    out_gain,
    w_out,
    ffn_gain,
    w_ffn_gate,
    w_ffn_up,
    w_ffn_down,
    d_mixed,
):
    lanes = lax.axis_size("tensor")
    lane = lax.axis_index("tensor")
    place = lax.axis_index("ctx")
    taps = conv_query.shape[0]
    rim_rows = taps - 1
    seq_count, own_rows, model_width = tokens.shape
    block_rows = own_rows * lanes
    flat_rows = seq_count * block_rows
    key_cols = w_query.shape[1]
    value_cols = w_value.shape[1]
    local_heads = w_alpha.shape[1]
    token_rows, cot_rows = (
        lax.all_gather(tokens, "tensor", axis=1, tiled=True),
        lax.all_gather(d_mixed, "tensor", axis=1, tiled=True),
    )
    gathered = (
        lax.all_gather(w_query, ("dp", "ctx"), axis=0, tiled=True),
        lax.all_gather(w_key, ("dp", "ctx"), axis=0, tiled=True),
        lax.all_gather(w_value, ("dp", "ctx"), axis=0, tiled=True),
        lax.all_gather(w_gate, ("dp", "ctx"), axis=0, tiled=True),
        lax.all_gather(w_alpha, ("dp", "ctx"), axis=0, tiled=True),
        lax.all_gather(w_beta, ("dp", "ctx"), axis=0, tiled=True),
        lax.all_gather(w_out, ("dp", "ctx"), axis=1, tiled=True),
        lax.all_gather(w_ffn_gate, ("dp", "ctx"), axis=0, tiled=True),
        lax.all_gather(w_ffn_up, ("dp", "ctx"), axis=0, tiled=True),
        lax.all_gather(w_ffn_down, ("dp", "ctx"), axis=1, tiled=True),
    )
    (
        full_query,
        full_key,
        full_value,
        full_gate,
        full_alpha,
        full_beta,
        full_out,
        full_ffn_gate,
        full_ffn_up,
        full_ffn_down,
    ) = gathered
    inputs = token_rows.astype(jnp.float32).reshape(flat_rows, model_width)
    cot_flat = cot_rows.reshape(flat_rows, model_width)
    own_inputs = tokens.astype(jnp.float32)
    normed = (rms_rows(inputs) * norm_gain).astype(jnp.bfloat16)
    seq_shape = (seq_count, block_rows, -1)
    pre_query = matmul(normed, full_query).reshape(seq_shape)
    pre_key = matmul(normed, full_key).reshape(seq_shape)
    pre_value = matmul(normed, full_value).reshape(seq_shape)
    pre_gate = matmul(normed, full_gate).reshape(seq_shape)
    pre_alpha = matmul(normed, full_alpha).reshape(seq_shape)
    pre_beta = matmul(normed, full_beta).reshape(seq_shape)
    tail_start = block_rows - rim_rows
    rim_query, rim_key, rim_value = passed_along(
        (pre_query[:, tail_start:], pre_key[:, tail_start:], pre_value[:, tail_start:]), "ctx", 1
    )
    base = place * block_rows
    ext_positions = base + jnp.arange(-rim_rows, block_rows, dtype=jnp.int32)
    seg_ext = jax.vmap(seg_ids, in_axes=(0, None))(seg_starts, ext_positions)
    seg = seg_ext[:, rim_rows:]
    seg_before = jax.vmap(seg_ids, in_axes=(0, None))(
        seg_starts, base + jnp.arange(0, block_rows, BLK, dtype=jnp.int32) - 1
    )
    taps_query = lax.dynamic_slice_in_dim(conv_query, lane * key_cols, key_cols, 1)
    taps_key = lax.dynamic_slice_in_dim(conv_key, lane * key_cols, key_cols, 1)
    taps_value = lax.dynamic_slice_in_dim(conv_value, lane * value_cols, value_cols, 1)
    log_scale = lax.dynamic_slice_in_dim(a_log, lane * local_heads, local_heads, 0)
    decay_bias = lax.dynamic_slice_in_dim(dt_bias, lane * local_heads, local_heads, 0)

    def prep_local(
        ext_query,
        ext_key,
        ext_value,
        alpha_part,
        beta_part,
        conv_q_part,
        conv_k_part,
        conv_v_part,
        log_part,
        bias_part,
    ):
        return jax.vmap(prepare, in_axes=(0, 0, 0, 0, 0, None, None, None, None, None, 0))(
            ext_query,
            ext_key,
            ext_value,
            alpha_part,
            beta_part,
            conv_q_part,
            conv_k_part,
            conv_v_part,
            log_part,
            bias_part,
            seg_ext,
        )

    prepared, prep_pullback = jax.vjp(
        prep_local,
        jnp.concatenate([rim_query, pre_query], 1),
        jnp.concatenate([rim_key, pre_key], 1),
        jnp.concatenate([rim_value, pre_value], 1),
        pre_alpha,
        pre_beta,
        taps_query,
        taps_key,
        taps_value,
        log_scale,
        decay_bias,
    )
    query_rows, key_rows, values, decay, strength = prepared
    key_size = key_rows.shape[-1]
    value_size = values.shape[-1]
    flat_heads = seq_count * local_heads
    identity_map = jnp.broadcast_to(
        jnp.eye(key_size, dtype=jnp.float32), (seq_count, local_heads, key_size, key_size)
    )
    zeros_state = jnp.zeros((seq_count, local_heads, key_size, value_size), jnp.float32)
    start_ext = jnp.concatenate([zeros_state, identity_map], 3)
    values_ext = jnp.concatenate(
        [values, jnp.zeros((seq_count, local_heads, block_rows, key_size), jnp.float32)], 3
    )
    end_ext, out_ext = run_all(
        start_ext, query_rows, key_rows, values_ext, decay, strength, seg, seg_before
    )
    offset_part = end_ext[..., :value_size].reshape(flat_heads, key_size, value_size)
    linear_part = end_ext[..., value_size:].reshape(flat_heads, key_size, key_size)
    state_response = out_ext[..., value_size:]
    flat_zeros = jnp.zeros((flat_heads, key_size, value_size), jnp.float32)

    def forward_turn(turn, incoming):
        return passed_along(apply_map(linear_part, incoming) + offset_part, "ctx", 1)

    flat_state_in = lax.fori_loop(0, lax.axis_size("ctx") - 1, forward_turn, flat_zeros)
    state_in = flat_state_in.reshape(seq_count, local_heads, key_size, value_size)

    def mixer(query_part, key_part, value_part, decay_part, strength_part, state_part):
        return run_all(
            state_part, query_part, key_part, value_part, decay_part, strength_part, seg, seg_before
        )

    mixed_pair, mixer_pullback = jax.vjp(
        mixer, query_rows, key_rows, values, decay, strength, state_in
    )
    mixer_out = mixed_pair[1]

    def gate_all(mixer_part, gate_part, gain):
        return jax.vmap(gate_norm, in_axes=(0, 0, None))(mixer_part, gate_part, gain).reshape(
            flat_rows, -1
        )

    gated, gate_pullback = jax.vjp(gate_all, mixer_out, pre_gate, out_gain)
    gated_low = gated.astype(jnp.bfloat16)
    attn_terms = matmul(gated_low, full_out)
    middle = inputs + lax.psum(attn_terms, "tensor")
    normed_two = (rms_rows(middle) * ffn_gain).astype(jnp.bfloat16)
    own_middle = lax.dynamic_slice_in_dim(
        middle.reshape(seq_count, block_rows, model_width), lane * own_rows, own_rows, 1
    )
    gate_pre = matmul(normed_two, full_ffn_gate)
    up_pre = matmul(normed_two, full_ffn_up)
    hidden = (jax.nn.silu(gate_pre) * up_pre).astype(jnp.bfloat16)
    ffn_own = lax.psum_scatter(
        matmul(hidden, full_ffn_down)
        .reshape(seq_count, block_rows, model_width)
        .astype(jnp.bfloat16),
        "tensor",
        scatter_dimension=1,
        tiled=True,
    ).astype(jnp.float32)
    mixed = (own_middle + ffn_own).astype(jnp.bfloat16)
    grad_ffn_down = matmul_left_t(hidden, cot_flat)
    d_hidden = matmul_right_t(cot_flat, full_ffn_down)
    sigma = jax.nn.sigmoid(gate_pre)
    d_gate_pre = (d_hidden * up_pre * sigma * (1.0 + gate_pre * (1.0 - sigma))).astype(jnp.bfloat16)
    d_up_pre = (d_hidden * gate_pre * sigma).astype(jnp.bfloat16)
    grad_ffn_gate = matmul_left_t(normed_two, d_gate_pre)
    grad_ffn_up = matmul_left_t(normed_two, d_up_pre)
    ffn_terms = matmul_right_t(d_gate_pre, full_ffn_gate) + matmul_right_t(d_up_pre, full_ffn_up)
    d_normed_two = lax.psum(ffn_terms, "tensor")
    unused_norm, norm_two_pullback = jax.vjp(norm_scaled, middle, ffn_gain)
    d_middle = cot_flat.astype(jnp.float32) + norm_two_pullback(d_normed_two)[0]
    own_d_normed_two = lax.dynamic_slice_in_dim(
        d_normed_two.reshape(seq_count, block_rows, model_width), lane * own_rows, own_rows, 1
    )
    own_d_middle = lax.dynamic_slice_in_dim(
        d_middle.reshape(seq_count, block_rows, model_width), lane * own_rows, own_rows, 1
    )
    d_branch = d_middle.astype(jnp.bfloat16)
    grad_ffn_gain = jnp.sum(own_d_normed_two * rms_rows(own_middle), axis=(0, 1))
    grad_out = matmul_left_t(gated_low, d_branch)
    d_gated = matmul_right_t(d_branch, full_out)
    mixer_gradient, d_pre_gate, grad_out_gain = gate_pullback(d_gated)
    local_portion = jnp.einsum(
        "sbyu,sbyl->sbul", state_response, mixer_gradient, precision=FULL_ACCURACY
    ).reshape(flat_heads, key_size, value_size)
    linear_back = jnp.swapaxes(linear_part, 1, 2)

    def backward_turn(turn, incoming):
        return passed_along(apply_map(linear_back, incoming) + local_portion, "ctx", -1)

    flat_state_out = lax.fori_loop(0, lax.axis_size("ctx") - 1, backward_turn, flat_zeros)
    d_state_out = flat_state_out.reshape(seq_count, local_heads, key_size, value_size)
    d_query, d_keys, d_values, d_decay, d_strength, unused_state = mixer_pullback(
        (d_state_out, mixer_gradient)
    )
    (
        d_ext_query,
        d_ext_key,
        d_ext_value,
        d_pre_alpha,
        d_pre_beta,
        d_taps_query,
        d_taps_key,
        d_taps_value,
        d_log_scale,
        d_decay_bias,
    ) = prep_pullback((d_query, d_keys, d_values, d_decay, d_strength))
    back_query, back_key, back_value = (
        passed_along(d_ext_query[:, :rim_rows].astype(jnp.bfloat16), "ctx", -1).astype(jnp.float32),
        passed_along(d_ext_key[:, :rim_rows].astype(jnp.bfloat16), "ctx", -1).astype(jnp.float32),
        passed_along(d_ext_value[:, :rim_rows].astype(jnp.bfloat16), "ctx", -1).astype(jnp.float32),
    )
    tail_pad = ((0, 0), (block_rows - rim_rows, 0), (0, 0))
    d_pre_query = (
        (d_ext_query[:, rim_rows:] + jnp.pad(back_query, tail_pad))
        .astype(jnp.bfloat16)
        .reshape(flat_rows, -1)
    )
    d_pre_key = (
        (d_ext_key[:, rim_rows:] + jnp.pad(back_key, tail_pad))
        .astype(jnp.bfloat16)
        .reshape(flat_rows, -1)
    )
    d_pre_value = (
        (d_ext_value[:, rim_rows:] + jnp.pad(back_value, tail_pad))
        .astype(jnp.bfloat16)
        .reshape(flat_rows, -1)
    )
    d_pre_gate = d_pre_gate.astype(jnp.bfloat16).reshape(flat_rows, -1)
    d_pre_alpha = d_pre_alpha.astype(jnp.bfloat16).reshape(flat_rows, -1)
    d_pre_beta = d_pre_beta.astype(jnp.bfloat16).reshape(flat_rows, -1)
    grad_query = matmul_left_t(normed, d_pre_query)
    grad_key = matmul_left_t(normed, d_pre_key)
    grad_value = matmul_left_t(normed, d_pre_value)
    grad_gate = matmul_left_t(normed, d_pre_gate)
    grad_alpha = matmul_left_t(normed, d_pre_alpha)
    grad_beta = matmul_left_t(normed, d_pre_beta)
    d_normed = matmul_right_t(d_pre_query, full_query) + matmul_right_t(d_pre_key, full_key)
    d_normed = (
        d_normed + matmul_right_t(d_pre_value, full_value) + matmul_right_t(d_pre_gate, full_gate)
    )
    d_normed = (
        d_normed + matmul_right_t(d_pre_alpha, full_alpha) + matmul_right_t(d_pre_beta, full_beta)
    )
    own_d_normed = lax.psum_scatter(
        d_normed.reshape(seq_count, block_rows, model_width).astype(jnp.bfloat16),
        "tensor",
        scatter_dimension=1,
        tiled=True,
    ).astype(jnp.float32)
    unused_first, norm_pullback = jax.vjp(norm_scaled, own_inputs, norm_gain)
    d_inputs_part, grad_norm_gain = norm_pullback(own_d_normed)
    grad_tokens = own_d_middle + d_inputs_part
    conv_query_full = lax.dynamic_update_slice_in_dim(
        jnp.zeros(conv_query.shape, jnp.float32), d_taps_query, lane * key_cols, 1
    )
    conv_key_full = lax.dynamic_update_slice_in_dim(
        jnp.zeros(conv_key.shape, jnp.float32), d_taps_key, lane * key_cols, 1
    )
    conv_value_full = lax.dynamic_update_slice_in_dim(
        jnp.zeros(conv_value.shape, jnp.float32), d_taps_value, lane * value_cols, 1
    )
    log_full = lax.dynamic_update_slice_in_dim(
        jnp.zeros(a_log.shape, jnp.float32), d_log_scale, lane * local_heads, 0
    )
    bias_full = lax.dynamic_update_slice_in_dim(
        jnp.zeros(dt_bias.shape, jnp.float32), d_decay_bias, lane * local_heads, 0
    )
    small_sums = lax.psum(
        (
            grad_norm_gain,
            grad_ffn_gain,
            grad_out_gain,
            conv_query_full,
            conv_key_full,
            conv_value_full,
            log_full,
            bias_full,
        ),
        ("dp", "ctx", "tensor"),
    )
    weight_sums = (
        lax.psum_scatter(grad_query, ("dp", "ctx"), scatter_dimension=0, tiled=True),
        lax.psum_scatter(grad_key, ("dp", "ctx"), scatter_dimension=0, tiled=True),
        lax.psum_scatter(grad_value, ("dp", "ctx"), scatter_dimension=0, tiled=True),
        lax.psum_scatter(grad_gate, ("dp", "ctx"), scatter_dimension=0, tiled=True),
        lax.psum_scatter(grad_alpha, ("dp", "ctx"), scatter_dimension=0, tiled=True),
        lax.psum_scatter(grad_beta, ("dp", "ctx"), scatter_dimension=0, tiled=True),
        lax.psum_scatter(grad_out, ("dp", "ctx"), scatter_dimension=1, tiled=True),
        lax.psum_scatter(grad_ffn_gate, ("dp", "ctx"), scatter_dimension=0, tiled=True),
        lax.psum_scatter(grad_ffn_up, ("dp", "ctx"), scatter_dimension=0, tiled=True),
        lax.psum_scatter(grad_ffn_down, ("dp", "ctx"), scatter_dimension=1, tiled=True),
    )
    return (
        mixed,
        grad_tokens,
        small_sums[0],
        weight_sums[0],
        weight_sums[1],
        weight_sums[2],
        weight_sums[3],
        weight_sums[4],
        weight_sums[5],
        small_sums[3],
        small_sums[4],
        small_sums[5],
        small_sums[6],
        small_sums[7],
        small_sums[2],
        weight_sums[6],
        small_sums[1],
        weight_sums[7],
        weight_sums[8],
        weight_sums[9],
    )


def solution(mesh):
    placed = (
        P("dp", ("ctx", "tensor"), None),
        P("dp", None),
        P(),
        P(("dp", "ctx"), "tensor"),
        P(("dp", "ctx"), "tensor"),
        P(("dp", "ctx"), "tensor"),
        P(("dp", "ctx"), "tensor"),
        P(("dp", "ctx"), "tensor"),
        P(("dp", "ctx"), "tensor"),
        P(),
        P(),
        P(),
        P(),
        P(),
        P(),
        P("tensor", ("dp", "ctx")),
        P(),
        P(("dp", "ctx"), "tensor"),
        P(("dp", "ctx"), "tensor"),
        P("tensor", ("dp", "ctx")),
        P("dp", ("ctx", "tensor"), None),
    )
    return jax.shard_map(
        shards,
        mesh=mesh,
        in_specs=placed,
        out_specs=(
            P("dp", ("ctx", "tensor"), None),
            P("dp", ("ctx", "tensor"), None),
            P(),
            P(("dp", "ctx"), "tensor"),
            P(("dp", "ctx"), "tensor"),
            P(("dp", "ctx"), "tensor"),
            P(("dp", "ctx"), "tensor"),
            P(("dp", "ctx"), "tensor"),
            P(("dp", "ctx"), "tensor"),
            P(),
            P(),
            P(),
            P(),
            P(),
            P(),
            P("tensor", ("dp", "ctx")),
            P(),
            P(("dp", "ctx"), "tensor"),
            P(("dp", "ctx"), "tensor"),
            P("tensor", ("dp", "ctx")),
        ),
        check_vma=False,
    )
```

profile of v0, /device:TPU:8, one launch (start us, length us, event | category | flops | bytes accessed | tf_op | source)
XLA Modules:
  0.0 3395.5 jit_solution(492284208812887163)
XLA Ops:
  36.6 17.7 all_gather.38
  54.4 17.7 all_gather.41
  74.2 14.6 all-gather.9.cloned.1.call-done
  171.4 462.7 %while.60 = (s32[]{:T(128)}, f32[4,2,128,384]{3,2,1,0:T(8,128)S(1)}, f32[8,4,2,64,384]{4,3,0,2,1:T(8,128)}, f32[8,4,2,64]{3,2,1,0:T(2,128)}, s32[8,4,64]{2,1,0:T...) while((s32[]{:T(128)}, ...), condition=%wide.region_7.8_spmd, body=%wide.region_5.7_spmd.sunk | while | flops 1310996992 | bytes 19379984 | solution.py:161
  182.9 39.3 %custom-call.28 = f32[4,2,1,64,64]{3,4,2,1,0:T(8,128)S(1)} custom-call(f32[4,2,1,64,64]{4,3,2,1,0:T(8,128)S(1)} %fusion.464), custom_call_target="InvertDiagBlocksLowerTriangular" | custom-call | tf_op jit(solution)/shard_map/vmap()/while/body/eval_jaxpr/checkpoint/jit(_solve_triangular)/vmap()/triangular_solve | solution.py:117
  240.6 39.3 %custom-call.28 = f32[4,2,1,64,64]{3,4,2,1,0:T(8,128)S(1)} custom-call(f32[4,2,1,64,64]{4,3,2,1,0:T(8,128)S(1)} %fusion.464), custom_call_target="InvertDiagBlocksLowerTriangular" | custom-call | tf_op jit(solution)/shard_map/vmap()/while/body/eval_jaxpr/checkpoint/jit(_solve_triangular)/vmap()/triangular_solve | solution.py:117
  298.4 39.3 %custom-call.28 = f32[4,2,1,64,64]{3,4,2,1,0:T(8,128)S(1)} custom-call(f32[4,2,1,64,64]{4,3,2,1,0:T(8,128)S(1)} %fusion.464), custom_call_target="InvertDiagBlocksLowerTriangular" | custom-call | tf_op jit(solution)/shard_map/vmap()/while/body/eval_jaxpr/checkpoint/jit(_solve_triangular)/vmap()/triangular_solve | solution.py:117
  356.2 39.3 %custom-call.28 = f32[4,2,1,64,64]{3,4,2,1,0:T(8,128)S(1)} custom-call(f32[4,2,1,64,64]{4,3,2,1,0:T(8,128)S(1)} %fusion.464), custom_call_target="InvertDiagBlocksLowerTriangular" | custom-call | tf_op jit(solution)/shard_map/vmap()/while/body/eval_jaxpr/checkpoint/jit(_solve_triangular)/vmap()/triangular_solve | solution.py:117
  414.0 39.3 %custom-call.28 = f32[4,2,1,64,64]{3,4,2,1,0:T(8,128)S(1)} custom-call(f32[4,2,1,64,64]{4,3,2,1,0:T(8,128)S(1)} %fusion.464), custom_call_target="InvertDiagBlocksLowerTriangular" | custom-call | tf_op jit(solution)/shard_map/vmap()/while/body/eval_jaxpr/checkpoint/jit(_solve_triangular)/vmap()/triangular_solve | solution.py:117
  471.8 39.3 %custom-call.28 = f32[4,2,1,64,64]{3,4,2,1,0:T(8,128)S(1)} custom-call(f32[4,2,1,64,64]{4,3,2,1,0:T(8,128)S(1)} %fusion.464), custom_call_target="InvertDiagBlocksLowerTriangular" | custom-call | tf_op jit(solution)/shard_map/vmap()/while/body/eval_jaxpr/checkpoint/jit(_solve_triangular)/vmap()/triangular_solve | solution.py:117
  529.6 39.3 %custom-call.28 = f32[4,2,1,64,64]{3,4,2,1,0:T(8,128)S(1)} custom-call(f32[4,2,1,64,64]{4,3,2,1,0:T(8,128)S(1)} %fusion.464), custom_call_target="InvertDiagBlocksLowerTriangular" | custom-call | tf_op jit(solution)/shard_map/vmap()/while/body/eval_jaxpr/checkpoint/jit(_solve_triangular)/vmap()/triangular_solve | solution.py:117
  587.3 39.3 %custom-call.28 = f32[4,2,1,64,64]{3,4,2,1,0:T(8,128)S(1)} custom-call(f32[4,2,1,64,64]{4,3,2,1,0:T(8,128)S(1)} %fusion.464), custom_call_target="InvertDiagBlocksLowerTriangular" | custom-call | tf_op jit(solution)/shard_map/vmap()/while/body/eval_jaxpr/checkpoint/jit(_solve_triangular)/vmap()/triangular_solve | solution.py:117
  642.2 22.4 collective-permute-done.3
  667.1 448.2 %while.62 = (s32[]{:T(128)}, f32[4,2,128,256]{3,2,1,0:T(8,128)S(1)}, f32[8,4,2,64,256]{4,3,0,2,1:T(8,128)}, f32[8,4,2,128,256]{4,3,2,1,0:T(8,128)}, f32[8,4,2,64...) while((s32[]{:T(128)}, ...), condition=%wide.region_10.12_spmd.clone, body=%wide.region_8.11_spmd.clone.sunk | while | flops 907758144 | bytes 13745097 | solution.py:161
  677.4 39.3 %custom-call.30 = f32[4,2,1,64,64]{3,4,2,1,0:T(8,128)S(1)} custom-call(f32[4,2,1,64,64]{4,3,2,1,0:T(8,128)S(1)} %fusion.537), custom_call_target="InvertDiagBlocksLowerTriangular" | custom-call | tf_op jit(solution)/shard_map/jvp(vmap())/while/body/eval_jaxpr/jit(_solve_triangular)/vmap()/triangular_solve/custom-call.0 | solution.py:117
  733.4 39.3 %custom-call.30 = f32[4,2,1,64,64]{3,4,2,1,0:T(8,128)S(1)} custom-call(f32[4,2,1,64,64]{4,3,2,1,0:T(8,128)S(1)} %fusion.537), custom_call_target="InvertDiagBlocksLowerTriangular" | custom-call | tf_op jit(solution)/shard_map/jvp(vmap())/while/body/eval_jaxpr/jit(_solve_triangular)/vmap()/triangular_solve/custom-call.0 | solution.py:117
  789.5 39.3 %custom-call.30 = f32[4,2,1,64,64]{3,4,2,1,0:T(8,128)S(1)} custom-call(f32[4,2,1,64,64]{4,3,2,1,0:T(8,128)S(1)} %fusion.537), custom_call_target="InvertDiagBlocksLowerTriangular" | custom-call | tf_op jit(solution)/shard_map/jvp(vmap())/while/body/eval_jaxpr/jit(_solve_triangular)/vmap()/triangular_solve/custom-call.0 | solution.py:117
  845.5 39.3 %custom-call.30 = f32[4,2,1,64,64]{3,4,2,1,0:T(8,128)S(1)} custom-call(f32[4,2,1,64,64]{4,3,2,1,0:T(8,128)S(1)} %fusion.537), custom_call_target="InvertDiagBlocksLowerTriangular" | custom-call | tf_op jit(solution)/shard_map/jvp(vmap())/while/body/eval_jaxpr/jit(_solve_triangular)/vmap()/triangular_solve/custom-call.0 | solution.py:117
  901.4 39.3 %custom-call.30 = f32[4,2,1,64,64]{3,4,2,1,0:T(8,128)S(1)} custom-call(f32[4,2,1,64,64]{4,3,2,1,0:T(8,128)S(1)} %fusion.537), custom_call_target="InvertDiagBlocksLowerTriangular" | custom-call | tf_op jit(solution)/shard_map/jvp(vmap())/while/body/eval_jaxpr/jit(_solve_triangular)/vmap()/triangular_solve/custom-call.0 | solution.py:117
  957.4 39.3 %custom-call.30 = f32[4,2,1,64,64]{3,4,2,1,0:T(8,128)S(1)} custom-call(f32[4,2,1,64,64]{4,3,2,1,0:T(8,128)S(1)} %fusion.537), custom_call_target="InvertDiagBlocksLowerTriangular" | custom-call | tf_op jit(solution)/shard_map/jvp(vmap())/while/body/eval_jaxpr/jit(_solve_triangular)/vmap()/triangular_solve/custom-call.0 | solution.py:117
  1013.5 39.3 %custom-call.30 = f32[4,2,1,64,64]{3,4,2,1,0:T(8,128)S(1)} custom-call(f32[4,2,1,64,64]{4,3,2,1,0:T(8,128)S(1)} %fusion.537), custom_call_target="InvertDiagBlocksLowerTriangular" | custom-call | tf_op jit(solution)/shard_map/jvp(vmap())/while/body/eval_jaxpr/jit(_solve_triangular)/vmap()/triangular_solve/custom-call.0 | solution.py:117
  1069.4 39.3 %custom-call.30 = f32[4,2,1,64,64]{3,4,2,1,0:T(8,128)S(1)} custom-call(f32[4,2,1,64,64]{4,3,2,1,0:T(8,128)S(1)} %fusion.537), custom_call_target="InvertDiagBlocksLowerTriangular" | custom-call | tf_op jit(solution)/shard_map/jvp(vmap())/while/body/eval_jaxpr/jit(_solve_triangular)/vmap()/triangular_solve/custom-call.0 | solution.py:117
  1142.8 286.9 %all-reduce.36.cloned.1.call-done = f32[2048,1024]{1,0:T(8,128)} async-done(((f32[2048,1024]{1,0:T(8,128)}), f32[2048,1024]{1,0:T(8,128)}) %all-reduce.36.cloned.1.call-update) | async-done | bytes 8388624 | tf_op jit(solution)/shard_map/psum | solution.py:371
  1441.7 16.2 all-gather.17.cloned.1.call-done
  1466.2 18.9 all-gather.19.cloned.1.call-done
  1493.3 19.0 all-gather.21.cloned.1.call-done
  1512.3 79.7 %all-gather.23.cloned.1.call-done = bf16[4,512,1024]{2,1,0:T(8,128)(2,1)} async-done(((bf16[4,128,1024]{2,1,0:T(8,128)(2,1)}), bf16[4,512,1024]{2,1,0:T(8,128)(2,1)}) %all-gather.23.cloned.1.call-update) | async-done | bytes 4194320 | tf_op jit(solution)/shard_map/all_gather | solution.py:234
  1616.8 286.6 %all-reduce.38.cloned.1.call-done = f32[2048,1024]{1,0:T(8,128)} async-done(((f32[2048,1024]{1,0:T(8,128)}), f32[2048,1024]{1,0:T(8,128)}) %all-reduce.38.cloned.1.call-update) | async-done | bytes 8388624 | tf_op jit(solution)/shard_map/psum | solution.py:396
  1973.9 706.4 %while.61 = (s32[]{:T(128)}, f32[4,2,128,256]{3,2,1,0:T(8,128)S(1)}, f32[8,4,2,64,128]{4,3,0,2,1:T(8,128)}, f32[8,4,2,64,128]{4,3,0,2,1:T(8,128)}, f32[8,4,2,64,...) while((s32[]{:T(128)}, ...), condition=%wide.region_30.32_spmd, body=%wide.region_18.31_spmd.sunk | while | flops 2447722496 | bytes 57774436 | solution.py:161
  1992.2 40.7 %custom-call.29 = f32[4,2,1,64,64]{3,4,2,1,0:T(8,128)} custom-call(f32[4,2,1,64,64]{4,3,2,1,0:T(8,128)} %add_bitcast_fusion.5), custom_call_target="InvertDiagBlocksLowerTriangular" | custom-call | tf_op jit(solution)/shard_map/transpose(jvp(vmap()))/while/body/eval_jaxpr/checkpoint/jit(_solve_triangular)/vmap()/triangular_solve | solution.py:117
  2080.5 40.7 %custom-call.29 = f32[4,2,1,64,64]{3,4,2,1,0:T(8,128)} custom-call(f32[4,2,1,64,64]{4,3,2,1,0:T(8,128)} %add_bitcast_fusion.5), custom_call_target="InvertDiagBlocksLowerTriangular" | custom-call | tf_op jit(solution)/shard_map/transpose(jvp(vmap()))/while/body/eval_jaxpr/checkpoint/jit(_solve_triangular)/vmap()/triangular_solve | solution.py:117
  2168.7 40.7 %custom-call.29 = f32[4,2,1,64,64]{3,4,2,1,0:T(8,128)} custom-call(f32[4,2,1,64,64]{4,3,2,1,0:T(8,128)} %add_bitcast_fusion.5), custom_call_target="InvertDiagBlocksLowerTriangular" | custom-call | tf_op jit(solution)/shard_map/transpose(jvp(vmap()))/while/body/eval_jaxpr/checkpoint/jit(_solve_triangular)/vmap()/triangular_solve | solution.py:117
  2256.9 40.7 %custom-call.29 = f32[4,2,1,64,64]{3,4,2,1,0:T(8,128)} custom-call(f32[4,2,1,64,64]{4,3,2,1,0:T(8,128)} %add_bitcast_fusion.5), custom_call_target="InvertDiagBlocksLowerTriangular" | custom-call | tf_op jit(solution)/shard_map/transpose(jvp(vmap()))/while/body/eval_jaxpr/checkpoint/jit(_solve_triangular)/vmap()/triangular_solve | solution.py:117
  2345.1 40.7 %custom-call.29 = f32[4,2,1,64,64]{3,4,2,1,0:T(8,128)} custom-call(f32[4,2,1,64,64]{4,3,2,1,0:T(8,128)} %add_bitcast_fusion.5), custom_call_target="InvertDiagBlocksLowerTriangular" | custom-call | tf_op jit(solution)/shard_map/transpose(jvp(vmap()))/while/body/eval_jaxpr/checkpoint/jit(_solve_triangular)/vmap()/triangular_solve | solution.py:117
  2433.3 40.7 %custom-call.29 = f32[4,2,1,64,64]{3,4,2,1,0:T(8,128)} custom-call(f32[4,2,1,64,64]{4,3,2,1,0:T(8,128)} %add_bitcast_fusion.5), custom_call_target="InvertDiagBlocksLowerTriangular" | custom-call | tf_op jit(solution)/shard_map/transpose(jvp(vmap()))/while/body/eval_jaxpr/checkpoint/jit(_solve_triangular)/vmap()/triangular_solve | solution.py:117
  2521.5 40.7 %custom-call.29 = f32[4,2,1,64,64]{3,4,2,1,0:T(8,128)} custom-call(f32[4,2,1,64,64]{4,3,2,1,0:T(8,128)} %add_bitcast_fusion.5), custom_call_target="InvertDiagBlocksLowerTriangular" | custom-call | tf_op jit(solution)/shard_map/transpose(jvp(vmap()))/while/body/eval_jaxpr/checkpoint/jit(_solve_triangular)/vmap()/triangular_solve | solution.py:117
  2609.8 40.7 %custom-call.29 = f32[4,2,1,64,64]{3,4,2,1,0:T(8,128)} custom-call(f32[4,2,1,64,64]{4,3,2,1,0:T(8,128)} %add_bitcast_fusion.5), custom_call_target="InvertDiagBlocksLowerTriangular" | custom-call | tf_op jit(solution)/shard_map/transpose(jvp(vmap()))/while/body/eval_jaxpr/checkpoint/jit(_solve_triangular)/vmap()/triangular_solve | solution.py:117
  2753.8 16.4 add_convert_fusion
  2836.3 46.8 %reduce-scatter.19.cloned.1.call-done = bf16[4,128,1024]{2,1,0:T(8,128)(2,1)} async-done(((bf16[4,512,1024]{2,1,0:T(8,128)(2,1)}), bf16[4,128,1024]{2,1,0:T(8,128)(2,1)}) %reduce-scatter.19.cloned.1.call-update) | async-done | bytes 1048592 | tf_op jit(solution)/shard_map/reduce_scatter | solution.py:472
  2889.5 42.8 %reduce-scatter.31.cloned.1.call-done = f32[128,704]{0,1:T(8,128)} async-done(((f32[1024,704]{0,1:T(8,128)}), f32[128,704]{0,1:T(8,128)}) %reduce-scatter.31.cloned.1.call-update) | async-done | bytes 360464 | tf_op jit(solution)/shard_map/reduce_scatter | solution.py:517
  2932.3 49.1 %reduce-scatter.33.cloned.1.call-done = f32[128,704]{0,1:T(8,128)} async-done(((f32[1024,704]{0,1:T(8,128)}), f32[128,704]{0,1:T(8,128)}) %reduce-scatter.33.cloned.1.call-update) | async-done | bytes 360464 | tf_op jit(solution)/shard_map/reduce_scatter | solution.py:518
  2981.4 48.7 %reduce-scatter.35.cloned.1.call-done = f32[704,128]{1,0:T(8,128)} async-done(((f32[704,1024]{1,0:T(8,128)}), f32[704,128]{1,0:T(8,128)}) %reduce-scatter.35.cloned.1.call-update) | async-done | bytes 360464 | tf_op jit(solution)/shard_map/reduce_scatter | solution.py:519
  3030.2 40.0 %reduce-scatter.21.cloned.1.call-done = f32[128,256]{1,0:T(8,128)} async-done(((f32[1024,256]{1,0:T(8,128)}), f32[128,256]{1,0:T(8,128)}) %reduce-scatter.21.cloned.1.call-update) | async-done | bytes 131088 | tf_op jit(solution)/shard_map/reduce_scatter | solution.py:510
  3070.1 40.1 %reduce-scatter.23.cloned.1.call-done = f32[128,256]{1,0:T(8,128)} async-done(((f32[1024,256]{1,0:T(8,128)}), f32[128,256]{1,0:T(8,128)}) %reduce-scatter.23.cloned.1.call-update) | async-done | bytes 131088 | tf_op jit(solution)/shard_map/reduce_scatter | solution.py:511
  3110.3 45.3 %reduce-scatter.27.cloned.1.call-done = f32[128,512]{1,0:T(8,128)} async-done(((f32[1024,512]{1,0:T(8,128)}), f32[128,512]{1,0:T(8,128)}) %reduce-scatter.27.cloned.1.call-update) | async-done | bytes 262160 | tf_op jit(solution)/shard_map/reduce_scatter | solution.py:513
  3155.6 45.1 %reduce-scatter.29.cloned.1.call-done = f32[512,128]{1,0:T(8,128)} async-done(((f32[512,1024]{1,0:T(8,128)}), f32[512,128]{1,0:T(8,128)}) %reduce-scatter.29.cloned.1.call-update) | async-done | bytes 262160 | tf_op jit(solution)/shard_map/reduce_scatter | solution.py:516
  3200.7 45.5 %reduce-scatter.25.cloned.1.call-done = f32[128,512]{1,0:T(8,128)} async-done(((f32[1024,512]{1,0:T(8,128)}), f32[128,512]{1,0:T(8,128)}) %reduce-scatter.25.cloned.1.call-update) | async-done | bytes 262160 | tf_op jit(solution)/shard_map/reduce_scatter | solution.py:512
  3246.1 132.6 %all-reduce.40.cloned.1.call-done = (f32[1024]{0:T(1024)}, f32[4,1024]{1,0:T(4,128)}, f32[4,1024]{1,0:T(4,128)}, f32[4,2048]{1,0:T(4,128)}, f32[8]{0:T(128)}, /*index=5*/f32[8]{0:T(128)}, f32[256]{0:T(256)}, f32[1024]{0:T(1024)}) async-done(((f32[1024]{0:T(1024)}, f32[4,1024]{1,0:T(4,128)}, f32[4,1024]{1,0:T(4,128)}, f32[4,2048]{1,0:T(4,128)}, f32[8]{0:T(128)}, /*index=5*/f32[8]{0:T(128)}, f32[256]{0:T(256)}, ...) | async-done | bytes 74832 | tf_op jit(solution)/shard_map/psum | solution.py:496
  (1723 shorter events, 1086.4 us)
Async XLA Ops:
  7.2 81.7 %all-gather.9.cloned.1.call-start = ((), (), s32[]{:S(2)}) async-start(), calls=%async_computation.12 | async-start | bytes 5242880 | tf_op jit(solution)/shard_map/all_gather | solution.py:233
  7.9 107.6 %all-gather.11.cloned.1.call-start = ((), (), s32[]{:S(2)}) async-start(), calls=%async_computation.13 | async-start | bytes 1179648 | tf_op jit(solution)/shard_map/all_gather | solution.py:239
  8.7 1114.8 %all-gather.13.cloned.1.call-start = ((), (), s32[]{:S(2)}) async-start(), calls=%async_computation.14 | async-start | bytes 1179648 | tf_op jit(solution)/shard_map/all_gather | solution.py:240
  9.4 1122.8 %all-gather.15.cloned.1.call-start = ((), (), s32[]{:S(2)}) async-start(), calls=%async_computation.15 | async-start | bytes 1179648 | tf_op jit(solution)/shard_map/all_gather | solution.py:243
  10.6 150.6 %copy-start.59 = (f32[4,512]{1,0:T(4,128)}, f32[4,512]{1,0:T(4,128)S(1)}, u32[]{:S(2)}) copy-start(f32[4,512]{1,0:T(4,128)S(1)} %get-tuple-element.1026) | copy-start | bytes 24580
  10.6 150.6 %copy-start.61 = (f32[4,512]{1,0:T(4,128)}, f32[4,512]{1,0:T(4,128)S(1)}, u32[]{:S(2)}) copy-start(f32[4,512]{1,0:T(4,128)S(1)} %get-tuple-element.1027) | copy-start | bytes 24580
  10.6 150.6 %copy-start.63 = (f32[4,512]{1,0:T(4,128)}, f32[4,512]{1,0:T(4,128)S(1)}, u32[]{:S(2)}) copy-start(f32[4,512]{1,0:T(4,128)S(1)} %get-tuple-element.1028) | copy-start | bytes 24580
  22.4 69.8 %copy-start.99 = (bf16[1024,2]{0,1:T(2,128)(2,1)}, bf16[1024,2]{0,1:T(2,128)(2,1)S(1)}, u32[]{:S(2)}) copy-start(bf16[1024,2]{0,1:T(2,128)(2,1)S(1)} %all_gather.39) | copy-start | bytes 12292
  23.1 70.6 %copy-start.125 = (f32[2]{0:T(128)}, f32[2]{0:T(128)S(1)}, u32[]{:S(2)}) copy-start(f32[2]{0:T(128)S(1)} %fusion.231) | copy-start | bytes 28
  35.2 58.5 %copy-start.101 = (bf16[1024,2]{0,1:T(2,128)(2,1)}, bf16[1024,2]{0,1:T(2,128)(2,1)S(1)}, u32[]{:S(2)}) copy-start(bf16[1024,2]{0,1:T(2,128)(2,1)S(1)} %all_gather.37) | copy-start | bytes 12292
  73.2 88.0 %copy-start.89 = (f32[1,512]{1,0:T(1,128)}, f32[1,512]{1,0:T(1,128)S(1)}, u32[]{:S(2)}) copy-start(f32[1,512]{1,0:T(1,128)S(1)} %get-tuple-element.1008) | copy-start | bytes 6148
  73.2 88.0 %copy-start.91 = (f32[1,512]{1,0:T(1,128)}, f32[1,512]{1,0:T(1,128)S(1)}, u32[]{:S(2)}) copy-start(f32[1,512]{1,0:T(1,128)S(1)} %get-tuple-element.1009) | copy-start | bytes 6148
  73.2 88.0 %copy-start.93 = (f32[1,512]{1,0:T(1,128)}, f32[1,512]{1,0:T(1,128)S(1)}, u32[]{:S(2)}) copy-start(f32[1,512]{1,0:T(1,128)S(1)} %get-tuple-element.1010) | copy-start | bytes 6148
  73.2 88.0 %copy-start.95 = (f32[1,512]{1,0:T(1,128)}, f32[1,512]{1,0:T(1,128)S(1)}, u32[]{:S(2)}) copy-start(f32[1,512]{1,0:T(1,128)S(1)} %get-tuple-element.1011) | copy-start | bytes 6148
  74.1 55.3 %copy-start.104 = (f32[1,256]{1,0:T(1,128)}, f32[1,256]{1,0:T(1,128)S(1)}, u32[]{:S(2)}) copy-start(f32[1,256]{1,0:T(1,128)S(1)} %get-tuple-element.1022) | copy-start | bytes 3076
  74.2 55.3 %copy-start.106 = (f32[1,256]{1,0:T(1,128)}, f32[1,256]{1,0:T(1,128)S(1)}, u32[]{:S(2)}) copy-start(f32[1,256]{1,0:T(1,128)S(1)} %get-tuple-element.1023) | copy-start | bytes 3076
  74.2 66.7 %copy-start.112 = (f32[1,256]{1,0:T(1,128)}, f32[1,256]{1,0:T(1,128)S(1)}, u32[]{:S(2)}) copy-start(f32[1,256]{1,0:T(1,128)S(1)} %get-tuple-element.1033) | copy-start | bytes 3076
  74.2 66.7 %copy-start.114 = (f32[1,256]{1,0:T(1,128)}, f32[1,256]{1,0:T(1,128)S(1)}, u32[]{:S(2)}) copy-start(f32[1,256]{1,0:T(1,128)S(1)} %get-tuple-element.1034) | copy-start | bytes 3076
  74.2 66.7 %copy-start.116 = (f32[1,256]{1,0:T(1,128)}, f32[1,256]{1,0:T(1,128)S(1)}, u32[]{:S(2)}) copy-start(f32[1,256]{1,0:T(1,128)S(1)} %get-tuple-element.1035) | copy-start | bytes 3076
  74.2 66.7 %copy-start.118 = (f32[1,256]{1,0:T(1,128)}, f32[1,256]{1,0:T(1,128)S(1)}, u32[]{:S(2)}) copy-start(f32[1,256]{1,0:T(1,128)S(1)} %get-tuple-element.1036) | copy-start | bytes 3076
  102.9 26.5 collective-permute-start
  120.7 40.5 %collective-permute-start.1 = (f32[4,3,512]{2,1,0:T(4,128)S(1)}, f32[4,3,512]{2,1,0:T(4,128)S(1)}, u32[]{:S(2)}, u32[]{:S(2)}) collective-permute-start(f32[4,3,512]{2,1,0:T(4,128)S(1)} %slice.252), channel_id=1, source_target_pairs={{0,4},{1,5},{2,6},{3,7},{8,12},{9,13},{10,14},{11,15},{16,20},{17,... | collective-permute-start | bytes 73736 | tf_op jit(solution)/shard_map/ppermute | solution.py:19
  127.2 13.7 collective-permute-start.2
  635.8 28.8 collective-permute-start.3
  637.3 792.3 %all-reduce.36.cloned.1.call-start = ((), (), s32[]{:S(2)}) async-start(), calls=%async_computation.16 | async-start | bytes 16777216 | tf_op jit(solution)/shard_map/psum | solution.py:371
  1139.9 318.0 %all-gather.17.cloned.1.call-start = ((), (), s32[]{:S(2)}) async-start(), calls=%async_computation.17 | async-start | bytes 1622016 | tf_op jit(solution)/shard_map/all_gather | solution.py:244
  1140.5 344.6 %all-gather.19.cloned.1.call-start = ((), (), s32[]{:S(2)}) async-start(), calls=%async_computation.18 | async-start | bytes 1622016 | tf_op jit(solution)/shard_map/all_gather | solution.py:245
  1141.2 371.1 %all-gather.21.cloned.1.call-start = ((), (), s32[]{:S(2)}) async-start(), calls=%async_computation.19 | async-start | bytes 1622016 | tf_op jit(solution)/shard_map/all_gather | solution.py:246
  1142.0 450.0 %all-gather.23.cloned.1.call-start = ((), (), s32[]{:S(2)}) async-start(), calls=%async_computation.21 | async-start | bytes 5242880 | tf_op jit(solution)/shard_map/all_gather | solution.py:234
  1142.7 296.0 %copy-start.88 = (f32[1024]{0:T(1024)S(1)}, f32[1024]{0:T(1024)}, u32[]{:S(2)}) copy-start(f32[1024]{0:T(1024)} %param.45) | copy-start | bytes 12292
  1142.7 760.6 %all-reduce.38.cloned.1.call-start = ((), (), s32[]{:S(2)}) async-start(), calls=%async_computation.22 | async-start | bytes 16777216 | tf_op jit(solution)/shard_map/psum | solution.py:396
  1613.3 1215.0 %reduce-scatter.17.cloned.1.call-start = ((), (), s32[]{:S(2)}) async-start(), calls=%async_computation.20 | async-start | bytes 5242880 | tf_op jit(solution)/shard_map/reduce_scatter | solution.py:379
  1939.8 27.1 collective-permute-start.4
  1946.2 887.1 %reduce-scatter.37.cloned.1.call-start = ((), (), s32[]{:S(2)}) async-start(), calls=%async_computation.32 | async-start | bytes 589824
  2702.4 44.5 %collective-permute-start.7 = (bf16[4,3,512]{2,1,0:T(4,128)(2,1)S(1)}, bf16[4,3,512]{2,1,0:T(4,128)(2,1)S(1)}, u32[]{:S(2)}, u32[]{:S(2)}) collective-permute-start(bf16[4,3,512]{2,1,0:T(4,128)(2,1)S(1)} %slice.370), channel_id=1, source_target_pairs={{4,0},{5,1},{6,2},{7,3},{12,8},{13,9},{14,10},{15,11},{20,16},{21,... | collective-permute-start | bytes 36872 | tf_op jit(solution)/shard_map/ppermute | solution.py:19
  2717.8 17.5 collective-permute-start.5
  2721.1 20.2 collective-permute-start.6
  2730.2 104.6 %reduce-scatter.39.cloned.1.call-start = ((), (), s32[]{:S(2)}) async-start(), calls=%async_computation.33 | async-start | bytes 589824
  2735.2 147.8 %reduce-scatter.19.cloned.1.call-start = ((), (), s32[]{:S(2)}) async-start(), calls=%async_computation.23 | async-start | bytes 5242880 | tf_op jit(solution)/shard_map/reduce_scatter | solution.py:472
  2770.2 162.1 %reduce-scatter.31.cloned.1.call-start = ((), (), s32[]{:S(2)}) async-start(), calls=%async_computation.29 | async-start | bytes 3244032 | tf_op jit(solution)/shard_map/reduce_scatter | solution.py:517
  2778.3 203.1 %reduce-scatter.33.cloned.1.call-start = ((), (), s32[]{:S(2)}) async-start(), calls=%async_computation.30 | async-start | bytes 3244032 | tf_op jit(solution)/shard_map/reduce_scatter | solution.py:518
  2786.7 243.5 %reduce-scatter.35.cloned.1.call-start = ((), (), s32[]{:S(2)}) async-start(), calls=%async_computation.31 | async-start | bytes 3244032 | tf_op jit(solution)/shard_map/reduce_scatter | solution.py:519
  2794.5 275.6 %reduce-scatter.21.cloned.1.call-start = ((), (), s32[]{:S(2)}) async-start(), calls=%async_computation.24 | async-start | bytes 1179648 | tf_op jit(solution)/shard_map/reduce_scatter | solution.py:510
  2799.6 310.7 %reduce-scatter.23.cloned.1.call-start = ((), (), s32[]{:S(2)}) async-start(), calls=%async_computation.25 | async-start | bytes 1179648 | tf_op jit(solution)/shard_map/reduce_scatter | solution.py:511
  2804.8 350.8 %reduce-scatter.27.cloned.1.call-start = ((), (), s32[]{:S(2)}) async-start(), calls=%async_computation.27 | async-start | bytes 2359296 | tf_op jit(solution)/shard_map/reduce_scatter | solution.py:513
  2810.9 389.8 %reduce-scatter.29.cloned.1.call-start = ((), (), s32[]{:S(2)}) async-start(), calls=%async_computation.28 | async-start | bytes 2359296 | tf_op jit(solution)/shard_map/reduce_scatter | solution.py:516
  2819.6 426.5 %reduce-scatter.25.cloned.1.call-start = ((), (), s32[]{:S(2)}) async-start(), calls=%async_computation.26 | async-start | bytes 2359296 | tf_op jit(solution)/shard_map/reduce_scatter | solution.py:512
  2826.0 552.7 %all-reduce.40.cloned.1.call-start = ((), (), s32[]{:S(2)}) async-start(), calls=%async_computation.34 | async-start | bytes 151552 | tf_op jit(solution)/shard_map/psum | solution.py:496
  (292 other events, 2955.9 us)
Sparse Core Ops, SparseCore 0:
  9.6 79.2 all-gather.8
  90.8 24.6 all-gather.10
  117.4 23.4 all-gather.12
  637.5 24.1 all-gather.14
  1140.0 289.6 all-reduce.35
  1431.4 26.4 all-gather.16
  1459.8 25.2 all-gather.18
  1487.0 25.2 all-gather.20
  1513.9 78.0 all-gather.22
  1613.4 289.8 all-reduce.37
  1946.3 79.2 reduce-scatter.16
  2730.3 36.4 reduce-scatter.36
  2769.8 34.1 reduce-scatter.38
  2806.2 76.7 reduce-scatter.18
  2886.8 45.4 reduce-scatter.30
  2936.5 44.8 reduce-scatter.32
  2985.2 44.8 reduce-scatter.34
  3034.1 36.0 reduce-scatter.20
  3074.2 36.0 reduce-scatter.22
  3114.3 41.1 reduce-scatter.26
  3159.4 41.2 reduce-scatter.28
  3204.9 41.2 reduce-scatter.24
  3254.3 124.3 all-reduce.39
where the time goes:
time: 3410 us; the launch traced here: 3400 us
  waiting for transfers between devices  1310 us (38%)
  other arithmetic  1170 us (34%)
  matrix products  593 us (17%)
  local copies, waits for them, and re-layouts  232 us (7%)
  blocking collectives  58.5 us (2%)
    another operation x96, other arithmetic, delta_block(): jax.scipy.linalg.solve_triangular(system, right_side, lower=True, unit_di...  964 us
    psum x1, waiting for transfers between devices, shards(): middle = inputs + lax.psum(attn_terms, 'tensor')  287 us
    psum x1, waiting for transfers between devices, shards(): d_normed_two = lax.psum(ffn_terms, 'tensor')  287 us
    psum x1, waiting for transfers between devices, shards(): lax.psum((grad_norm_gain, grad_ffn_gain, grad_out_gain, conv_query_full,...  133 us
    all_gather x1, waiting for transfers between devices, shards(): lax.all_gather(d_mixed, 'tensor', axis=1, tiled=True)  79.7 us
    dot_general x40, matrix products, delta_block(): jnp.einsum('yzd,ydf->yzf', query_rows, running_state, precision=FULL_ACCU...  78.1 us
    dot_general x32, matrix products, delta_block(): jnp.einsum('nqu,nql->nul', closing_state[:, :, None] * key_rows, state_up...  77.7 us
  transfers between devices with their start and end apart: 31, of which 20 were waited for; matrix products, arithmetic and copies ran while one was open for 56% of the time, Pallas kernels for 0%

commit v1 on v0

v1 whole, which is shorter than its diff:
```python
from functools import partial

import jax
import jax.numpy as jnp
from jax import lax
from jax.experimental import pallas as pl
from jax.experimental.pallas import tpu as pltpu
from jax.sharding import Mesh, PartitionSpec as P

CHUNK = 128
RIM = 8
EPS_NORM = 1e-05
EPS_UNIT = 1e-06
FULL_ACCURACY = lax.Precision.HIGHEST
NN = (((1,), (0,)), ((), ()))
NT = (((1,), (1,)), ((), ()))
TN = (((0,), (0,)), ((), ()))


def dot_low(left, right, dims):
    return lax.dot_general(
        left.astype(jnp.bfloat16),
        right.astype(jnp.bfloat16),
        dims,
        preferred_element_type=jnp.float32,
    )


def halves(value):
    high = value.astype(jnp.bfloat16)
    return high, (value - high.astype(jnp.float32)).astype(jnp.bfloat16)


def dot_split(left, right, dims):
    left_high, left_low = halves(left)
    right_high, right_low = halves(right)
    total = lax.dot_general(left_high, right_high, dims, preferred_element_type=jnp.float32)
    total += lax.dot_general(left_high, right_low, dims, preferred_element_type=jnp.float32)
    return total + lax.dot_general(left_low, right_high, dims, preferred_element_type=jnp.float32)


def sigmoid(value):
    return 1.0 / (1.0 + jnp.exp(-value))


def positions():
    row = lax.broadcasted_iota(jnp.int32, (CHUNK, CHUNK), 0)
    col = lax.broadcasted_iota(jnp.int32, (CHUNK, CHUNK), 1)
    return row, col


def unit_lower_inverses(lowers):
    row, col = positions()
    eye = (row == col).astype(jnp.float32)
    diag = [jnp.where(row // 8 == col // 8, low, 0.0) for low in lowers]
    result = [eye - d for d in diag]
    power = [dot_split(d, d, NN) for d in diag]
    result = [x + dot_split(x, p, NN) for x, p in zip(result, power)]
    power = [dot_split(p, p, NN) for p in power]
    result = [x + dot_split(x, p, NN) for x, p in zip(result, power)]
    size = 8
    while size < CHUNK:
        across = (row // (2 * size) == col // (2 * size)) & (row // size != col // size)
        mixed = [dot_split(jnp.where(across, low, 0.0), x, NN) for low, x in zip(lowers, result)]
        result = [x - dot_split(x, m, NN) for x, m in zip(result, mixed)]
        size *= 2
    return result


KEY = 128
VAL = 256
GATE_AT = 2 * KEY + VAL
AB_AT = GATE_AT + VAL
HEAD = AB_AT + 128
VMEM_BYTES = 48 * 2**20


def thirds(value):
    high = value.astype(jnp.bfloat16)
    rest = value - high.astype(jnp.float32)
    middle = rest.astype(jnp.bfloat16)
    return high, middle, (rest - middle.astype(jnp.float32)).astype(jnp.bfloat16)


def dot_ones(ones, value, dims):
    left = ones.astype(jnp.bfloat16)
    return sum(
        lax.dot_general(left, part, dims, preferred_element_type=jnp.float32)
        for part in thirds(value)
    )


def unit(values):
    scale = lax.rsqrt(jnp.sum(values * values, axis=-1, keepdims=True) + EPS_UNIT)
    return values * scale, scale


def last_value(column):
    return column[CHUNK - 1 : CHUNK, :]


def spread_lanes(column):
    return jnp.broadcast_to(column, (CHUNK, CHUNK))


def chunk_parts(pre, par, segs, index):
    rows = slice(index * CHUNK, (index + 1) * CHUNK)
    row, col = positions()
    tile = segs[0, index]
    columns = jnp.concatenate([tile, jnp.zeros((CHUNK - 8, CHUNK), jnp.float32)], axis=0).T
    seg = columns[:, 0:1]
    masks = [(seg == columns[:, n : n + 1]).astype(jnp.float32) for n in range(1, 4)]
    shifted = pre[0, rows, AB_AT : AB_AT + 1] + par[0, 1:2, 0:1]
    strength = sigmoid(pre[0, rows, AB_AT + 1 : AB_AT + 2])
    soft = jnp.maximum(shifted, 0.0) + jnp.log1p(jnp.exp(-jnp.abs(shifted)))
    decay = par[0, 0:1, 0:1] * soft
    lower = (row >= col).astype(jnp.float32)
    cumul = dot_ones(lower, spread_lanes(decay), NN)
    allowed = (row >= col) & (seg == tile[0:1, :])
    within = jnp.where(allowed, jnp.exp(jnp.minimum(cumul - cumul.T, 0.0)), 0.0)
    cum = cumul[:, 0:1]
    opening = jnp.where(seg == tile[1:2, 0:1], jnp.exp(cum), 0.0)
    closing = jnp.where(
        seg == tile[0:1, CHUNK - 1 :], jnp.exp(jnp.minimum(last_value(cum) - cum, 0.0)), 0.0
    )
    return dict(
        rows=rows,
        masks=masks,
        shifted=shifted,
        decay=decay,
        strength=strength,
        opening=opening,
        closing=closing,
        within=within,
    )


def fill_ext(ext, rim, pre):
    ext[0:RIM, :] = rim[0, :, :GATE_AT]
    ext[RIM:, :] = pre[0, :, :GATE_AT]


def conv_chunk(ext, taps, part):
    first = RIM + part["rows"].start
    total = taps[0:1, :] * ext[first : first + CHUNK, :]
    for offset in range(1, 4):
        shifted = ext[first - offset : first - offset + CHUNK, :]
        total = total + taps[offset : offset + 1, :] * shifted * part["masks"][offset - 1]
    return total


def split_qkv(array):
    return array[:, :KEY], array[:, KEY : 2 * KEY], array[:, 2 * KEY :]


def front_kernel(
    pre, rim, taps, par, segs,
    inverse_out, step_out, push_out, read_out, base_out, end_map, end_push,
    ext,
):
    count = pre.shape[1] // CHUNK
    fill_ext(ext, rim, pre)
    row, col = positions()
    eye = (row == col).astype(jnp.float32)
    parts = [chunk_parts(pre, par, segs, n) for n in range(count)]
    convs = [conv_chunk(ext, taps, p) for p in parts]
    acts = [split_qkv(c * sigmoid(c)) for c in convs]
    queries = [unit(a[0])[0] * (float(KEY) ** -0.5) for a in acts]
    keys = [unit(a[1])[0] for a in acts]
    inner = [dot_split(k, k, NT) for k in keys]
    lowers = [
        jnp.where(row > col, p["strength"] * p["within"] * i, 0.0) for p, i in zip(parts, inner)
    ]
    inverses = unit_lower_inverses(lowers)
    scores = [dot_low(q, k, NT) * p["within"] for q, k, p in zip(queries, keys, parts)]
    known = [
        dot_low(t, p["strength"] * a[2], NN) for t, p, a in zip(inverses, parts, acts)
    ]
    write = [
        dot_low(t, p["strength"] * p["opening"] * k, NN)
        for t, p, k in zip(inverses, parts, keys)
    ]
    closed = [p["closing"] * k for p, k in zip(parts, keys)]
    steps = [
        last_value(p["opening"]) * eye - dot_low(c, w, TN)
        for p, c, w in zip(parts, closed, write)
    ]
    pushes = [dot_low(c, u, TN) for c, u in zip(closed, known)]
    total_map, total_push = steps[0], pushes[0]
    for n in range(count):
        rows = parts[n]["rows"]
        inverse_out[0, 0, rows, :] = inverses[n]
        step_out[0, 0, rows, :] = steps[n]
        push_out[0, 0, rows, :] = pushes[n]
        read_out[0, 0, rows, :] = parts[n]["opening"] * queries[n] - dot_low(
            scores[n], write[n], NN
        )
        base_out[0, 0, rows, :] = dot_low(scores[n], known[n], NN)
        if n:
            total_push = dot_low(steps[n], total_push, NN) + pushes[n]
            total_map = dot_low(steps[n], total_map, NN)
    end_map[0, 0] = total_map
    end_push[0, 0] = total_push


def output_kernel(
    state_in, step, push, read, base, pre, gain, states_out, mixer_out, gated_out
):
    count = step.shape[2] // CHUNK
    state = state_in[0, 0]
    for n in range(count):
        rows = slice(n * CHUNK, (n + 1) * CHUNK)
        states_out[0, 0, rows, :] = state
        mixer = base[0, 0, rows, :] + dot_low(read[0, 0, rows, :], state, NN)
        mixer_out[0, 0, rows, :] = mixer
        scale = lax.rsqrt(jnp.mean(mixer * mixer, axis=-1, keepdims=True) + EPS_NORM)
        gate = pre[0, rows, GATE_AT:AB_AT]
        gated_out[0, rows, :] = (mixer * scale * gain[...] * gate * sigmoid(gate)).astype(
            jnp.bfloat16
        )
        if n < count - 1:
            state = dot_low(step[0, 0, rows, :], state, NN) + push[0, 0, rows, :]


def mixer_back(d_gated, mixer_in, pre, gain, rows):
    mixer = mixer_in[0, 0, rows, :]
    scale = lax.rsqrt(jnp.mean(mixer * mixer, axis=-1, keepdims=True) + EPS_NORM)
    normed = mixer * scale
    gate = pre[0, rows, GATE_AT:AB_AT]
    sig = sigmoid(gate)
    grad = d_gated[0, rows, :]
    through = grad * gate * sig
    d_normed = through * gain[...]
    d_mixer = scale * (d_normed - normed * jnp.mean(d_normed * normed, axis=-1, keepdims=True))
    d_gate = grad * normed * gain[...] * sig * (1.0 + gate * (1.0 - sig))
    return d_mixer, d_gate, jnp.sum(through * normed, axis=0, keepdims=True)


def pull_kernel(d_gated, mixer_in, pre, gain, step, read, pull_out, start_out):
    count = step.shape[2] // CHUNK
    carried = None
    for n in reversed(range(count)):
        rows = slice(n * CHUNK, (n + 1) * CHUNK)
        d_mixer = mixer_back(d_gated, mixer_in, pre, gain, rows)[0]
        pull = dot_low(read[0, 0, rows, :], d_mixer, TN)
        pull_out[0, 0, rows, :] = pull
        if carried is None:
            carried = pull
        else:
            carried = dot_low(step[0, 0, rows, :], carried, TN) + pull
    start_out[0, 0] = carried


def back_kernel(
    pre, rim, taps, par, segs, inverse, step, states, d_gated, mixer_in, gain, pull, d_end,
    d_all_out, d_rim_out, d_small_out,
    ext, pad,
):
    length = pre.shape[1]
    count = length // CHUNK
    fill_ext(ext, rim, pre)
    row, col = positions()
    lane = col
    last_row = lax.broadcasted_iota(jnp.int32, (CHUNK, 1), 0) == CHUNK - 1
    lower = (row >= col).astype(jnp.float32)
    d_states = [None] * count
    d_states[count - 1] = d_end[0, 0]
    for n in reversed(range(1, count)):
        block = slice(n * CHUNK, (n + 1) * CHUNK)
        d_states[n - 1] = dot_low(step[0, 0, block, :], d_states[n], TN) + pull[0, 0, block, :]
    pad[:, 0:RIM, :] = jnp.zeros((4, RIM, GATE_AT), jnp.float32)
    pad[:, RIM + length :, :] = jnp.zeros((4, RIM, GATE_AT), jnp.float32)
    d_gain = jnp.zeros((1, VAL), jnp.float32)
    d_log = jnp.zeros((1, 1), jnp.float32)
    d_bias = jnp.zeros((1, 1), jnp.float32)
    d_taps = [jnp.zeros((1, GATE_AT), jnp.float32) for _ in range(4)]
    for n in range(count):
        part = chunk_parts(pre, par, segs, n)
        block, within = part["rows"], part["within"]
        strength, opening, closing = part["strength"], part["opening"], part["closing"]
        conv = conv_chunk(ext, taps, part)
        sig = sigmoid(conv)
        act_q, act_k, value = split_qkv(conv * sig)
        unit_q, scale_q = unit(act_q)
        key, scale_k = unit(act_k)
        query = unit_q * (float(KEY) ** -0.5)
        state, d_state = states[0, 0, block, :], d_states[n]
        solve = inverse[0, 0, block, :]
        grad, d_gate, d_gain_part = mixer_back(d_gated, mixer_in, pre, gain, block)
        d_gain = d_gain + d_gain_part
        rest = value - opening * dot_low(key, state, NN)
        update = dot_low(solve, strength * rest, NN)
        scores = dot_low(query, key, NT) * within
        inner = dot_low(key, key, NT) * within
        closed = closing * key
        d_update = dot_low(scores, grad, TN) + dot_low(closed, d_state, NN)
        d_right = dot_low(solve, d_update, TN)
        d_scores = dot_low(grad, update, NT)
        d_lower = jnp.where(row > col, -dot_low(d_right, update, NT), 0.0)
        d_plain = d_scores * within
        d_inner = d_lower * strength * within
        read_back = dot_low(grad, state, NT)
        known_back = -dot_low(strength * d_right, state, NT)
        closed_back = dot_low(update, d_state, NT)
        d_query = opening * read_back + dot_low(d_plain, key, NN)
        d_key = (
            dot_low(d_plain, query, TN)
            + dot_low(d_inner, key, NN)
            + dot_low(d_inner, key, TN)
            + opening * known_back
            + closing * closed_back
        )
        lower_parts = d_lower * inner
        d_strength = jnp.sum(lower_parts, axis=1, keepdims=True) + jnp.sum(
            d_right * rest, axis=1, keepdims=True
        )
        spread = d_scores * scores + strength * lower_parts
        d_opening = jnp.sum(query * read_back + key * known_back, axis=1, keepdims=True)
        d_closing = jnp.sum(key * closed_back, axis=1, keepdims=True) * closing
        through = jnp.sum(
            jnp.sum(state * d_state, axis=1, keepdims=True), axis=0, keepdims=True
        )
        end_sum = jnp.sum(d_closing, axis=0, keepdims=True) + through * last_value(opening)
        d_cumul = (
            jnp.sum(spread, axis=1, keepdims=True)
            + d_opening * opening
            - d_closing
            + jnp.where(last_row, end_sum, 0.0)
        )
        down = spread_lanes(jnp.sum(spread, axis=0, keepdims=True)).T
        d_decay = dot_ones(lower, spread_lanes(d_cumul) - down, TN)[:, 0:1]
        d_alpha = d_decay * par[0, 0:1, 0:1] * sigmoid(part["shifted"])
        d_beta = d_strength * strength * (1.0 - strength)
        d_log = d_log + jnp.sum(d_decay * part["decay"], axis=0, keepdims=True)
        d_bias = d_bias + jnp.sum(d_alpha, axis=0, keepdims=True)
        d_all_out[0, block, GATE_AT:AB_AT] = d_gate.astype(jnp.bfloat16)
        d_all_out[0, block, AB_AT:] = jnp.where(
            lane == 0, d_alpha, jnp.where(lane == 1, d_beta, 0.0)
        ).astype(jnp.bfloat16)
        d_query = d_query * (float(KEY) ** -0.5)
        d_act = jnp.concatenate(
            [
                scale_q * (d_query - unit_q * jnp.sum(unit_q * d_query, axis=-1, keepdims=True)),
                scale_k * (d_key - key * jnp.sum(key * d_key, axis=-1, keepdims=True)),
                strength * d_right,
            ],
            axis=1,
        )
        d_conv = d_act * sig * (1.0 + conv * (1.0 - sig))
        first = RIM + block.start
        for offset in range(4):
            masked = d_conv if offset == 0 else d_conv * part["masks"][offset - 1]
            shifted = ext[first - offset : first - offset + CHUNK, :]
            d_taps[offset] = d_taps[offset] + jnp.sum(masked * shifted, axis=0, keepdims=True)
            pad[offset, first : first + CHUNK, :] = masked * taps[offset : offset + 1, :]
    d_rim = pad[0, 0:RIM, :]
    for offset in range(1, 4):
        d_rim = d_rim + pad[offset, offset : offset + RIM, :]
    d_rim_out[0] = d_rim
    for n in range(count):
        first = RIM + n * CHUNK
        total = pad[0, first : first + CHUNK, :]
        for offset in range(1, 4):
            total = total + pad[offset, first + offset : first + offset + CHUNK, :]
        d_all_out[0, n * CHUNK : (n + 1) * CHUNK, :GATE_AT] = total.astype(jnp.bfloat16)
    for offset in range(4):
        d_small_out[0, 0, offset : offset + 1, :] = d_taps[offset]
    d_small_out[0, 0, 4:5, :] = jnp.concatenate([d_gain, d_gain], axis=1)
    d_small_out[0, 0, 5:6, :] = jnp.broadcast_to(d_log, (1, GATE_AT))
    d_small_out[0, 0, 6:7, :] = jnp.broadcast_to(d_bias, (1, GATE_AT))
    d_small_out[0, 0, 7:8, :] = jnp.zeros((1, GATE_AT), jnp.float32)


def per_head(*tail):
    return pl.BlockSpec((1, 1) + tail, lambda s, h: (s, h) + (0,) * len(tail))


def lanes_at(rows, width):
    return pl.BlockSpec((1, rows, width), lambda s, h: (s, 0, h))


def front_specs(length):
    return [
        lanes_at(length, HEAD),
        lanes_at(RIM, HEAD),
        pl.BlockSpec((4, GATE_AT), lambda s, h: (0, h)),
        pl.BlockSpec((1, 8, 128), lambda s, h: (h, 0, 0)),
        pl.BlockSpec((1, length // CHUNK, 8, CHUNK), lambda s, h: (s, 0, 0, 0)),
    ]


def gain_spec():
    return pl.BlockSpec((1, VAL), lambda s, h: (0, 0))


def shape(dims, kind=jnp.float32):
    return jax.ShapeDtypeStruct(dims, kind)


def call(kernel, lead, in_specs, outs, scratch, units, args):
    length = args[0].shape[1] if args[0].ndim == 3 else args[1].shape[2]
    flops = lead[0] * lead[1] * length * 128 * 128 * 2 * units
    return pl.pallas_call(
        kernel,
        grid=lead,
        in_specs=in_specs,
        out_specs=[spec for spec, _ in outs],
        out_shape=[kind for _, kind in outs],
        scratch_shapes=[pltpu.VMEM(dims, jnp.float32) for dims in scratch],
        compiler_params=pltpu.CompilerParams(vmem_limit_bytes=VMEM_BYTES),
        cost_estimate=pl.CostEstimate(
            flops=flops, bytes_accessed=flops // 100, transcendentals=0
        ),
    )(*args)


def run_front(pre, rim, taps, par, segs):
    seqs, length, wide = pre.shape
    lead = (seqs, wide // HEAD)
    widths = (KEY, KEY, VAL, KEY, VAL)
    outs = [(per_head(length, width), shape(lead + (length, width))) for width in widths]
    outs += [(per_head(KEY, width), shape(lead + (KEY, width))) for width in (KEY, VAL)]
    return call(
        front_kernel,
        lead,
        front_specs(length),
        outs,
        [(length + RIM, GATE_AT)],
        60,
        (pre, rim, taps, par, segs),
    )


def run_output(state_in, step, push, read, base, pre, gain):
    seqs, heads, length, _ = step.shape
    lead = (seqs, heads)
    in_specs = [per_head(KEY, VAL)]
    in_specs += [per_head(length, width) for width in (KEY, VAL, KEY, VAL)]
    in_specs += [lanes_at(length, HEAD), gain_spec()]
    outs = [
        (per_head(length, VAL), shape(lead + (length, VAL))),
        (per_head(length, VAL), shape(lead + (length, VAL))),
        (lanes_at(length, VAL), shape((seqs, length, heads * VAL), jnp.bfloat16)),
    ]
    args = (state_in, step, push, read, base, pre, gain)
    return call(output_kernel, lead, in_specs, outs, [], 15, args)


def run_pull(d_gated, mixer, pre, gain, step, read):
    seqs, heads, length, _ = step.shape
    lead = (seqs, heads)
    in_specs = [lanes_at(length, VAL), per_head(length, VAL), lanes_at(length, HEAD)]
    in_specs += [gain_spec(), per_head(length, KEY), per_head(length, KEY)]
    outs = [
        (per_head(length, VAL), shape(lead + (length, VAL))),
        (per_head(KEY, VAL), shape(lead + (KEY, VAL))),
    ]
    return call(
        pull_kernel, lead, in_specs, outs, [], 15, (d_gated, mixer, pre, gain, step, read)
    )


def run_back(pre, rim, taps, par, segs, inverse, step, states, d_gated, mixer, gain, pull, d_end):
    seqs, length, wide = pre.shape
    heads = wide // HEAD
    lead = (seqs, heads)
    in_specs = front_specs(length)
    in_specs += [per_head(length, width) for width in (KEY, KEY, VAL)]
    in_specs += [lanes_at(length, VAL), per_head(length, VAL), gain_spec()]
    in_specs += [per_head(length, VAL), per_head(KEY, VAL)]
    outs = [
        (lanes_at(length, HEAD), shape((seqs, length, wide), jnp.bfloat16)),
        (lanes_at(RIM, GATE_AT), shape((seqs, RIM, heads * GATE_AT))),
        (per_head(8, GATE_AT), shape(lead + (8, GATE_AT))),
    ]
    scratch = [(length + RIM, GATE_AT), (4, length + 2 * RIM, GATE_AT)]
    args = (pre, rim, taps, par, segs, inverse, step, states)
    args += (d_gated, mixer, gain, pull, d_end)
    return call(back_kernel, lead, in_specs, outs, scratch, 60, args)


def passed_along(value, axis, steps):
    count = lax.axis_size(axis)
    first, last = (max(0, -steps), min(count, count - steps))
    return lax.ppermute(value, axis, [(source, source + steps) for source in range(first, last)])


def swapped(value, axis, bits):
    count = lax.axis_size(axis)
    return lax.ppermute(value, axis, [(place, place ^ bits) for place in range(count)])


def summed_everywhere(value):
    for axis in ("core", "px", "ctx", "tensor"):
        bits = 1
        while bits < lax.axis_size(axis):
            value = value + swapped(value, axis, bits)
            bits *= 2
    return value


def seg_ids(starts, spots):
    return jnp.sum((starts[:, None, :] <= spots[None, :, None]).astype(jnp.int32), axis=2) - 1


def rms_rows(values):
    return values * lax.rsqrt(jnp.mean(values * values, axis=-1, keepdims=True) + EPS_NORM)


def norm_scaled(values, gain):
    return rms_rows(values) * gain


def matmul(left, right):
    return lax.dot_general(left, right, NN, preferred_element_type=jnp.float32)


def matmul_left_t(left, right):
    return lax.dot_general(left, right, TN, preferred_element_type=jnp.float32)


def matmul_right_t(left, right):
    return lax.dot_general(left, right, NT, preferred_element_type=jnp.float32)


def apply_map(linear, state):
    return jnp.einsum("shij,shjv->shiv", linear, state, precision=FULL_ACCURACY)


def apply_map_t(linear, state):
    return jnp.einsum("shji,shjv->shiv", linear, state, precision=FULL_ACCURACY)


def dealt_by_sequence(own):
    lane, lanes = lax.axis_index("tensor"), lax.axis_size("tensor")
    each = own.shape[0] // lanes
    tokens = own.shape[1]
    result = jnp.zeros((each, tokens * lanes) + own.shape[2:], own.dtype)
    for bits in range(lanes):
        other = lane ^ bits
        part = lax.dynamic_slice_in_dim(own, other * each, each, 0)
        if bits:
            part = swapped(part, "tensor", bits)
        result = lax.dynamic_update_slice_in_dim(result, part, other * tokens, 1)
    return result


def dealt_by_tokens(rows):
    lane, lanes = lax.axis_index("tensor"), lax.axis_size("tensor")
    each, tokens = rows.shape[0], rows.shape[1] // lanes
    result = jnp.zeros((each * lanes, tokens) + rows.shape[2:], rows.dtype)
    for bits in range(lanes):
        other = lane ^ bits
        part = lax.dynamic_slice_in_dim(rows, other * tokens, tokens, 1)
        if bits:
            part = swapped(part, "tensor", bits)
        result = lax.dynamic_update_slice_in_dim(result, part, other * each, 0)
    return result


def with_partner(own):
    return jnp.concatenate([own, swapped(own, "core", 1)], 0)


def sum_with_partner(partial_sums):
    half = partial_sums.shape[0] // 2
    received = swapped(partial_sums[half:], "core", 1)
    return partial_sums[:half].astype(jnp.float32) + received.astype(jnp.float32)


SPREAD = ("tensor", "px", "ctx")


def gather_weights(halves_of_cols):
    core = lax.axis_index("core")
    first, second = halves_of_cols
    mine = jnp.where(core == 0, first, second)
    received = swapped(jnp.where(core == 0, second, first), "core", 1)
    rows, cols = mine.shape
    pair = jnp.stack(
        [jnp.where(core == 0, mine, received), jnp.where(core == 0, received, mine)]
    )
    full = lax.all_gather(pair.reshape(2 * rows, cols), SPREAD, axis=0, tiled=True)
    return full.reshape(tuple(lax.axis_size(axis) for axis in SPREAD) + (2, rows, cols))


def whole_rows(gathered, first, width):
    part = gathered[..., first : first + width]
    part = jnp.transpose(part, (1, 3, 2, 4, 0, 5))
    return part.reshape(-1, part.shape[4] * width)


def split_rows(grad, lanes):
    px, pieces = lax.axis_size("px"), lax.axis_size("ctx")
    rows = grad.shape[0] // (2 * px * pieces)
    shaped = grad.reshape(px, 2, pieces, rows, lanes, grad.shape[1] // lanes)
    return jnp.transpose(shaped, (4, 0, 2, 1, 3, 5))


def scatter_grads(parts):
    core = lax.axis_index("core")
    joined = jnp.concatenate(parts, -1)
    rows, cols = joined.shape[-2:]
    summed = lax.psum_scatter(
        joined.reshape(-1, cols), SPREAD, scatter_dimension=0, tiled=True
    )
    top, bottom = summed[:rows], summed[rows:]
    mine = jnp.where(core == 0, top, bottom)
    received = swapped(jnp.where(core == 0, bottom, top), "core", 1)
    first = jnp.where(core == 0, mine, received).astype(jnp.float32)
    second = jnp.where(core == 0, received, mine).astype(jnp.float32)
    return first, second


def padded_cols(array, width):
    return jnp.pad(array, ((0, 0), (0, width - array.shape[1])))


def up_to(value, step):
    return -(-value // step) * step


def shards(
    tokens,
    seg_starts,
    norm_gain,
    w_query,
    w_key,
    w_value,
    w_gate,
    w_alpha,
    w_beta,
    conv_query,
    conv_key,
    conv_value,
    a_log,
    dt_bias,
    out_gain,
    w_out,
    ffn_gain,
    w_ffn_gate,
    w_ffn_up,
    w_ffn_down,
    d_mixed,
):
    low = jnp.bfloat16
    core = lax.axis_index("core")
    lane = lax.axis_index("tensor")
    place = lax.axis_index("ctx")
    lanes = lax.axis_size("tensor")
    pieces = lax.axis_size("ctx")
    model = tokens.shape[2]
    length = tokens.shape[1] * lanes
    own_seqs = tokens.shape[0] // lanes
    seqs = 2 * own_seqs
    flat = seqs * length
    quarter_heads = w_alpha.shape[1]
    per_quarter = quarter_heads // 2
    heads = per_quarter * lanes
    units = w_ffn_gate.shape[1]
    half_units = units // 2
    wide = up_to(half_units, 128)
    val_cols = per_quarter * VAL
    count = length // CHUNK

    def head_block(number):
        key = slice(number * KEY, (number + 1) * KEY)
        val = slice(number * VAL, (number + 1) * VAL)
        one = slice(number, number + 1)
        parts = [w_query[:, key], w_key[:, key], w_value[:, val], w_gate[:, val]]
        return padded_cols(
            jnp.concatenate(parts + [w_alpha[:, one], w_beta[:, one]], 1), HEAD
        )

    def mix_half(half):
        numbers = range(half * per_quarter, (half + 1) * per_quarter)
        return jnp.concatenate([head_block(number) for number in numbers], 1)

    def rest_half(half):
        inner = slice(half * half_units, (half + 1) * half_units)
        outer = slice(half * val_cols, (half + 1) * val_cols)
        parts = [w_ffn_gate[:, inner], w_ffn_up[:, inner], w_ffn_down[inner].T]
        return jnp.concatenate(
            [padded_cols(part, wide) for part in parts] + [w_out[outer].T], 1
        )

    def of_heads(array, width):
        shaped = array.reshape(array.shape[0], lanes, 2, per_quarter * width)
        return jnp.where(core == 0, shaped[:, :, 0], shaped[:, :, 1]).reshape(
            array.shape[0], heads, width
        )

    mix_parts = gather_weights((mix_half(0), mix_half(1)))
    own = dealt_by_sequence(tokens).astype(jnp.float32)
    normed_own = (rms_rows(own) * norm_gain).astype(low)
    normed = with_partner(normed_own).reshape(flat, model)
    rest_parts = gather_weights((rest_half(0), rest_half(1)))
    w_mix = whole_rows(mix_parts, 0, per_quarter * HEAD)
    pre = matmul(normed, w_mix).reshape(seqs, length, heads * HEAD)
    rim = passed_along(pre[:, length - RIM :], "ctx", 1)
    starts_own = lax.dynamic_slice_in_dim(seg_starts, lane * own_seqs, own_seqs, 0)
    starts = with_partner(starts_own.astype(jnp.float32)).astype(jnp.int32)
    base = place * length
    seg_ext = seg_ids(starts, base + jnp.arange(-3, length, dtype=jnp.int32))
    segs = jnp.stack(
        [seg_ext[:, 3 - n : 3 - n + length].reshape(seqs, count, CHUNK) for n in range(4)], 2
    ).astype(jnp.float32)
    segs = jnp.pad(segs, ((0, 0), (0, 0), (0, 4), (0, 0)))
    taps = jnp.concatenate(
        [of_heads(conv_query, KEY), of_heads(conv_key, KEY), of_heads(conv_value, VAL)], 2
    ).reshape(4, heads * GATE_AT)
    par = jnp.stack(
        [of_heads(-jnp.exp(a_log)[None], 1)[0, :, 0], of_heads(dt_bias[None], 1)[0, :, 0]], 1
    )
    par = jnp.broadcast_to(
        jnp.pad(par, ((0, 0), (0, 6)))[:, :, None], (heads, 8, 128)
    )
    gain_row = out_gain[None]
    inverse, step, push, read, base_out, end_map, end_push = run_front(
        pre, rim, taps, par, segs
    )
    cot_own = dealt_by_sequence(d_mixed)
    cot = with_partner(cot_own).reshape(flat, model)
    state_in = passed_along(end_push, "ctx", 1)
    if pieces > 2:
        state_in = lax.fori_loop(
            0,
            pieces - 2,
            lambda turn, state: passed_along(apply_map(end_map, state) + end_push, "ctx", 1),
            state_in,
        )
    states, mixer, gated = run_output(state_in, step, push, read, base_out, pre, gain_row)
    gated_flat = gated.reshape(flat, heads * VAL)
    w_pair = jnp.concatenate(
        [whole_rows(rest_parts, 0, wide), whole_rows(rest_parts, wide, wide)], 1
    )
    w_down_t = whole_rows(rest_parts, 2 * wide, wide)
    w_out_t = whole_rows(rest_parts, 3 * wide, val_cols)
    attn_part = matmul_right_t(gated_flat, w_out_t).astype(low)
    middle = own + sum_with_partner(attn_part.reshape(seqs, length, model))
    normed_two_own = (rms_rows(middle) * ffn_gain).astype(low)
    normed_two = with_partner(normed_two_own).reshape(flat, model)
    width = lanes * wide
    pair = matmul(normed_two, w_pair)
    gate_pre, up_pre = pair[:, :width], pair[:, width:]
    sigma = jax.nn.sigmoid(gate_pre)
    hidden = (gate_pre * sigma * up_pre).astype(low)
    d_hidden = matmul(cot, w_down_t)
    d_gate_pre = (d_hidden * up_pre * sigma * (1.0 + gate_pre * (1.0 - sigma))).astype(low)
    d_up_pre = (d_hidden * gate_pre * sigma).astype(low)
    d_pair = jnp.concatenate([d_gate_pre, d_up_pre], 1)
    ffn_terms = matmul_right_t(d_pair, w_pair).astype(low)
    d_normed_two = sum_with_partner(ffn_terms.reshape(seqs, length, model))
    _, norm_two_back = jax.vjp(norm_scaled, middle, ffn_gain)
    d_middle_part, grad_ffn_gain = norm_two_back(d_normed_two)
    d_middle = cot_own.astype(jnp.float32) + d_middle_part
    d_branch = with_partner(d_middle.astype(low)).reshape(flat, model)
    d_gated = matmul(d_branch, w_out_t).reshape(seqs, length, heads * VAL)
    pull, d_start = run_pull(d_gated, mixer, pre, gain_row, step, read)
    d_end = passed_along(d_start, "ctx", -1)
    if pieces > 2:
        d_end = lax.fori_loop(
            0,
            pieces - 2,
            lambda turn, state: passed_along(apply_map_t(end_map, state) + d_start, "ctx", -1),
            d_end,
        )
    grad_pair = matmul_left_t(normed_two, d_pair).astype(low)
    rest_first, rest_second = scatter_grads(
        [
            split_rows(grad_pair[:, :width], lanes),
            split_rows(grad_pair[:, width:], lanes),
            split_rows(matmul_left_t(cot, hidden).astype(low), lanes),
            split_rows(matmul_left_t(d_branch, gated_flat).astype(low), lanes),
        ]
    )
    ffn_part = matmul_right_t(hidden, w_down_t).astype(low)
    ffn_own = sum_with_partner(ffn_part.reshape(seqs, length, model))
    mixed = dealt_by_tokens((middle + ffn_own).astype(low))
    d_all, d_rim, d_small = run_back(
        pre, rim, taps, par, segs, inverse, step, states, d_gated, mixer, gain_row, pull, d_end
    )
    back_rim = passed_along(d_rim, "ctx", -1).reshape(seqs, RIM, heads, GATE_AT)
    back_rim = jnp.pad(back_rim, ((0, 0),) * 3 + ((0, HEAD - GATE_AT),))
    tail = d_all[:, length - RIM :].astype(jnp.float32) + back_rim.reshape(seqs, RIM, -1)
    d_all = lax.dynamic_update_slice(d_all, tail.astype(low), (0, length - RIM, 0))
    d_all = d_all.reshape(flat, heads * HEAD)
    d_normed = matmul_right_t(d_all, w_mix).astype(low)
    own_d_normed = sum_with_partner(d_normed.reshape(seqs, length, model))
    mix_first, mix_second = scatter_grads(
        [split_rows(matmul_left_t(normed, d_all).astype(low), lanes)]
    )
    _, norm_back = jax.vjp(norm_scaled, own, norm_gain)
    d_own, grad_norm_gain = norm_back(own_d_normed)
    grad_tokens = dealt_by_tokens((d_middle + d_own).astype(low)).astype(jnp.float32)

    small = jnp.sum(d_small, axis=0)

    def placed(part):
        rows, _, each = part.shape
        shaped = part.reshape(rows, lanes, 1, per_quarter * each)
        empty = jnp.zeros_like(shaped)
        both = jnp.where(
            core == 0,
            jnp.concatenate([shaped, empty], 2),
            jnp.concatenate([empty, shaped], 2),
        )
        return both.reshape(-1)

    conv_parts = jnp.transpose(small[:, :4], (1, 0, 2))
    items = [
        grad_ffn_gain,
        placed(conv_parts[..., :KEY]),
        placed(conv_parts[..., KEY : 2 * KEY]),
        placed(conv_parts[..., 2 * KEY :]),
        jnp.sum(small[:, 4, :VAL], axis=0),
        placed(small[None, :, 5, :1]),
        placed(small[None, :, 6, :1]),
    ]
    sizes = [item.shape[0] for item in items]
    total = up_to(sum(sizes), 1024)
    joined = jnp.concatenate(items + [jnp.zeros((total - sum(sizes),), jnp.float32)])
    joined = summed_everywhere(joined.reshape(-1, 128)).reshape(-1)
    norm_sum = summed_everywhere(grad_norm_gain.reshape(8, -1)).reshape(-1)
    ends = [sum(sizes[: n + 1]) for n in range(len(sizes))]
    sums = [joined[end - size : end] for size, end in zip(sizes, ends)]

    def mix_cols(first, width):
        halves_of = [
            half.reshape(half.shape[0], per_quarter, HEAD)[:, :, first : first + width].reshape(
                half.shape[0], -1
            )
            for half in (mix_first, mix_second)
        ]
        return jnp.concatenate(halves_of, 1)

    def rest_cols(first, width):
        return jnp.concatenate(
            [half[:, first : first + width] for half in (rest_first, rest_second)], 1
        )

    return (
        mixed,
        grad_tokens,
        norm_sum,
        mix_cols(0, KEY),
        mix_cols(KEY, KEY),
        mix_cols(2 * KEY, VAL),
        mix_cols(GATE_AT, VAL),
        mix_cols(AB_AT, 1),
        mix_cols(AB_AT + 1, 1),
        sums[1].reshape(4, -1),
        sums[2].reshape(4, -1),
        sums[3].reshape(4, -1),
        sums[5],
        sums[6],
        sums[4],
        rest_cols(3 * wide, val_cols).T,
        sums[0],
        rest_cols(0, half_units),
        rest_cols(wide, half_units),
        rest_cols(2 * wide, half_units).T,
    )


def solution(mesh):
    sizes = tuple(mesh.shape[axis] for axis in ("dp", "ctx", "tensor"))
    fine = Mesh(
        mesh.devices.reshape((sizes[0] // 2, 2) + sizes[1:]), ("px", "core", "ctx", "tensor")
    )
    dp = ("px", "core")
    rows = P(("px", "core", "ctx"), "tensor")
    cols = P("tensor", ("px", "core", "ctx"))
    own = P(dp, ("ctx", "tensor"), None)
    return jax.shard_map(
        shards,
        mesh=fine,
        in_specs=(own, P(dp, None), P())
        + (rows,) * 6
        + (P(),) * 6
        + (cols, P(), rows, rows, cols, own),
        out_specs=(own, own, P())
        + (rows,) * 6
        + (P(),) * 6
        + (cols, P(), rows, rows, cols),
        check_vma=False,
    )
```

time: 3410 us -> 973 us (0.29)
  other arithmetic: 1170 us -> 35.8 us
  waiting for transfers between devices: 1310 us -> 500 us
  matrix products: 593 us -> 102 us
  Pallas kernels: 0 us -> 128 us
  local copies, waits for them, and re-layouts: 232 us -> 137 us
  blocking collectives: 58.5 us -> 0 us
    another operation x136 -> x5, other arithmetic: 1000 us -> 2.05 us  [the longest x4 2.04 us: gather_weights(): jnp.stack([jnp.where(core == 0, mine, received), jnp.where(core == 0, rec...]
    psum x3 -> x0, waiting for transfers between devices: 706 us -> none  [the longest x1 287 us: shards(): middle = inputs + lax.psum(attn_terms, 'tensor')]
    dot_general x265 -> x12, matrix products: 541 us -> 102 us  [the longest x4 39.7 us: matmul(): return lax.dot_general(left, right, NN, preferred_element_type=jnp.float32)]
    reduce_scatter x10 -> x2, waiting for transfers between devices: 403 us -> 234 us  [scatter_grads(): lax.psum_scatter(joined.reshape(-1, cols), SPREAD, scatter_dimension=0, t...]
    ppermute x0 -> x35, waiting for transfers between devices: none -> 152 us  [swapped(): lax.ppermute(value, axis, [(place, place ^ bits) for place in range(count)])]
    pallas_call x0 -> x4, Pallas kernels: none -> 128 us  [call(): pl.pallas_call(kernel, grid=lead, in_specs=in_specs, out_specs=[spec for...]
    all_gather x8 -> x2, waiting for transfers between devices: 157 us -> 76.3 us  [gather_weights(): lax.all_gather(pair.reshape(2 * rows, cols), SPREAD, axis=0, tiled=True)]
    reduce_sum x44 -> x3, other arithmetic: 62.1 us -> 0.13 us  [the longest x1 0.09 us: seg_ids(): jnp.sum((starts[:, None, :] <= spots[None, :, None]).astype(jnp.int32), a...]
  transfers between devices with their start and end apart: 31 -> 43, of which waited for: 20 -> 28; matrix products, arithmetic and copies ran while one was open for 56% -> 18% of each run, Pallas kernels for 0% -> 7%
where the time goes in v1:
time: 973 us; the launch traced here: 960 us
  waiting for transfers between devices  500 us (51%)
  local copies, waits for them, and re-layouts  137 us (14%)
  Pallas kernels  128 us (13%)
  matrix products  102 us (10%)
  starting transfers between devices  40.9 us (4%)
  other arithmetic  35.8 us (4%)
  between operations  15.5 us (2%)
    reduce_scatter x2, waiting for transfers between devices, scatter_grads(): lax.psum_scatter(joined.reshape(-1, cols), SPREAD, scatter_dimension=0, t...  234 us
    ppermute x35, waiting for transfers between devices, swapped(): lax.ppermute(value, axis, [(place, place ^ bits) for place in range(count)])  152 us
    pallas_call x4, Pallas kernels, call(): pl.pallas_call(kernel, grid=lead, in_specs=in_specs, out_specs=[spec for...  128 us
    all_gather x2, waiting for transfers between devices, gather_weights(): lax.all_gather(pair.reshape(2 * rows, cols), SPREAD, axis=0, tiled=True)  76.3 us
    dot_general x4, matrix products, matmul(): return lax.dot_general(left, right, NN, preferred_element_type=jnp.float32)  39.7 us
    ppermute x4, waiting for transfers between devices, passed_along(): lax.ppermute(value, axis, [(source, source + steps) for source in range(f...  37.5 us
    dot_general x4, matrix products, matmul_left_t(): return lax.dot_general(left, right, TN, preferred_element_type=jnp.float32)  35 us
    reshape x5, local copies, waits for them, and re-layouts, split_rows(): shaped = grad.reshape(px, 2, pieces, rows, lanes, grad.shape[1] // lanes)  33 us
  transfers between devices with their start and end apart: 43, of which 28 were waited for; matrix products, arithmetic and copies ran while one was open for 18% of the time, Pallas kernels for 7%

profile of v1, /device:TPU:8, one launch (start us, length us, event | category | flops | bytes accessed | tf_op | source)
XLA Modules:
  0.0 959.8 jit_solution(13424874732101550367)
XLA Ops:
  24.7 10.9 %collective-permute-done = bf16[1,128,1024]{2,1,0:T(8,128)(2,1)S(1)} collective-permute-done((bf16[1,128,1024]{2,1,0:T(8,128)(2,1)S(1)}, bf16[1,128,1024]{2,1,0:T(8,128)(2,1)S(1)}, u32[]{:S(2)}, u32[]{:S(2)}) %collective-permute-start) | collective-permute-done | bytes 262176 | tf_op jit(solution)/shard_map/ppermute | solution.py:490
  35.7 12.8 %collective-permute-done.1 = bf16[1,128,1024]{2,1,0:T(8,128)(2,1)S(1)} collective-permute-done((bf16[1,128,1024]{2,1,0:T(8,128)(2,1)S(1)}, bf16[1,128,1024]{2,1,0:T(8,128)(2,1)S(1)}, u32[]{:S(2)}, u32[]{:S(2)}) %collective-permute-start.1) | collective-permute-done | bytes 262176 | tf_op jit(solution)/shard_map/ppermute | solution.py:490
  48.5 7.9 collective-permute-done.2
  58.1 76.3 %all-gather.3.cloned.1.call-done = bf16[4096,896]{1,0:T(8,128)(2,1)} async-done(((bf16[256,896]{1,0:T(8,128)(2,1)}), bf16[4096,896]{1,0:T(8,128)(2,1)}) %all-gather.3.cloned.1.call-update) | async-done | bytes 7340048 | tf_op jit(solution)/shard_map/all_gather | solution.py:583
  134.4 11.8 %copy.207 = bf16[2,2,2,128,4,896]{5,4,3,2,1,0:T(4,128)(2,1)} copy(bf16[2,2,2,128,4,896]{5,3,1,2,0,4:T(8,128)(2,1)} %bitcast.217) | data formatting | bytes 14680064 | tf_op jit(solution)/shard_map/transpose | solution.py:589
  146.2 12.7 %reshape.478 = bf16[1024,3584,1]{1,0,2:T(8,128)(2,1)} reshape(bf16[2,2,2,128,4,896]{5,4,3,2,1,0:T(4,128)(2,1)} %copy.207) | data formatting | bytes 14680064 | tf_op jit(solution)/shard_map/reshape | solution.py:590
  158.8 10.3 %fusion.16.pre = f32[2,512,3584]{2,1,0:T(8,128)S(1)} fusion(bf16[1024,3584,1]{1,0,2:T(8,128)(2,1)} %reshape.478, bf16[1,512,1024]{2,1,0:T(8,128)(2,1)} %collective-permute-done.3, bf16[1,512,1024]{2,1,0:T(8,128)(2,1)S(1)} %fusion.3), kind=kOutput, calls=%fused_computation.52 | convolution fusion | flops 7517241344 | bytes 24117248 | tf_op jit(solution)/shard_map/dot_general | solution.py:515
  169.2 5.5 copy-done.7
  174.6 3.9 collective-permute-start.5
  178.7 6.2 collective-permute-done.5.rim
  185.0 48.3 %shard_map.356 = (f32[2,4,512,128]{3,2,1,0:T(8,128)S(1)}, f32[2,4,512,128]{3,2,1,0:T(8,128)S(1)}, f32[2,4,512,256]{3,2,1,0:T(8,128)}, f32[2,4,512,128]{3,2,1,0:T...) custom-call(f32[2,512,3584]{2,1,0:T(8,128)} %copy-done.7, ...), custom_call_target="tpu_custom_call" | custom-call | flops 8053063680 | bytes 80530640 | tf_op jit(solution)/shard_map/pallas_call | solution.py:403
  234.6 4.6 collective-permute-start.7
  244.5 20.6 %collective-permute-done.15 = bf16[1,128,1024]{2,1,0:T(8,128)(2,1)S(1)} collective-permute-done((bf16[1,128,1024]{2,1,0:T(8,128)(2,1)S(1)}, bf16[1,128,1024]{2,1,0:T(8,128)(2,1)S(1)}, u32[]{:S(2)}, u32[]{:S(2)}) %collective-permute-start.15) | collective-permute-done | bytes 262176 | tf_op jit(solution)/shard_map/ppermute | solution.py:490
  269.1 24.9 %collective-permute-done.17 = bf16[1,128,1024]{2,1,0:T(8,128)(2,1)S(1)} collective-permute-done((bf16[1,128,1024]{2,1,0:T(8,128)(2,1)S(1)}, bf16[1,128,1024]{2,1,0:T(8,128)(2,1)S(1)}, u32[]{:S(2)}, u32[]{:S(2)}) %collective-permute-start.17) | collective-permute-done | bytes 262176 | tf_op jit(solution)/shard_map/ppermute | solution.py:490
  294.7 14.7 %shard_map.357 = (f32[2,4,512,256]{3,2,1,0:T(8,128)}, f32[2,4,512,256]{3,2,1,0:T(8,128)}, bf16[2,512,1024]{2,1,0:T(8,128)(2,1)S(1)}) custom-call(f32[2,4,128,256]{3,2,1,0:T(8,128)S(1)} %collective-permute-done.7.state_in, f32[2,4,512,128]{3,2,1,0:T(8,128)S(1)} %get-tuple-element.35.step, f32[2,4,512,256]{3,2,1,0:T(8,128)} %get-tuple-element.36.push, ...), custom_call_target="tpu_custom_call" | custom-call | flops 2013265920 | bytes 20132660 | tf_op jit(solution)/shard_map/pallas_call | solution.py:403
  336.9 13.1 %fusion.59 = f32[1024,3072]{1,0:T(8,128)} fusion(bf16[1024,1024]{1,0:T(8,128)(2,1)S(1)} %bitcast.224, bf16[1024,3072]{1,0:T(8,128)(2,1)} %copy-done.18), kind=kOutput, calls=%fused_computation.215 | convolution fusion | flops 6442450944 | bytes 20971520 | tf_op jit(solution)/shard_map/dot_general | solution.py:515
  350.0 9.7 %multiply_convert_fusion.1 = (bf16[1024,1536]{1,0:T(8,128)(2,1)S(1)}, bf16[1024,1536]{1,0:T(8,128)(2,1)S(1)}, bf16[1024,1536]{1,0:T(8,128)(2,1)}) fusion(f32[1024,3072]{1,0:T(8,128)} %fusion.59, bf16[1024,1024]{1,0:T(8,128)(2,1)S(1)} %bitcast.222, bf16[1024,1536]{1,0:T(8,128)(2,1)S(1)} %bitcast.219), kind=kOutput, calls=%fused_computation.4 | convolution fusion | flops 3246391296 | bytes 27262976 | tf_op jit(solution)/shard_map/dot_general | solution.py:515
  361.4 9.3 fusion.14
  371.0 3.7 convolution_convert_fusion.3
  377.5 4.4 fusion.40
  382.2 4.9 reshape.479
  387.1 6.6 fusion.15.d_gated
  393.8 13.7 %shard_map.358 = (f32[2,4,512,256]{3,2,1,0:T(8,128)}, f32[2,4,128,256]{3,2,1,0:T(8,128)S(1)}) custom-call(f32[2,512,1024]{2,1,0:T(8,128)} %fusion.15.d_gated, f32[2,4,512,256]{3,2,1,0:T(8,128)} %get-tuple-element.42.mixer_in, f32[2,512,3584]{2,1,0:T(8,128)} %copy-done.7, f32[1,256]{1,0:T(1,128)S(1)} %bitcast.196, ...), custom_call_target="tpu_custom_call" | custom-call | flops 2013265920 | bytes 20132660 | tf_op jit(solution)/shard_map/pallas_call | solution.py:403
  408.7 25.8 %collective-permute-done.21.d_end = f32[2,4,128,256]{3,2,1,0:T(8,128)S(1)} collective-permute-done((f32[2,4,128,256]{3,2,1,0:T(8,128)S(1)}, f32[2,4,128,256]{3,2,1,0:T(8,128)S(1)}, u32[]{:S(2)}, u32[]{:S(2)}) %collective-permute-start.21) | collective-permute-done | bytes 1048608 | tf_op jit(solution)/shard_map/ppermute | solution.py:485
  434.5 51.8 %shard_map.359 = (bf16[2,512,3584]{2,1,0:T(8,128)(2,1)}, f32[2,8,2048]{2,1,0:T(8,128)S(1)}, f32[2,4,8,512]{3,2,1,0:T(8,128)S(1)}) custom-call(f32[2,512,3584]{2,1,0:T(8,128)} %copy-done.7, f32[2,8,3584]{2,1,0:T(8,128)S(1)} %collective-permute-done.5.rim, f32[4,2048]{1,0:T(4,128)S(1)} %bitcast.194, f32[4,8,128]{2,1,0:T(8,128)S(1)} %broadcast_in_dim.10.par, ...), custom_call_target="tpu_custom_call" | custom-call | flops 8053063680 | bytes 80530640 | tf_op jit(solution)/shard_map/pallas_call | solution.py:403
  487.6 5.6 collective-permute-done.22
  494.7 12.3 %bitcast_convert_fusion = bf16[1024,3584]{1,0:T(8,128)(2,1)} fusion(bf16[2,512,3584]{2,1,0:T(8,128)(2,1)} %fusion.28, bf16[1,512,1024]{2,1,0:T(8,128)(2,1)} %collective-permute-done.3, bf16[1,512,1024]{2,1,0:T(8,128)(2,1)S(1)} %copy-done.20), kind=kOutput, calls=%fused_computation | convolution fusion | flops 7520911360 | bytes 16777216 | tf_op jit(solution)/shard_map/dot_general | solution.py:519
  507.0 13.1 %reshape.434 = bf16[2,2,2,128,4,896]{5,4,3,2,1,0:T(4,128)(2,1)} reshape(bf16[1024,3584]{1,0:T(8,128)(2,1)} %bitcast_convert_fusion) | data formatting | bytes 14680064 | tf_op jit(solution)/shard_map/reshape | solution.py:596
  520.2 7.3 copy.229
  529.1 10.0 %convolution_convert_fusion = bf16[1024,3072]{1,0:T(8,128)(2,1)S(1)} fusion(bf16[1024,1024]{1,0:T(8,128)(2,1)S(1)} %bitcast.225, bf16[1024,1536]{1,0:T(8,128)(2,1)} %copy-done.42, bf16[1024,1536]{1,0:T(8,128)(2,1)} %copy-done.41), kind=kOutput, calls=%fused_computation.7 | convolution fusion | flops 6458179584 | bytes 14680064 | tf_op jit(solution)/shard_map/dot_general | solution.py:519
  541.3 6.3 reshape.465
  550.0 7.7 convolution_convert_fusion.1
  557.7 6.5 reshape.467
  564.2 4.9 bitcast_convert_fusion.1
  569.1 4.7 reshape.468
  573.8 10.2 %pad_maximum_fusion = bf16[4,2,2,2,128,1408]{5,0,4,2,3,1:T(4,128)(2,1)S(1)} fusion(bf16[4,2,2,2,128,256]{5,0,4,2,3,1:T(4,128)(2,1)} %bitcast.216, bf16[4,2,2,2,128,384]{5,0,4,2,3,1:T(4,128)(2,1)} %bitcast.211, bf16[4,2,2,2,128,384]{5,0,4,2,3,1:T(4,128)(2,1)} %bitcast.210, bf16[4,2,2,2,128,384]{5,0,4,2,3,1:T(4,128)(2,1)S(1)} %bitcast.209), kind=kLoop, calls=%fused_computation.1 | loop fusion | flops 46137344 | bytes 23068672 | tf_op jit(solution)/shard_map/concatenate | solution.py:602
  584.0 6.4 copy.236
  590.5 7.4 copy.263
  601.5 12.3 %convolution_convert_fusion.2 = bf16[1024,1024]{1,0:T(8,128)(2,1)S(1)} fusion(bf16[1024,3584]{1,0:T(8,128)(2,1)} %bitcast.257, bf16[1024,3584]{1,0:T(8,128)(2,1)} %bitcast.218), kind=kOutput, calls=%fused_computation.47 | convolution fusion | flops 7517241344 | bytes 16777216 | tf_op jit(solution)/shard_map/dot_general | solution.py:523
  616.7 9.2 collective-permute-done.35
  626.1 20.2 %collective-permute-done.13 = bf16[1,128,1024]{2,1,0:T(8,128)(2,1)S(1)} collective-permute-done((bf16[1,128,1024]{2,1,0:T(8,128)(2,1)S(1)}, bf16[1,128,1024]{2,1,0:T(8,128)(2,1)S(1)}, u32[]{:S(2)}, u32[]{:S(2)}) %collective-permute-start.13) | collective-permute-done | bytes 262176 | tf_op jit(solution)/shard_map/ppermute | solution.py:490
  646.4 7.4 collective-permute-start.37
  653.8 7.8 collective-permute-done.14
  666.6 3.6 collective-permute-done.28
  677.4 4.8 collective-permute-start.31
  691.8 7.6 collective-permute-done.25
  699.4 7.7 collective-permute-done.26
  710.3 233.5 %reduce-scatter.5.cloned.1.call-done = bf16[256,1408]{1,0:T(8,128)(2,1)} async-done(((bf16[4096,1408]{1,0:T(8,128)(2,1)}), bf16[256,1408]{1,0:T(8,128)(2,1)}) %reduce-scatter.5.cloned.1.call-update) | async-done | bytes 720912 | tf_op jit(solution)/shard_map/reduce_scatter | solution.py:604
  (351 shorter events, 113.8 us)
Async XLA Ops:
  7.2 127.2 %all-gather.3.cloned.1.call-start = ((), (), s32[]{:S(2)}) async-start(), calls=%async_computation.2 | async-start | bytes 7798784 | tf_op jit(solution)/shard_map/all_gather | solution.py:583
  13.0 1.6 collective-permute-start.4
  15.5 295.1 %all-gather.5.cloned.1.call-start = ((), (), s32[]{:S(2)}) async-start(), calls=%async_computation.3 | async-start | bytes 12255232 | tf_op jit(solution)/shard_map/all_gather | solution.py:583
  16.8 1.7 collective-permute-start.8
  19.8 670.8 %reduce-scatter.3.cloned.1.call-start = ((), (), s32[]{:S(2)}) async-start(), calls=%async_computation.4 | async-start | bytes 7798784 | tf_op jit(solution)/shard_map/reduce_scatter | solution.py:604
  20.1 15.5 %collective-permute-start = (bf16[1,128,1024]{2,1,0:T(8,128)(2,1)S(1)}, bf16[1,128,1024]{2,1,0:T(8,128)(2,1)S(1)}, u32[]{:S(2)}, u32[]{:S(2)}) collective-permute-start(bf16[1,128,1024]{2,1,0:T(8,128)(2,1)S(1)} %get-tuple-element.188), channel_id=1, source_target_pairs={{0,1},{1,0},{2,3},{3,2},{4,5},{5,4},{6,7},{7,6},{8,9},{9,8},{10,11... | collective-permute-start | bytes 786440 | tf_op jit(solution)/shard_map/ppermute | solution.py:490
  20.2 28.3 %collective-permute-start.1 = (bf16[1,128,1024]{2,1,0:T(8,128)(2,1)S(1)}, bf16[1,128,1024]{2,1,0:T(8,128)(2,1)S(1)}, u32[]{:S(2)}, u32[]{:S(2)}) collective-permute-start(bf16[1,128,1024]{2,1,0:T(8,128)(2,1)S(1)} %get-tuple-element.190), channel_id=1, source_target_pairs={{0,2},{1,3},{2,0},{3,1},{4,6},{5,7},{6,4},{7,5},{8,10},{9,11},{10,... | collective-permute-start | bytes 786440 | tf_op jit(solution)/shard_map/ppermute | solution.py:490
  23.2 33.2 %collective-permute-start.2 = (bf16[1,128,1024]{2,1,0:T(8,128)(2,1)S(1)}, bf16[1,128,1024]{2,1,0:T(8,128)(2,1)S(1)}, u32[]{:S(2)}, u32[]{:S(2)}) collective-permute-start(bf16[1,128,1024]{2,1,0:T(8,128)(2,1)S(1)} %get-tuple-element.187), channel_id=1, source_target_pairs={{0,3},{1,2},{2,1},{3,0},{4,7},{5,6},{6,5},{7,4},{8,11},{9,10},{10,... | collective-permute-start | bytes 786440 | tf_op jit(solution)/shard_map/ppermute | solution.py:490
  24.3 33.5 %collective-permute-start.6 = (f32[1,7]{1,0:T(1,128)S(1)}, f32[1,7]{1,0:T(1,128)S(1)}, u32[]{:S(2)}, u32[]{:S(2)}) collective-permute-start(f32[1,7]{1,0:T(1,128)S(1)} %fusion.33), channel_id=1, source_target_pairs={{0,8},{8,0},{1,9},{9,1},{2,10},{10,2},{3,11},{11,3},{4,12},{12,4},... | collective-permute-start | bytes 92 | tf_op jit(solution)/shard_map/ppermute | solution.py:490
  56.4 265.3 %copy-start.8 = (bf16[1,512,1024]{2,1,0:T(8,128)(2,1)}, bf16[1,512,1024]{2,1,0:T(8,128)(2,1)S(1)}, u32[]{:S(2)}) copy-start(bf16[1,512,1024]{2,1,0:T(8,128)(2,1)S(1)} %constant_dynamic-update-slice_fusion.8) | copy-start | bytes 3145732
  57.1 101.8 %copy-start.19 = (bf16[1,512,1024]{2,1,0:T(8,128)(2,1)}, bf16[1,512,1024]{2,1,0:T(8,128)(2,1)S(1)}, u32[]{:S(2)}) copy-start(bf16[1,512,1024]{2,1,0:T(8,128)(2,1)S(1)} %fusion.3) | copy-start | bytes 3145732
  57.1 101.8 %collective-permute-start.3 = (bf16[1,512,1024]{2,1,0:T(8,128)(2,1)S(1)}, bf16[1,512,1024]{2,1,0:T(8,128)(2,1)}, u32[]{:S(2)}, u32[]{:S(2)}) collective-permute-start(bf16[1,512,1024]{2,1,0:T(8,128)(2,1)S(1)} %fusion.3), channel_id=1, source_target_pairs={{0,8},{8,0},{1,9},{9,1},{2,10},{10,2},{3,11},{11,3},{4,12},{12,4},... | collective-permute-start | bytes 3145736 | tf_op jit(solution)/shard_map/ppermute | solution.py:490
  174.6 10.3 %collective-permute-start.5 = (f32[2,8,3584]{2,1,0:T(8,128)S(1)}, f32[2,8,3584]{2,1,0:T(8,128)S(1)}, u32[]{:S(2)}, u32[]{:S(2)}) collective-permute-start(f32[2,8,3584]{2,1,0:T(8,128)S(1)} %slice.393), channel_id=1, source_target_pairs={{0,4},{1,5},{2,6},{3,7},{8,12},{9,13},{10,14},{11,15},{16,20},{17,... | collective-permute-start | bytes 688136 | tf_op jit(solution)/shard_map/ppermute | solution.py:485
  234.6 60.1 %copy-start.3 = (f32[256]{0:T(256)S(1)}, f32[256]{0:T(256)}, u32[]{:S(2)}) copy-start(f32[256]{0:T(256)} %param.35) | copy-start | bytes 3076
  234.6 60.1 %collective-permute-start.7 = (f32[2,4,128,256]{3,2,1,0:T(8,128)S(1)}, f32[2,4,128,256]{3,2,1,0:T(8,128)S(1)}, u32[]{:S(2)}, u32[]{:S(2)}) collective-permute-start(f32[2,4,128,256]{3,2,1,0:T(8,128)S(1)} %get-tuple-element.34), channel_id=1, source_target_pairs={{0,4},{1,5},{2,6},{3,7},{8,12},{9,13},{10,14},{11,15},{16,20},{17,... | collective-permute-start | bytes 3145736 | tf_op jit(solution)/shard_map/ppermute | solution.py:485
  241.0 24.0 %collective-permute-start.15 = (bf16[1,128,1024]{2,1,0:T(8,128)(2,1)S(1)}, bf16[1,128,1024]{2,1,0:T(8,128)(2,1)S(1)}, u32[]{:S(2)}, u32[]{:S(2)}) collective-permute-start(bf16[1,128,1024]{2,1,0:T(8,128)(2,1)S(1)} %get-tuple-element.180), channel_id=1, source_target_pairs={{0,1},{1,0},{2,3},{3,2},{4,5},{5,4},{6,7},{7,6},{8,9},{9,8},{10,11... | collective-permute-start | bytes 786440 | tf_op jit(solution)/shard_map/ppermute | solution.py:490
  241.3 27.0 %collective-permute-start.16 = (bf16[1,128,1024]{2,1,0:T(8,128)(2,1)S(1)}, bf16[1,128,1024]{2,1,0:T(8,128)(2,1)S(1)}, u32[]{:S(2)}, u32[]{:S(2)}) collective-permute-start(bf16[1,128,1024]{2,1,0:T(8,128)(2,1)S(1)} %get-tuple-element.182), channel_id=1, source_target_pairs={{0,2},{1,3},{2,0},{3,1},{4,6},{5,7},{6,4},{7,5},{8,10},{9,11},{10,... | collective-permute-start | bytes 786440 | tf_op jit(solution)/shard_map/ppermute | solution.py:490
  244.0 50.0 %collective-permute-start.17 = (bf16[1,128,1024]{2,1,0:T(8,128)(2,1)S(1)}, bf16[1,128,1024]{2,1,0:T(8,128)(2,1)S(1)}, u32[]{:S(2)}, u32[]{:S(2)}) collective-permute-start(bf16[1,128,1024]{2,1,0:T(8,128)(2,1)S(1)} %get-tuple-element.179), channel_id=1, source_target_pairs={{0,3},{1,2},{2,1},{3,0},{4,7},{5,6},{6,5},{7,4},{8,11},{9,10},{10,... | collective-permute-start | bytes 786440 | tf_op jit(solution)/shard_map/ppermute | solution.py:490
  294.7 24.8 %collective-permute-start.18 = (bf16[1,512,1024]{2,1,0:T(8,128)(2,1)}, bf16[1,512,1024]{2,1,0:T(8,128)(2,1)}, u32[]{:S(2)}, u32[]{:S(2)}) collective-permute-start(bf16[1,512,1024]{2,1,0:T(8,128)(2,1)} %constant_dynamic-update-slice_fusion.1), channel_id=1, source_target_pairs={{0,8},{8,0},{1,9},{9,1},{2,10},{10,2},{3,11},{11,3},{4,12},{12,4},... | collective-permute-start | bytes 3145736 | tf_op jit(solution)/shard_map/ppermute | solution.py:490
  318.9 2.8 collective-permute-start.9
  322.5 11.7 %collective-permute-start.10 = (bf16[1,512,1024]{2,1,0:T(8,128)(2,1)S(1)}, bf16[1,512,1024]{2,1,0:T(8,128)(2,1)S(1)}, u32[]{:S(2)}, u32[]{:S(2)}) collective-permute-start(bf16[1,512,1024]{2,1,0:T(8,128)(2,1)S(1)} %multiply_convert_fusion.3), channel_id=1, source_target_pairs={{0,8},{8,0},{1,9},{9,1},{2,10},{10,2},{3,11},{11,3},{4,12},{12,4},... | collective-permute-start | bytes 3145736 | tf_op jit(solution)/shard_map/ppermute | solution.py:490
  370.8 4.4 collective-permute-start.19
  374.8 2.7 collective-permute-start.11
  381.8 5.3 collective-permute-start.20
  407.4 27.1 %collective-permute-start.21 = (f32[2,4,128,256]{3,2,1,0:T(8,128)S(1)}, f32[2,4,128,256]{3,2,1,0:T(8,128)S(1)}, u32[]{:S(2)}, u32[]{:S(2)}) collective-permute-start(f32[2,4,128,256]{3,2,1,0:T(8,128)S(1)} %get-tuple-element.44), channel_id=1, source_target_pairs={{4,0},{5,1},{6,2},{7,3},{12,8},{13,9},{14,10},{15,11},{20,16},{21,... | collective-permute-start | bytes 3145736 | tf_op jit(solution)/shard_map/ppermute | solution.py:485
  434.5 60.2 %copy-start.20 = (bf16[1,512,1024]{2,1,0:T(8,128)(2,1)S(1)}, bf16[1,512,1024]{2,1,0:T(8,128)(2,1)}, u32[]{:S(2)}) copy-start(bf16[1,512,1024]{2,1,0:T(8,128)(2,1)} %copy-done.19) | copy-start | bytes 3145732
  486.3 6.8 collective-permute-start.22
  527.6 416.3 %reduce-scatter.5.cloned.1.call-start = ((), (), s32[]{:S(2)}) async-start(), calls=%async_computation.5 | async-start | bytes 12255232 | tf_op jit(solution)/shard_map/reduce_scatter | solution.py:604
  598.7 1.3 collective-permute-start.33
  598.9 17.8 %collective-permute-start.12 = (bf16[1,128,1024]{2,1,0:T(8,128)(2,1)S(1)}, bf16[1,128,1024]{2,1,0:T(8,128)(2,1)S(1)}, u32[]{:S(2)}, u32[]{:S(2)}) collective-permute-start(bf16[1,128,1024]{2,1,0:T(8,128)(2,1)S(1)} %get-tuple-element.185), channel_id=1, source_target_pairs={{0,1},{1,0},{2,3},{3,2},{4,5},{5,4},{6,7},{7,6},{8,9},{9,8},{10,11... | collective-permute-start | bytes 786440 | tf_op jit(solution)/shard_map/ppermute | solution.py:490
  600.0 16.6 %collective-permute-start.34 = (f32[144,128]{1,0:T(8,128)S(1)}, f32[144,128]{1,0:T(8,128)S(1)}, u32[]{:S(2)}, u32[]{:S(2)}) collective-permute-start(f32[144,128]{1,0:T(8,128)S(1)} %bitcast_add_fusion), channel_id=1, source_target_pairs={{0,16},{16,0},{1,17},{17,1},{2,18},{18,2},{3,19},{19,3},{4,20},{20... | collective-permute-start | bytes 221192 | tf_op jit(solution)/shard_map/ppermute | solution.py:490
  613.9 56.3 %copy-start.12 = (f32[1,512,1024]{2,1,0:T(8,128)S(1)}, f32[1,512,1024]{2,1,0:T(8,128)}, u32[]{:S(2)}) copy-start(f32[1,512,1024]{2,1,0:T(8,128)} %get-tuple-element.159) | copy-start | bytes 6291460
  613.9 50.5 %collective-permute-start.23 = (bf16[1,512,1024]{2,1,0:T(8,128)(2,1)S(1)}, bf16[1,512,1024]{2,1,0:T(8,128)(2,1)S(1)}, u32[]{:S(2)}, u32[]{:S(2)}) collective-permute-start(bf16[1,512,1024]{2,1,0:T(8,128)(2,1)S(1)} %slice_bitcast_fusion.4), channel_id=1, source_target_pairs={{0,8},{8,0},{1,9},{9,1},{2,10},{10,2},{3,11},{11,3},{4,12},{12,4},... | collective-permute-start | bytes 3145736 | tf_op jit(solution)/shard_map/ppermute | solution.py:490
  614.0 32.3 %collective-permute-start.13 = (bf16[1,128,1024]{2,1,0:T(8,128)(2,1)S(1)}, bf16[1,128,1024]{2,1,0:T(8,128)(2,1)S(1)}, u32[]{:S(2)}, u32[]{:S(2)}) collective-permute-start(bf16[1,128,1024]{2,1,0:T(8,128)(2,1)S(1)} %get-tuple-element.184), channel_id=1, source_target_pairs={{0,2},{1,3},{2,0},{3,1},{4,6},{5,7},{6,4},{7,5},{8,10},{9,11},{10,... | collective-permute-start | bytes 786440 | tf_op jit(solution)/shard_map/ppermute | solution.py:490
  614.8 46.8 %collective-permute-start.14 = (bf16[1,128,1024]{2,1,0:T(8,128)(2,1)S(1)}, bf16[1,128,1024]{2,1,0:T(8,128)(2,1)S(1)}, u32[]{:S(2)}, u32[]{:S(2)}) collective-permute-start(bf16[1,128,1024]{2,1,0:T(8,128)(2,1)S(1)} %get-tuple-element.183), channel_id=1, source_target_pairs={{0,3},{1,2},{2,1},{3,0},{4,7},{5,6},{6,5},{7,4},{8,11},{9,10},{10,... | collective-permute-start | bytes 786440 | tf_op jit(solution)/shard_map/ppermute | solution.py:490
  616.6 9.3 collective-permute-start.35
  625.9 20.4 %collective-permute-start.36 = (f32[144,128]{1,0:T(8,128)S(1)}, f32[144,128]{1,0:T(8,128)S(1)}, u32[]{:S(2)}, u32[]{:S(2)}) collective-permute-start(f32[144,128]{1,0:T(8,128)S(1)} %add.231), channel_id=1, source_target_pairs={{0,1},{1,0},{2,3},{3,2},{4,5},{5,4},{6,7},{7,6},{8,9},{9,8},{10,11... | collective-permute-start | bytes 221192 | tf_op jit(solution)/shard_map/ppermute | solution.py:490
  646.4 17.4 %collective-permute-start.37 = (f32[144,128]{1,0:T(8,128)S(1)}, f32[144,128]{1,0:T(8,128)S(1)}, u32[]{:S(2)}, u32[]{:S(2)}) collective-permute-start(f32[144,128]{1,0:T(8,128)S(1)} %add.232), channel_id=1, source_target_pairs={{0,2},{1,3},{2,0},{3,1},{4,6},{5,7},{6,4},{7,5},{8,10},{9,11},{10,... | collective-permute-start | bytes 221192 | tf_op jit(solution)/shard_map/ppermute | solution.py:490
  665.4 1.2 collective-permute-start.27
  666.6 3.6 collective-permute-start.28
  670.2 3.6 collective-permute-start.29
  673.8 3.6 collective-permute-start.30
  674.2 15.5 %collective-permute-start.24 = (bf16[1,128,1024]{2,1,0:T(8,128)(2,1)S(1)}, bf16[1,128,1024]{2,1,0:T(8,128)(2,1)S(1)}, u32[]{:S(2)}, u32[]{:S(2)}) collective-permute-start(bf16[1,128,1024]{2,1,0:T(8,128)(2,1)S(1)} %get-tuple-element.177), channel_id=1, source_target_pairs={{0,1},{1,0},{2,3},{3,2},{4,5},{5,4},{6,7},{7,6},{8,9},{9,8},{10,11... | collective-permute-start | bytes 786440 | tf_op jit(solution)/shard_map/ppermute | solution.py:490
  677.4 11.6 %collective-permute-start.31 = (f32[8,128]{1,0:T(8,128)S(1)}, f32[8,128]{1,0:T(8,128)S(1)}, u32[]{:S(2)}, u32[]{:S(2)}) collective-permute-start(f32[8,128]{1,0:T(8,128)S(1)} %add.227), channel_id=1, source_target_pairs={{0,2},{1,3},{2,0},{3,1},{4,6},{5,7},{6,4},{7,5},{8,10},{9,11},{10,... | collective-permute-start | bytes 12296 | tf_op jit(solution)/shard_map/ppermute | solution.py:490
  684.7 14.8 %collective-permute-start.25 = (bf16[1,128,1024]{2,1,0:T(8,128)(2,1)S(1)}, bf16[1,128,1024]{2,1,0:T(8,128)(2,1)S(1)}, u32[]{:S(2)}, u32[]{:S(2)}) collective-permute-start(bf16[1,128,1024]{2,1,0:T(8,128)(2,1)S(1)} %get-tuple-element.176), channel_id=1, source_target_pairs={{0,2},{1,3},{2,0},{3,1},{4,6},{5,7},{6,4},{7,5},{8,10},{9,11},{10,... | collective-permute-start | bytes 786440 | tf_op jit(solution)/shard_map/ppermute | solution.py:490
  684.7 22.5 %collective-permute-start.26 = (bf16[1,128,1024]{2,1,0:T(8,128)(2,1)S(1)}, bf16[1,128,1024]{2,1,0:T(8,128)(2,1)S(1)}, u32[]{:S(2)}, u32[]{:S(2)}) collective-permute-start(bf16[1,128,1024]{2,1,0:T(8,128)(2,1)S(1)} %get-tuple-element.175), channel_id=1, source_target_pairs={{0,3},{1,2},{2,1},{3,0},{4,7},{5,6},{6,5},{7,4},{8,11},{9,10},{10,... | collective-permute-start | bytes 786440 | tf_op jit(solution)/shard_map/ppermute | solution.py:490
  691.7 17.0 %collective-permute-start.32 = (bf16[128,896]{1,0:T(8,128)(2,1)S(1)}, bf16[128,896]{1,0:T(8,128)(2,1)S(1)}, u32[]{:S(2)}, u32[]{:S(2)}) collective-permute-start(bf16[128,896]{1,0:T(8,128)(2,1)S(1)} %broadcast_select_fusion.4), channel_id=1, source_target_pairs={{0,8},{8,0},{1,9},{9,1},{2,10},{10,2},{3,11},{11,3},{4,12},{12,4},... | collective-permute-start | bytes 688136 | tf_op jit(solution)/shard_map/ppermute | solution.py:490
  945.0 2.8 collective-permute-start.38
  (46 other events, 647.0 us)
Sparse Core Ops, SparseCore 0:
  15.6 118.6 all-gather.2
  137.2 157.5 all-gather.4
  527.7 162.8 reduce-scatter.2
  692.7 251.0 reduce-scatter.4

commit v2 on v1

--- a/solution.py
+++ b/solution.py
@@ -152,6 +152,57 @@
 def split_qkv(array):
     return array[:, :KEY], array[:, KEY : 2 * KEY], array[:, 2 * KEY :]
 
+GROUP = 4
+
+
+def front_terms(pre, ext, taps, par, segs, first, last):
+    row, col = positions()
+    eye = (row == col).astype(jnp.float32)
+    parts = [chunk_parts(pre, par, segs, n) for n in range(first, last)]
+    convs = [conv_chunk(ext, taps, p) for p in parts]
+    acts = [split_qkv(c * sigmoid(c)) for c in convs]
+    queries = [unit(a[0])[0] * (float(KEY) ** -0.5) for a in acts]
+    keys = [unit(a[1])[0] for a in acts]
+    inner = [dot_split(k, k, NT) for k in keys]
+    lowers = [
+        jnp.where(row > col, p["strength"] * p["within"] * i, 0.0) for p, i in zip(parts, inner)
+    ]
+    inverses = unit_lower_inverses(lowers)
+    scores = [dot_low(q, k, NT) * p["within"] for q, k, p in zip(queries, keys, parts)]
+    known = [
+        dot_low(t, p["strength"] * a[2], NN) for t, p, a in zip(inverses, parts, acts)
+    ]
+    write = [
+        dot_low(t, p["strength"] * p["opening"] * k, NN)
+        for t, p, k in zip(inverses, parts, keys)
+    ]
+    closed = [p["closing"] * k for p, k in zip(parts, keys)]
+    steps = [
+        last_value(p["opening"]) * eye - dot_low(c, w, TN)
+        for p, c, w in zip(parts, closed, write)
+    ]
+    pushes = [dot_low(c, u, TN) for c, u in zip(closed, known)]
+    reads = [
+        p["opening"] * q - dot_low(s, w, NN)
+        for p, q, s, w in zip(parts, queries, scores, write)
+    ]
+    bases = [dot_low(s, u, NN) for s, u in zip(scores, known)]
+    return inverses, steps, pushes, reads, bases
+
+
+def write_output(state, base, read, pre, gain, rows, mixer_out, gated_out):
+    mixer = base + dot_low(read, state, NN)
+    mixer_out[0, 0, rows, :] = mixer
+    scale = lax.rsqrt(jnp.mean(mixer * mixer, axis=-1, keepdims=True) + EPS_NORM)
+    gate = pre[0, rows, GATE_AT:AB_AT]
+    gated_out[0, rows, :] = (mixer * scale * gain[...] * gate * sigmoid(gate)).astype(
+        jnp.bfloat16
+    )
+
+
+def chunk_rows(number):
+    return slice(number * CHUNK, (number + 1) * CHUNK)
+
 
 def front_kernel(
     pre, rim, taps, par, segs,
@@ -160,47 +211,47 @@
 ):
     count = pre.shape[1] // CHUNK
     fill_ext(ext, rim, pre)
-    row, col = positions()
-    eye = (row == col).astype(jnp.float32)
-    parts = [chunk_parts(pre, par, segs, n) for n in range(count)]
-    convs = [conv_chunk(ext, taps, p) for p in parts]
-    acts = [split_qkv(c * sigmoid(c)) for c in convs]
-    queries = [unit(a[0])[0] * (float(KEY) ** -0.5) for a in acts]
-    keys = [unit(a[1])[0] for a in acts]
-    inner = [dot_split(k, k, NT) for k in keys]
-    lowers = [
-        jnp.where(row > col, p["strength"] * p["within"] * i, 0.0) for p, i in zip(parts, inner)
-    ]
-    inverses = unit_lower_inverses(lowers)
-    scores = [dot_low(q, k, NT) * p["within"] for q, k, p in zip(queries, keys, parts)]
-    known = [
-        dot_low(t, p["strength"] * a[2], NN) for t, p, a in zip(inverses, parts, acts)
-    ]
-    write = [
-        dot_low(t, p["strength"] * p["opening"] * k, NN)
-        for t, p, k in zip(inverses, parts, keys)
-    ]
-    closed = [p["closing"] * k for p, k in zip(parts, keys)]
-    steps = [
-        last_value(p["opening"]) * eye - dot_low(c, w, TN)
-        for p, c, w in zip(parts, closed, write)
-    ]
-    pushes = [dot_low(c, u, TN) for c, u in zip(closed, known)]
-    total_map, total_push = steps[0], pushes[0]
-    for n in range(count):
-        rows = parts[n]["rows"]
-        inverse_out[0, 0, rows, :] = inverses[n]
-        step_out[0, 0, rows, :] = steps[n]
-        push_out[0, 0, rows, :] = pushes[n]
-        read_out[0, 0, rows, :] = parts[n]["opening"] * queries[n] - dot_low(
-            scores[n], write[n], NN
-        )
-        base_out[0, 0, rows, :] = dot_low(scores[n], known[n], NN)
-        if n:
-            total_push = dot_low(steps[n], total_push, NN) + pushes[n]
-            total_map = dot_low(steps[n], total_map, NN)
+    total_map = total_push = None
+    for first in range(0, count, GROUP):
+        last = min(count, first + GROUP)
+        terms = front_terms(pre, ext, taps, par, segs, first, last)
+        for n in range(first, last):
+            rows = chunk_rows(n)
+            inverse, step, push, read, base = (term[n - first] for term in terms)
+            inverse_out[0, 0, rows, :] = inverse
+            step_out[0, 0, rows, :] = step
+            push_out[0, 0, rows, :] = push
+            read_out[0, 0, rows, :] = read
+            base_out[0, 0, rows, :] = base
+            if n:
+                total_push = dot_low(step, total_push, NN) + push
+                total_map = dot_low(step, total_map, NN)
+            else:
+                total_map, total_push = step, push
     end_map[0, 0] = total_map
     end_push[0, 0] = total_push
+
+
+def whole_kernel(
+    pre, rim, taps, par, segs, gain,
+    inverse_out, step_out, read_out, states_out, mixer_out, gated_out,
+    ext,
+):
+    count = pre.shape[1] // CHUNK
+    fill_ext(ext, rim, pre)
+    state = jnp.zeros((KEY, VAL), jnp.float32)
+    for first in range(0, count, GROUP):
+        last = min(count, first + GROUP)
+        terms = front_terms(pre, ext, taps, par, segs, first, last)
+        for n in range(first, last):
+            rows = chunk_rows(n)
+            inverse, step, push, read, base = (term[n - first] for term in terms)
+            inverse_out[0, 0, rows, :] = inverse
+            step_out[0, 0, rows, :] = step
+            read_out[0, 0, rows, :] = read
+            states_out[0, 0, rows, :] = state
+            write_output(state, base, read, pre, gain, rows, mixer_out, gated_out)
+            state = dot_low(step, state, NN) + push
 
 
 def output_kernel(
@@ -209,14 +260,10 @@
     count = step.shape[2] // CHUNK
     state = state_in[0, 0]
     for n in range(count):
-        rows = slice(n * CHUNK, (n + 1) * CHUNK)
+        rows = chunk_rows(n)
         states_out[0, 0, rows, :] = state
-        mixer = base[0, 0, rows, :] + dot_low(read[0, 0, rows, :], state, NN)
-        mixer_out[0, 0, rows, :] = mixer
-        scale = lax.rsqrt(jnp.mean(mixer * mixer, axis=-1, keepdims=True) + EPS_NORM)
-        gate = pre[0, rows, GATE_AT:AB_AT]
-        gated_out[0, rows, :] = (mixer * scale * gain[...] * gate * sigmoid(gate)).astype(
-            jnp.bfloat16
+        write_output(
+            state, base[0, 0, rows, :], read[0, 0, rows, :], pre, gain, rows, mixer_out, gated_out
         )
         if n < count - 1:
             state = dot_low(step[0, 0, rows, :], state, NN) + push[0, 0, rows, :]
@@ -251,11 +298,11 @@
     start_out[0, 0] = carried
 
 
-def back_kernel(
-    pre, rim, taps, par, segs, inverse, step, states, d_gated, mixer_in, gain, pull, d_end,
-    d_all_out, d_rim_out, d_small_out,
-    ext, pad,
-):
+def back_kernel(alone, pre, rim, taps, par, segs, inverse, step, states, d_gated, mixer_in, gain, *refs):
+    if alone:
+        read, d_all_out, d_rim_out, d_small_out, ext, pad = refs
+    else:
+        pull, d_end, d_all_out, d_rim_out, d_small_out, ext, pad = refs
     length = pre.shape[1]
     count = length // CHUNK
     fill_ext(ext, rim, pre)
@@ -264,10 +311,15 @@
     last_row = lax.broadcasted_iota(jnp.int32, (CHUNK, 1), 0) == CHUNK - 1
     lower = (row >= col).astype(jnp.float32)
     d_states = [None] * count
-    d_states[count - 1] = d_end[0, 0]
+    d_states[count - 1] = jnp.zeros((KEY, VAL), jnp.float32) if alone else d_end[0, 0]
     for n in reversed(range(1, count)):
-        block = slice(n * CHUNK, (n + 1) * CHUNK)
-        d_states[n - 1] = dot_low(step[0, 0, block, :], d_states[n], TN) + pull[0, 0, block, :]
+        block = chunk_rows(n)
+        if alone:
+            d_mixer = mixer_back(d_gated, mixer_in, pre, gain, block)[0]
+            back = dot_low(read[0, 0, block, :], d_mixer, TN)
+        else:
+            back = pull[0, 0, block, :]
+        d_states[n - 1] = dot_low(step[0, 0, block, :], d_states[n], TN) + back
     pad[:, 0:RIM, :] = jnp.zeros((4, RIM, GATE_AT), jnp.float32)
     pad[:, RIM + length :, :] = jnp.zeros((4, RIM, GATE_AT), jnp.float32)
     d_gain = jnp.zeros((1, VAL), jnp.float32)
@@ -460,14 +512,33 @@
     )
 
 
-def run_back(pre, rim, taps, par, segs, inverse, step, states, d_gated, mixer, gain, pull, d_end):
+def run_whole(pre, rim, taps, par, segs, gain):
     seqs, length, wide = pre.shape
     heads = wide // HEAD
     lead = (seqs, heads)
+    widths = (KEY, KEY, KEY, VAL, VAL)
+    outs = [(per_head(length, width), shape(lead + (length, width))) for width in widths]
+    outs.append((lanes_at(length, VAL), shape((seqs, length, heads * VAL), jnp.bfloat16)))
+    return call(
+        whole_kernel,
+        lead,
+        front_specs(length) + [gain_spec()],
+        outs,
+        [(length + RIM, GATE_AT)],
+        70,
+        (pre, rim, taps, par, segs, gain),
+    )
+
+
+def run_back(pre, rim, taps, par, segs, inverse, step, states, d_gated, mixer, gain, *ends):
+    seqs, length, wide = pre.shape
+    heads = wide // HEAD
+    lead = (seqs, heads)
+    alone = len(ends) == 1
     in_specs = front_specs(length)
     in_specs += [per_head(length, width) for width in (KEY, KEY, VAL)]
     in_specs += [lanes_at(length, VAL), per_head(length, VAL), gain_spec()]
-    in_specs += [per_head(length, VAL), per_head(KEY, VAL)]
+    in_specs += [per_head(length, KEY)] if alone else [per_head(length, VAL), per_head(KEY, VAL)]
     outs = [
         (lanes_at(length, HEAD), shape((seqs, length, wide), jnp.bfloat16)),
         (lanes_at(RIM, GATE_AT), shape((seqs, RIM, heads * GATE_AT))),
@@ -475,8 +546,8 @@
     ]
     scratch = [(length + RIM, GATE_AT), (4, length + 2 * RIM, GATE_AT)]
     args = (pre, rim, taps, par, segs, inverse, step, states)
-    args += (d_gated, mixer, gain, pull, d_end)
-    return call(back_kernel, lead, in_specs, outs, scratch, 60, args)
+    args += (d_gated, mixer, gain) + ends
+    return call(partial(back_kernel, alone), lead, in_specs, outs, scratch, 60, args)
 
 
 def passed_along(value, axis, steps):
@@ -491,7 +562,7 @@
 
 
 def summed_everywhere(value):
-    for axis in ("core", "px", "ctx", "tensor"):
+    for axis in ("core", "px", "cg", "cl", "tensor"):
         bits = 1
         while bits < lax.axis_size(axis):
             value = value + swapped(value, axis, bits)
@@ -562,54 +633,96 @@
     return jnp.concatenate([own, swapped(own, "core", 1)], 0)
 
 
-def sum_with_partner(partial_sums):
+def with_group(own):
+    side = lax.axis_index("cl")
+    tokens = own.shape[1]
+    both = jnp.zeros((own.shape[0], 2 * tokens) + own.shape[2:], own.dtype)
+    both = lax.dynamic_update_slice_in_dim(both, own, side * tokens, 1)
+    both = lax.dynamic_update_slice_in_dim(
+        both, swapped(own, "cl", 1), (1 - side) * tokens, 1
+    )
+    return with_partner(both)
+
+
+def sum_in_group(partial_sums):
+    side = lax.axis_index("cl")
     half = partial_sums.shape[0] // 2
     received = swapped(partial_sums[half:], "core", 1)
-    return partial_sums[:half].astype(jnp.float32) + received.astype(jnp.float32)
-
-
-SPREAD = ("tensor", "px", "ctx")
-
-
-def gather_weights(halves_of_cols):
+    both = (partial_sums[:half].astype(jnp.float32) + received.astype(jnp.float32)).astype(
+        partial_sums.dtype
+    )
+    tokens = both.shape[1] // 2
+    mine = lax.dynamic_slice_in_dim(both, side * tokens, tokens, 1)
+    other = lax.dynamic_slice_in_dim(both, (1 - side) * tokens, tokens, 1)
+    return mine.astype(jnp.float32) + swapped(other, "cl", 1).astype(jnp.float32)
+
+
+SPREAD = ("tensor", "px", "cg")
+
+
+def traded(value):
+    lanes = lax.axis_size("tensor")
+    pairs = [
+        (side * lanes + lane, (1 - side) * lanes + (lane ^ 1))
+        for side in range(2)
+        for lane in range(lanes)
+        if lane % 2 != side
+    ]
+    received = lax.ppermute(value, ("cl", "tensor"), pairs)
+    stays = lax.axis_index("cl") == lax.axis_index("tensor") % 2
+    return jnp.where(stays, value, received)
+
+
+def gather_weights(first, second):
     core = lax.axis_index("core")
-    first, second = halves_of_cols
     mine = jnp.where(core == 0, first, second)
     received = swapped(jnp.where(core == 0, second, first), "core", 1)
     rows, cols = mine.shape
     pair = jnp.stack(
         [jnp.where(core == 0, mine, received), jnp.where(core == 0, received, mine)]
     )
-    full = lax.all_gather(pair.reshape(2 * rows, cols), SPREAD, axis=0, tiled=True)
-    return full.reshape(tuple(lax.axis_size(axis) for axis in SPREAD) + (2, rows, cols))
+    pair = traded(pair.reshape(2 * rows, cols))
+    full = lax.all_gather(pair, SPREAD, axis=0, tiled=True)
+    lanes, px, groups = (lax.axis_size(axis) for axis in SPREAD)
+    return full.reshape(lanes // 2, 2, px, groups, 2, rows, cols)
 
 
 def whole_rows(gathered, first, width):
-    part = gathered[..., first : first + width]
-    part = jnp.transpose(part, (1, 3, 2, 4, 0, 5))
-    return part.reshape(-1, part.shape[4] * width)
-
-
-def split_rows(grad, lanes):
-    px, pieces = lax.axis_size("px"), lax.axis_size("ctx")
-    rows = grad.shape[0] // (2 * px * pieces)
-    shaped = grad.reshape(px, 2, pieces, rows, lanes, grad.shape[1] // lanes)
-    return jnp.transpose(shaped, (4, 0, 2, 1, 3, 5))
-
-
-def scatter_grads(parts):
+    pieces = [
+        jnp.transpose(part[..., first : first + width], (1, 3, 2, 0, 4, 5)).reshape(-1, width)
+        for part in gathered
+    ]
+    return jnp.concatenate(pieces, 1)
+
+
+def split_rows(grad):
+    px, groups = lax.axis_size("px"), lax.axis_size("cg")
+    rows = grad.shape[0] // (4 * px * groups)
+    shaped = grad.reshape(px, 2, groups, 2, rows, grad.shape[1])
+    return jnp.transpose(shaped, (3, 0, 2, 1, 4, 5)).reshape(-1, grad.shape[1])
+
+
+def joined_grads(by_k):
+    return jnp.concatenate(
+        [jnp.concatenate([split_rows(part) for part in parts], 1) for parts in by_k], 0
+    )
+
+
+def scatter_grads(joined):
     core = lax.axis_index("core")
-    joined = jnp.concatenate(parts, -1)
-    rows, cols = joined.shape[-2:]
-    summed = lax.psum_scatter(
-        joined.reshape(-1, cols), SPREAD, scatter_dimension=0, tiled=True
-    )
+    summed = traded(lax.psum_scatter(joined, SPREAD, scatter_dimension=0, tiled=True))
+    rows = summed.shape[0] // 2
     top, bottom = summed[:rows], summed[rows:]
     mine = jnp.where(core == 0, top, bottom)
     received = swapped(jnp.where(core == 0, bottom, top), "core", 1)
     first = jnp.where(core == 0, mine, received).astype(jnp.float32)
     second = jnp.where(core == 0, received, mine).astype(jnp.float32)
     return first, second
+
+
+def columns_of(array, groups):
+    width = array.shape[1] // groups
+    return [array[:, n * width : (n + 1) * width] for n in range(groups)]
 
 
 def padded_cols(array, width):
@@ -646,17 +759,19 @@
     low = jnp.bfloat16
     core = lax.axis_index("core")
     lane = lax.axis_index("tensor")
-    place = lax.axis_index("ctx")
+    side = lax.axis_index("cl")
+    place = lax.axis_index("cg")
     lanes = lax.axis_size("tensor")
-    pieces = lax.axis_size("ctx")
+    pieces = lax.axis_size("cg")
+    groups = lanes // 2
     model = tokens.shape[2]
-    length = tokens.shape[1] * lanes
+    length = 2 * tokens.shape[1] * lanes
     own_seqs = tokens.shape[0] // lanes
     seqs = 2 * own_seqs
     flat = seqs * length
     quarter_heads = w_alpha.shape[1]
     per_quarter = quarter_heads // 2
-    heads = per_quarter * lanes
+    heads = per_quarter * groups
     units = w_ffn_gate.shape[1]
     half_units = units // 2
     wide = up_to(half_units, 128)
@@ -685,19 +800,21 @@
         )
 
     def of_heads(array, width):
-        shaped = array.reshape(array.shape[0], lanes, 2, per_quarter * width)
-        return jnp.where(core == 0, shaped[:, :, 0], shaped[:, :, 1]).reshape(
-            array.shape[0], heads, width
-        )
-
-    mix_parts = gather_weights((mix_half(0), mix_half(1)))
+        shaped = array.reshape(array.shape[0], groups, 2, 2, per_quarter * width)
+        mine = jnp.where(side == 0, shaped[:, :, 0], shaped[:, :, 1])
+        mine = jnp.where(core == 0, mine[:, :, 0], mine[:, :, 1])
+        return mine.reshape(array.shape[0], heads, width)
+
+    mix_parts = gather_weights(mix_half(0), mix_half(1))
     own = dealt_by_sequence(tokens).astype(jnp.float32)
     normed_own = (rms_rows(own) * norm_gain).astype(low)
-    normed = with_partner(normed_own).reshape(flat, model)
-    rest_parts = gather_weights((rest_half(0), rest_half(1)))
+    normed = with_group(normed_own).reshape(flat, model)
+    rest_parts = gather_weights(rest_half(0), rest_half(1))
     w_mix = whole_rows(mix_parts, 0, per_quarter * HEAD)
     pre = matmul(normed, w_mix).reshape(seqs, length, heads * HEAD)
-    rim = passed_along(pre[:, length - RIM :], "ctx", 1)
+    rim = jnp.zeros((seqs, RIM, heads * HEAD), jnp.float32)
+    if pieces > 1:
+        rim = passed_along(pre[:, length - RIM :], "cg", 1)
     starts_own = lax.dynamic_slice_in_dim(seg_starts, lane * own_seqs, own_seqs, 0)
     starts = with_partner(starts_own.astype(jnp.float32)).astype(jnp.int32)
     base = place * length
@@ -716,20 +833,21 @@
         jnp.pad(par, ((0, 0), (0, 6)))[:, :, None], (heads, 8, 128)
     )
     gain_row = out_gain[None]
-    inverse, step, push, read, base_out, end_map, end_push = run_front(
-        pre, rim, taps, par, segs
-    )
+    front = (pre, rim, taps, par, segs)
     cot_own = dealt_by_sequence(d_mixed)
-    cot = with_partner(cot_own).reshape(flat, model)
-    state_in = passed_along(end_push, "ctx", 1)
-    if pieces > 2:
+    cot = with_group(cot_own).reshape(flat, model)
+    if pieces == 1:
+        inverse, step, read, states, mixer, gated = run_whole(*front, gain_row)
+    else:
+        inverse, step, push, read, base_out, end_map, end_push = run_front(*front)
+        state_in = passed_along(end_push, "cg", 1)
         state_in = lax.fori_loop(
             0,
             pieces - 2,
-            lambda turn, state: passed_along(apply_map(end_map, state) + end_push, "ctx", 1),
+            lambda turn, state: passed_along(apply_map(end_map, state) + end_push, "cg", 1),
             state_in,
         )
-    states, mixer, gated = run_output(state_in, step, push, read, base_out, pre, gain_row)
+        states, mixer, gated = run_output(state_in, step, push, read, base_out, pre, gain_row)
     gated_flat = gated.reshape(flat, heads * VAL)
     w_pair = jnp.concatenate(
         [whole_rows(rest_parts, 0, wide), whole_rows(rest_parts, wide, wide)], 1
@@ -737,10 +855,10 @@
     w_down_t = whole_rows(rest_parts, 2 * wide, wide)
     w_out_t = whole_rows(rest_parts, 3 * wide, val_cols)
     attn_part = matmul_right_t(gated_flat, w_out_t).astype(low)
-    middle = own + sum_with_partner(attn_part.reshape(seqs, length, model))
+    middle = own + sum_in_group(attn_part.reshape(seqs, length, model))
     normed_two_own = (rms_rows(middle) * ffn_gain).astype(low)
-    normed_two = with_partner(normed_two_own).reshape(flat, model)
-    width = lanes * wide
+    normed_two = with_group(normed_two_own).reshape(flat, model)
+    width = groups * wide
     pair = matmul(normed_two, w_pair)
     gate_pre, up_pre = pair[:, :width], pair[:, width:]
     sigma = jax.nn.sigmoid(gate_pre)
@@ -750,46 +868,51 @@
     d_up_pre = (d_hidden * gate_pre * sigma).astype(low)
     d_pair = jnp.concatenate([d_gate_pre, d_up_pre], 1)
     ffn_terms = matmul_right_t(d_pair, w_pair).astype(low)
-    d_normed_two = sum_with_partner(ffn_terms.reshape(seqs, length, model))
+    d_normed_two = sum_in_group(ffn_terms.reshape(seqs, length, model))
     _, norm_two_back = jax.vjp(norm_scaled, middle, ffn_gain)
     d_middle_part, grad_ffn_gain = norm_two_back(d_normed_two)
     d_middle = cot_own.astype(jnp.float32) + d_middle_part
-    d_branch = with_partner(d_middle.astype(low)).reshape(flat, model)
+    grad_pair = matmul_left_t(normed_two, d_pair).astype(low)
+    grad_down = matmul_left_t(cot, hidden).astype(low)
+    rest_joined = joined_grads(
+        zip(
+            columns_of(grad_pair[:, :width], groups),
+            columns_of(grad_pair[:, width:], groups),
+            columns_of(grad_down, groups),
+        )
+    )
+    d_branch = with_group(d_middle.astype(low)).reshape(flat, model)
+    d_branch, rest_joined = lax.optimization_barrier((d_branch, rest_joined))
+    rest_first, rest_second = scatter_grads(rest_joined)
     d_gated = matmul(d_branch, w_out_t).reshape(seqs, length, heads * VAL)
-    pull, d_start = run_pull(d_gated, mixer, pre, gain_row, step, read)
-    d_end = passed_along(d_start, "ctx", -1)
-    if pieces > 2:
+    if pieces == 1:
+        ends = (read,)
+    else:
+        pull, d_start = run_pull(d_gated, mixer, pre, gain_row, step, read)
+        d_end = passed_along(d_start, "cg", -1)
         d_end = lax.fori_loop(
             0,
             pieces - 2,
-            lambda turn, state: passed_along(apply_map_t(end_map, state) + d_start, "ctx", -1),
+            lambda turn, state: passed_along(apply_map_t(end_map, state) + d_start, "cg", -1),
             d_end,
         )
-    grad_pair = matmul_left_t(normed_two, d_pair).astype(low)
-    rest_first, rest_second = scatter_grads(
-        [
-            split_rows(grad_pair[:, :width], lanes),
-            split_rows(grad_pair[:, width:], lanes),
-            split_rows(matmul_left_t(cot, hidden).astype(low), lanes),
-            split_rows(matmul_left_t(d_branch, gated_flat).astype(low), lanes),
-        ]
-    )
+        ends = (pull, d_end)
     ffn_part = matmul_right_t(hidden, w_down_t).astype(low)
-    ffn_own = sum_with_partner(ffn_part.reshape(seqs, length, model))
+    ffn_own = sum_in_group(ffn_part.reshape(seqs, length, model))
     mixed = dealt_by_tokens((middle + ffn_own).astype(low))
-    d_all, d_rim, d_small = run_back(
-        pre, rim, taps, par, segs, inverse, step, states, d_gated, mixer, gain_row, pull, d_end
-    )
-    back_rim = passed_along(d_rim, "ctx", -1).reshape(seqs, RIM, heads, GATE_AT)
-    back_rim = jnp.pad(back_rim, ((0, 0),) * 3 + ((0, HEAD - GATE_AT),))
-    tail = d_all[:, length - RIM :].astype(jnp.float32) + back_rim.reshape(seqs, RIM, -1)
-    d_all = lax.dynamic_update_slice(d_all, tail.astype(low), (0, length - RIM, 0))
+    d_all, d_rim, d_small = run_back(*front, inverse, step, states, d_gated, mixer, gain_row, *ends)
+    if pieces > 1:
+        back_rim = passed_along(d_rim, "cg", -1).reshape(seqs, RIM, heads, GATE_AT)
+        back_rim = jnp.pad(back_rim, ((0, 0),) * 3 + ((0, HEAD - GATE_AT),))
+        tail = d_all[:, length - RIM :].astype(jnp.float32) + back_rim.reshape(seqs, RIM, -1)
+        d_all = lax.dynamic_update_slice(d_all, tail.astype(low), (0, length - RIM, 0))
     d_all = d_all.reshape(flat, heads * HEAD)
+    grad_mix = matmul_left_t(normed, d_all).astype(low)
+    grad_out = matmul_left_t(d_branch, gated_flat).astype(low)
+    mix_joined = joined_grads(zip(columns_of(grad_mix, groups), columns_of(grad_out, groups)))
+    mix_first, mix_second = scatter_grads(mix_joined)
     d_normed = matmul_right_t(d_all, w_mix).astype(low)
-    own_d_normed = sum_with_partner(d_normed.reshape(seqs, length, model))
-    mix_first, mix_second = scatter_grads(
-        [split_rows(matmul_left_t(normed, d_all).astype(low), lanes)]
-    )
+    own_d_normed = sum_in_group(d_normed.reshape(seqs, length, model))
     _, norm_back = jax.vjp(norm_scaled, own, norm_gain)
     d_own, grad_norm_gain = norm_back(own_d_normed)
     grad_tokens = dealt_by_tokens((d_middle + d_own).astype(low)).astype(jnp.float32)
@@ -798,14 +921,9 @@
 
     def placed(part):
         rows, _, each = part.shape
-        shaped = part.reshape(rows, lanes, 1, per_quarter * each)
-        empty = jnp.zeros_like(shaped)
-        both = jnp.where(
-            core == 0,
-            jnp.concatenate([shaped, empty], 2),
-            jnp.concatenate([empty, shaped], 2),
-        )
-        return both.reshape(-1)
+        shaped = part.reshape(rows, groups, 1, 1, per_quarter * each)
+        spots = jnp.arange(4).reshape(1, 1, 2, 2, 1)
+        return jnp.where(spots == 2 * side + core, shaped, 0.0).reshape(-1)
 
     conv_parts = jnp.transpose(small[:, :4], (1, 0, 2))
     items = [
@@ -827,17 +945,15 @@
 
     def mix_cols(first, width):
         halves_of = [
-            half.reshape(half.shape[0], per_quarter, HEAD)[:, :, first : first + width].reshape(
+            half[:, : per_quarter * HEAD].reshape(half.shape[0], per_quarter, HEAD)[:, :, first : first + width].reshape(
                 half.shape[0], -1
             )
             for half in (mix_first, mix_second)
         ]
         return jnp.concatenate(halves_of, 1)
 
-    def rest_cols(first, width):
-        return jnp.concatenate(
-            [half[:, first : first + width] for half in (rest_first, rest_second)], 1
-        )
+    def rest_cols(first, width, pair=(rest_first, rest_second)):
+        return jnp.concatenate([half[:, first : first + width] for half in pair], 1)
 
     return (
         mixed,
@@ -855,7 +971,7 @@
         sums[5],
         sums[6],
         sums[4],
-        rest_cols(3 * wide, val_cols).T,
+        rest_cols(per_quarter * HEAD, val_cols, (mix_first, mix_second)).T,
         sums[0],
         rest_cols(0, half_units),
         rest_cols(wide, half_units),
@@ -866,12 +982,13 @@
 def solution(mesh):
     sizes = tuple(mesh.shape[axis] for axis in ("dp", "ctx", "tensor"))
     fine = Mesh(
-        mesh.devices.reshape((sizes[0] // 2, 2) + sizes[1:]), ("px", "core", "ctx", "tensor")
+        mesh.devices.reshape(sizes[0] // 2, 2, sizes[1] // 2, 2, sizes[2]),
+        ("px", "core", "cg", "cl", "tensor"),
     )
     dp = ("px", "core")
-    rows = P(("px", "core", "ctx"), "tensor")
-    cols = P("tensor", ("px", "core", "ctx"))
-    own = P(dp, ("ctx", "tensor"), None)
+    rows = P(("px", "core", "cg", "cl"), "tensor")
+    cols = P("tensor", ("px", "core", "cg", "cl"))
+    own = P(dp, ("cg", "cl", "tensor"), None)
     return jax.shard_map(
         shards,
         mesh=fine,

time: 973 us -> 840 us (0.86)
  waiting for transfers between devices: 500 us -> 391 us
  local copies, waits for them, and re-layouts: 137 us -> 112 us
  other arithmetic: 35.8 us -> 60.4 us
  Pallas kernels: 128 us -> 104 us
  starting transfers between devices: 40.9 us -> 51.6 us
    reduce_scatter x2, waiting for transfers between devices: 234 us -> 57.1 us  [scatter_grads(): lax.psum_scatter(joined, SPREAD, scatter_dimension=0, tiled=True)]
    ppermute x35 -> x43, waiting for transfers between devices: 152 us -> 264 us  [swapped(): lax.ppermute(value, axis, [(place, place ^ bits) for place in range(count)])]
    all_gather x2, waiting for transfers between devices: 76.3 us -> 10.7 us  [gather_weights(): full = lax.all_gather(pair, SPREAD, axis=0, tiled=True)]
    pallas_call x4 -> x2, Pallas kernels: 128 us -> 104 us  [call(): pl.pallas_call(kernel, grid=lead, in_specs=in_specs, out_specs=[spec for...]
    reshape x17 -> x22, local copies, waits for them, and re-layouts: 51 us -> 30.1 us  [the longest x10 29.8 us: split_rows(): return jnp.transpose(shaped, (3, 0, 2, 1, 4, 5)).reshape(-1, grad.shape[1])]
    ppermute x4, waiting for transfers between devices: 37.5 us -> 57.9 us  [traded(): received = lax.ppermute(value, ('cl', 'tensor'), pairs)]
    concatenate x3 -> x4, other arithmetic: 10.4 us -> 29.8 us  [the longest x2 28.3 us: joined_grads(): jnp.concatenate([jnp.concatenate([split_rows(part) for part in parts], 1)...]
    unnamed x115 -> x133, local copies, waits for them, and re-layouts: 30.4 us -> 15.8 us
  transfers between devices with their start and end apart: 43 -> 51, of which waited for: 28 -> 32; matrix products, arithmetic and copies ran while one was open for 18% -> 17% of each run, Pallas kernels for 7% -> 6%
where the time goes in v2:
time: 840 us; the launch traced here: 833 us
  waiting for transfers between devices  391 us (47%)
  local copies, waits for them, and re-layouts  112 us (13%)
  Pallas kernels  104 us (12%)
  matrix products  98.9 us (12%)
  other arithmetic  60.4 us (7%)
  starting transfers between devices  51.6 us (6%)
  between operations  16 us (2%)
    ppermute x43, waiting for transfers between devices, swapped(): lax.ppermute(value, axis, [(place, place ^ bits) for place in range(count)])  264 us
    pallas_call x2, Pallas kernels, call(): pl.pallas_call(kernel, grid=lead, in_specs=in_specs, out_specs=[spec for...  104 us
    ppermute x4, waiting for transfers between devices, traded(): received = lax.ppermute(value, ('cl', 'tensor'), pairs)  57.9 us
    reduce_scatter x2, waiting for transfers between devices, scatter_grads(): lax.psum_scatter(joined, SPREAD, scatter_dimension=0, tiled=True)  57.1 us
    dot_general x4, matrix products, matmul(): return lax.dot_general(left, right, NN, preferred_element_type=jnp.float32)  39.7 us
    ppermute x43, starting transfers between devices, swapped(): lax.ppermute(value, axis, [(place, place ^ bits) for place in range(count)])  38.1 us
    dot_general x4, matrix products, matmul_right_t(): return lax.dot_general(left, right, NT, preferred_element_type=jnp.float32)  30.1 us
    reshape x10, local copies, waits for them, and re-layouts, split_rows(): return jnp.transpose(shaped, (3, 0, 2, 1, 4, 5)).reshape(-1, grad.shape[1])  29.8 us
  transfers between devices with their start and end apart: 51, of which 32 were waited for; matrix products, arithmetic and copies ran while one was open for 17% of the time, Pallas kernels for 6%

profile of v2, /device:TPU:8, one launch (start us, length us, event | category | flops | bytes accessed | tf_op | source)
XLA Modules:
  0.0 833.3 jit_solution(1810783785401680844)
XLA Ops:
  16.5 12.0 %collective-permute-done.6 = bf16[256,896]{1,0:T(8,128)(2,1)S(1)} collective-permute-done((bf16[256,896]{1,0:T(8,128)(2,1)S(1)}, bf16[256,896]{1,0:T(8,128)(2,1)S(1)}, u32[]{:S(2)}, u32[]{:S(2)}) %collective-permute-start.6) | collective-permute-done | bytes 458784 | tf_op jit(solution)/shard_map/ppermute | solution.py:671
  32.8 3.4 collective-permute-start.9
  36.2 31.5 %collective-permute-done.9 = bf16[256,1408]{1,0:T(8,128)(2,1)S(1)} collective-permute-done((bf16[256,1408]{1,0:T(8,128)(2,1)S(1)}, bf16[256,1408]{1,0:T(8,128)(2,1)S(1)}, u32[]{:S(2)}, u32[]{:S(2)}) %collective-permute-start.9) | collective-permute-done | bytes 720928 | tf_op jit(solution)/shard_map/ppermute | solution.py:671
  69.1 3.6 collective-permute-start.1
  74.1 7.4 collective-permute-done
  81.5 24.3 %collective-permute-done.1 = bf16[1,128,1024]{2,1,0:T(8,128)(2,1)S(1)} collective-permute-done((bf16[1,128,1024]{2,1,0:T(8,128)(2,1)S(1)}, bf16[1,128,1024]{2,1,0:T(8,128)(2,1)S(1)}, u32[]{:S(2)}, u32[]{:S(2)}) %collective-permute-start.1) | collective-permute-done | bytes 262176 | tf_op jit(solution)/shard_map/ppermute | solution.py:561
  105.9 14.4 %collective-permute-done.2 = bf16[1,128,1024]{2,1,0:T(8,128)(2,1)S(1)} collective-permute-done((bf16[1,128,1024]{2,1,0:T(8,128)(2,1)S(1)}, bf16[1,128,1024]{2,1,0:T(8,128)(2,1)S(1)}, u32[]{:S(2)}, u32[]{:S(2)}) %collective-permute-start.2) | collective-permute-done | bytes 262176 | tf_op jit(solution)/shard_map/ppermute | solution.py:561
  123.8 17.3 %collective-permute-done.3 = bf16[1,512,1024]{2,1,0:T(8,128)(2,1)S(1)} collective-permute-done((bf16[1,512,1024]{2,1,0:T(8,128)(2,1)S(1)}, bf16[1,512,1024]{2,1,0:T(8,128)(2,1)S(1)}, u32[]{:S(2)}, u32[]{:S(2)}) %collective-permute-start.3) | collective-permute-done | bytes 1048608 | tf_op jit(solution)/shard_map/ppermute | solution.py:561
  146.6 12.6 %fusion.8.pre = f32[2,1024,1792]{2,1,0:T(8,128)} fusion(bf16[1,1024,1024]{2,1,0:T(8,128)(2,1)} %collective-permute-done.4, bf16[1,1024,1024]{2,1,0:T(8,128)(2,1)} %constant_dynamic-update-slice_fusion.15, bf16[1024,896]{1,0:T(8,128)(2,1)S(1)} %bitcast.254, bf16[1024,896]{1,0:T(8,128)(2,1)S(1)} %bitcast.252), kind=kOutput, calls=%fused_computation.33 | convolution fusion | flops 7525629952 | bytes 22544384 | tf_op jit(solution)/shard_map/dot_general | solution.py:586
  159.3 47.8 %shard_map.356 = (f32[2,2,1024,128]{3,2,1,0:T(8,128)S(1)}, f32[2,2,1024,128]{3,2,1,0:T(8,128)S(1)}, f32[2,2,1024,128]{3,2,1,0:T(8,128)}, f32[2,2,1024,256]{3,2,1...) custom-call(f32[2,1024,1792]{2,1,0:T(8,128)} %fusion.8.pre, ...), custom_call_target="tpu_custom_call" | custom-call | flops 9395240960 | bytes 93952408 | tf_op jit(solution)/shard_map/pallas_call | solution.py:455
  208.5 10.7 %all-gather.5.cloned.1.call-done = bf16[2048,1408]{1,0:T(8,128)(2,1)} async-done(((bf16[256,1408]{1,0:T(8,128)(2,1)}), bf16[2048,1408]{1,0:T(8,128)(2,1)}) %all-gather.5.cloned.1.call-update) | async-done | bytes 5767184 | tf_op jit(solution)/shard_map/all_gather | solution.py:685
  227.0 4.1 collective-permute-done.10
  237.5 8.9 %collective-permute-done.19 = bf16[1,128,1024]{2,1,0:T(8,128)(2,1)S(1)} collective-permute-done((bf16[1,128,1024]{2,1,0:T(8,128)(2,1)S(1)}, bf16[1,128,1024]{2,1,0:T(8,128)(2,1)S(1)}, u32[]{:S(2)}, u32[]{:S(2)}) %collective-permute-start.19) | collective-permute-done | bytes 262176 | tf_op jit(solution)/shard_map/ppermute | solution.py:561
  246.5 8.9 %collective-permute-done.20 = bf16[1,128,1024]{2,1,0:T(8,128)(2,1)S(1)} collective-permute-done((bf16[1,128,1024]{2,1,0:T(8,128)(2,1)S(1)}, bf16[1,128,1024]{2,1,0:T(8,128)(2,1)S(1)}, u32[]{:S(2)}, u32[]{:S(2)}) %collective-permute-start.20) | collective-permute-done | bytes 262176 | tf_op jit(solution)/shard_map/ppermute | solution.py:561
  255.4 5.0 collective-permute-done.21
  264.1 22.5 %collective-permute-done.22 = bf16[1,512,1024]{2,1,0:T(8,128)(2,1)S(1)} collective-permute-done((bf16[1,512,1024]{2,1,0:T(8,128)(2,1)S(1)}, bf16[1,512,1024]{2,1,0:T(8,128)(2,1)S(1)}, u32[]{:S(2)}, u32[]{:S(2)}) %collective-permute-start.22) | collective-permute-done | bytes 1048608 | tf_op jit(solution)/shard_map/ppermute | solution.py:561
  286.7 20.1 %collective-permute-done.12 = bf16[1,512,1024]{2,1,0:T(8,128)(2,1)S(1)} collective-permute-done((bf16[1,512,1024]{2,1,0:T(8,128)(2,1)S(1)}, bf16[1,512,1024]{2,1,0:T(8,128)(2,1)S(1)}, u32[]{:S(2)}, u32[]{:S(2)}) %collective-permute-start.12) | collective-permute-done | bytes 1048608 | tf_op jit(solution)/shard_map/ppermute | solution.py:561
  313.6 10.9 %fusion.29 = f32[2048,1536]{0,1:T(8,128)} fusion(bf16[2048,1024]{1,0:T(8,128)(2,1)S(1)} %bitcast.238, bf16[1024,384]{1,0:T(8,128)(2,1)} %bitcast.271, bf16[1024,384]{1,0:T(8,128)(2,1)S(1)} %bitcast.270, bf16[1024,384]{1,0:T(8,128)(2,1)S(1)} %bitcast.268, bf16[1024,384]{1,0:T(8,128)(2,1)S(1)} %bitcast.265), kind=kOutput, calls=%fused_computation.85 | convolution fusion | flops 6455033856 | bytes 19922944 | tf_op jit(solution)/shard_map/dot_general | solution.py:586
  324.5 11.8 %multiply_convert_fusion.1 = (bf16[2048,768]{0,1:T(8,128)(2,1)}, bf16[2048,768]{0,1:T(8,128)(2,1)}, bf16[2048,768]{0,1:T(8,128)(2,1)}) fusion(f32[2048,1536]{0,1:T(8,128)} %fusion.29, bf16[2048,1024]{1,0:T(8,128)(2,1)S(1)} %bitcast.236, bf16[1024,384]{1,0:T(8,128)(2,1)S(1)} %bitcast.263, bf16[1024,384]{1,0:T(8,128)(2,1)S(1)} %bitcast.261), kind=kOutput, calls=%fused_computation.3 | convolution fusion | flops 3249537024 | bytes 27787264 | tf_op jit(solution)/shard_map/dot_general | solution.py:586
  336.3 10.2 %fusion.6 = bf16[2048,1024]{1,0:T(8,128)(2,1)S(1)} fusion(bf16[2048,768]{0,1:T(8,128)(2,1)} %get-tuple-element.155, bf16[2048,768]{0,1:T(8,128)(2,1)} %get-tuple-element.154, bf16[1024,384]{1,0:T(8,128)(2,1)} %bitcast.272, bf16[1024,384]{1,0:T(8,128)(2,1)} %bitcast.269, bf16[1024,384]{1,0:T(8,128)(2,1)} %bitcast.267, bf16[1024,384]{1,0:T(8,128)(2,1)S(1)} %bitcast.266), kind=kOutput, calls=%fused_computation.27 | convolution fusion | flops 6469713920 | bytes 13631488 | tf_op jit(solution)/shard_map/dot_general | solution.py:594
  347.3 3.8 collective-permute-done.24
  353.7 23.9 %collective-permute-done.25 = bf16[1,512,1024]{2,1,0:T(8,128)(2,1)S(1)} collective-permute-done((bf16[1,512,1024]{2,1,0:T(8,128)(2,1)S(1)}, bf16[1,512,1024]{2,1,0:T(8,128)(2,1)S(1)}, u32[]{:S(2)}, u32[]{:S(2)}) %collective-permute-start.25) | collective-permute-done | bytes 1048608 | tf_op jit(solution)/shard_map/ppermute | solution.py:561
  382.0 8.1 fusion.7
  417.1 6.7 convolution_convert_fusion.3
  437.4 12.4 %maximum_maximum_fusion = bf16[2048,1152]{0,1:T(8,128)(2,1)} fusion(bf16[1024,384]{0,1:T(8,128)(2,1)} %reshape.578, bf16[1024,384]{0,1:T(8,128)(2,1)} %reshape.576, bf16[1024,384]{0,1:T(8,128)(2,1)} %reshape.574, bf16[1024,384]{0,1:T(8,128)(2,1)} %reshape.572, bf16[1024,384]{0,1:T(8,128)(2,1)} %reshape.570, bf16[1024,384]{0,1:T(8,128)(2,1)S(1)} %reshape.568), kind=kLoop, calls=%fused_computation.6 | loop fusion | flops 28311552 | bytes 9437184 | tf_op jit(solution)/shard_map/concatenate | solution.py:706
  455.0 4.4 fusion.26
  466.1 55.7 %shard_map.357 = (bf16[2,1024,1792]{2,1,0:T(8,128)(2,1)}, f32[2,8,1024]{2,1,0:T(8,128)}, f32[2,2,8,512]{3,2,1,0:T(8,128)S(1)}) custom-call(f32[2,1024,1792]{2,1,0:T(8,128)} %fusion.8.pre, f32[2,8,1792]{2,1,0:T(8,128)S(1)} %broadcast_in_dim.116.rim, f32[4,1024]{1,0:T(4,128)S(1)} %bitcast.225, f32[2,8,128]{2,1,0:T(8,128)S(1)} %broadcast_in_dim.117.par, ...), custom_call_target="tpu_custom_call" | custom-call | flops 8053063680 | bytes 80530640 | tf_op jit(solution)/shard_map/pallas_call | solution.py:455
  521.9 11.9 %bitcast_convert_fusion = bf16[1024,1792]{1,0:T(8,128)(2,1)S(1)} fusion(bf16[2,1024,1792]{2,1,0:T(8,128)(2,1)} %get-tuple-element.37, bf16[1,1024,1024]{2,1,0:T(8,128)(2,1)} %collective-permute-done.4, bf16[1,1024,1024]{2,1,0:T(8,128)(2,1)} %constant_dynamic-update-slice_fusion.15), kind=kOutput, calls=%fused_computation | convolution fusion | flops 7520124928 | bytes 15204352 | tf_op jit(solution)/shard_map/dot_general | solution.py:590
  535.3 3.7 copy.248
  539.0 4.4 reshape.584
  543.4 5.5 copy.250
  548.9 5.3 reshape.588
  554.2 16.0 %maximum_maximum_fusion.1 = bf16[2048,1152]{0,1:T(8,128)(2,1)} fusion(bf16[1024,256]{0,1:T(8,128)(2,1)S(1)} %reshape.590, bf16[1024,896]{0,1:T(8,128)(2,1)} %reshape.588, bf16[1024,256]{0,1:T(8,128)(2,1)S(1)} %reshape.586, bf16[1024,896]{0,1:T(8,128)(2,1)S(1)} %reshape.584), kind=kLoop, calls=%fused_computation.7 | loop fusion | flops 18874368 | bytes 9437184 | tf_op jit(solution)/shard_map/concatenate | solution.py:706
  571.6 6.0 convolution_convert_fusion.2
  577.6 11.5 %convolution_convert_fusion = bf16[2048,1024]{1,0:T(8,128)(2,1)S(1)} fusion(bf16[2048,1792]{1,0:T(8,128)(2,1)} %bitcast.292, bf16[1024,896]{1,0:T(8,128)(2,1)S(1)} %bitcast.255, bf16[1024,896]{1,0:T(8,128)(2,1)S(1)} %bitcast.253), kind=kOutput, calls=%fused_computation.29 | convolution fusion | flops 7525629952 | bytes 15204352 | tf_op jit(solution)/shard_map/dot_general | solution.py:594
  596.0 5.7 collective-permute-done.41
  602.1 4.0 collective-permute-done.42
  613.4 3.7 collective-permute-start.44
  621.1 14.1 %collective-permute-done.29 = bf16[1,512,1024]{2,1,0:T(8,128)(2,1)S(1)} collective-permute-done((bf16[1,512,1024]{2,1,0:T(8,128)(2,1)S(1)}, bf16[1,512,1024]{2,1,0:T(8,128)(2,1)S(1)}, u32[]{:S(2)}, u32[]{:S(2)}) %collective-permute-start.29) | collective-permute-done | bytes 1048608 | tf_op jit(solution)/shard_map/ppermute | solution.py:561
  642.7 13.3 %collective-permute-done.15 = bf16[1,512,1024]{2,1,0:T(8,128)(2,1)} collective-permute-done((bf16[1,512,1024]{2,1,0:T(8,128)(2,1)}, bf16[1,512,1024]{2,1,0:T(8,128)(2,1)}, u32[]{:S(2)}, u32[]{:S(2)}) %collective-permute-start.15) | collective-permute-done | bytes 1048608 | tf_op jit(solution)/shard_map/ppermute | solution.py:561
  656.0 4.2 fusion.16
  670.0 26.7 %collective-permute-done.37 = f32[8,128]{1,0:T(8,128)S(1)} collective-permute-done((f32[8,128]{1,0:T(8,128)S(1)}, f32[8,128]{1,0:T(8,128)S(1)}, u32[]{:S(2)}, u32[]{:S(2)}) %collective-permute-start.37) | collective-permute-done | bytes 4128 | tf_op jit(solution)/shard_map/ppermute | solution.py:561
  696.7 5.4 collective-permute-start.17
  705.0 3.4 collective-permute-start.38
  711.9 13.9 %collective-permute-done.17 = bf16[1,128,1024]{2,1,0:T(8,128)(2,1)} collective-permute-done((bf16[1,128,1024]{2,1,0:T(8,128)(2,1)}, bf16[1,128,1024]{2,1,0:T(8,128)(2,1)}, u32[]{:S(2)}, u32[]{:S(2)}) %collective-permute-start.17) | collective-permute-done | bytes 262176 | tf_op jit(solution)/shard_map/ppermute | solution.py:561
  726.7 14.6 %collective-permute-done.18 = bf16[1,128,1024]{2,1,0:T(8,128)(2,1)} collective-permute-done((bf16[1,128,1024]{2,1,0:T(8,128)(2,1)}, bf16[1,128,1024]{2,1,0:T(8,128)(2,1)}, u32[]{:S(2)}, u32[]{:S(2)}) %collective-permute-start.18) | collective-permute-done | bytes 262176 | tf_op jit(solution)/shard_map/ppermute | solution.py:561
  742.3 57.1 %reduce-scatter.5.cloned.1.call-done = bf16[256,1152]{0,1:T(8,128)(2,1)} async-done(((bf16[2048,1152]{0,1:T(8,128)(2,1)}), bf16[256,1152]{0,1:T(8,128)(2,1)}) %reduce-scatter.5.cloned.1.call-update) | async-done | bytes 589840 | tf_op jit(solution)/shard_map/reduce_scatter | solution.py:713
  802.8 14.4 %collective-permute-done.45 = bf16[256,1152]{0,1:T(8,128)(2,1)S(1)} collective-permute-done((bf16[256,1152]{0,1:T(8,128)(2,1)}, bf16[256,1152]{0,1:T(8,128)(2,1)S(1)}, u32[]{:S(2)}, u32[]{:S(2)}) %collective-permute-start.45) | collective-permute-done | bytes 589856 | tf_op jit(solution)/shard_map/ppermute | solution.py:671
  (423 shorter events, 170.1 us)
Async XLA Ops:
  7.2 135.8 %all-gather.3.cloned.1.call-start = ((), (), s32[]{:S(2)}) async-start(), calls=%async_computation.2 | async-start | bytes 4128768 | tf_op jit(solution)/shard_map/all_gather | solution.py:685
  13.2 15.4 %collective-permute-start.6 = (bf16[256,896]{1,0:T(8,128)(2,1)S(1)}, bf16[256,896]{1,0:T(8,128)(2,1)S(1)}, u32[]{:S(2)}, u32[]{:S(2)}) collective-permute-start(bf16[256,896]{1,0:T(8,128)(2,1)S(1)} %bitcast.256), channel_id=1, source_target_pairs={{1,4},{3,6},{4,1},{6,3},{9,12},{11,14},{12,9},{14,11},{17,20},{19,... | collective-permute-start | bytes 1376264 | tf_op jit(solution)/shard_map/ppermute | solution.py:671
  29.4 189.8 %all-gather.5.cloned.1.call-start = ((), (), s32[]{:S(2)}) async-start(), calls=%async_computation.3 | async-start | bytes 6488064 | tf_op jit(solution)/shard_map/all_gather | solution.py:685
  30.7 1.7 collective-permute-start.8
  32.8 34.9 %collective-permute-start.9 = (bf16[256,1408]{1,0:T(8,128)(2,1)S(1)}, bf16[256,1408]{1,0:T(8,128)(2,1)S(1)}, u32[]{:S(2)}, u32[]{:S(2)}) collective-permute-start(bf16[256,1408]{1,0:T(8,128)(2,1)S(1)} %bitcast.249), channel_id=1, source_target_pairs={{1,4},{3,6},{4,1},{6,3},{9,12},{11,14},{12,9},{14,11},{17,20},{19,... | collective-permute-start | bytes 2162696 | tf_op jit(solution)/shard_map/ppermute | solution.py:671
  68.7 636.2 %reduce-scatter.3.cloned.1.call-start = ((), (), s32[]{:S(2)}) async-start(), calls=%async_computation.4 | async-start | bytes 5308416 | tf_op jit(solution)/shard_map/reduce_scatter | solution.py:713
  69.0 12.5 %collective-permute-start = (bf16[1,128,1024]{2,1,0:T(8,128)(2,1)S(1)}, bf16[1,128,1024]{2,1,0:T(8,128)(2,1)S(1)}, u32[]{:S(2)}, u32[]{:S(2)}) collective-permute-start(bf16[1,128,1024]{2,1,0:T(8,128)(2,1)S(1)} %get-tuple-element.194), channel_id=1, source_target_pairs={{0,1},{1,0},{2,3},{3,2},{4,5},{5,4},{6,7},{7,6},{8,9},{9,8},{10,11... | collective-permute-start | bytes 786440 | tf_op jit(solution)/shard_map/ppermute | solution.py:561
  69.1 36.7 %collective-permute-start.1 = (bf16[1,128,1024]{2,1,0:T(8,128)(2,1)S(1)}, bf16[1,128,1024]{2,1,0:T(8,128)(2,1)S(1)}, u32[]{:S(2)}, u32[]{:S(2)}) collective-permute-start(bf16[1,128,1024]{2,1,0:T(8,128)(2,1)S(1)} %get-tuple-element.196), channel_id=1, source_target_pairs={{0,2},{1,3},{2,0},{3,1},{4,6},{5,7},{6,4},{7,5},{8,10},{9,11},{10,... | collective-permute-start | bytes 786440 | tf_op jit(solution)/shard_map/ppermute | solution.py:561
  72.7 47.6 %collective-permute-start.2 = (bf16[1,128,1024]{2,1,0:T(8,128)(2,1)S(1)}, bf16[1,128,1024]{2,1,0:T(8,128)(2,1)S(1)}, u32[]{:S(2)}, u32[]{:S(2)}) collective-permute-start(bf16[1,128,1024]{2,1,0:T(8,128)(2,1)S(1)} %get-tuple-element.193), channel_id=1, source_target_pairs={{0,3},{1,2},{2,1},{3,0},{4,7},{5,6},{6,5},{7,4},{8,11},{9,10},{10,... | collective-permute-start | bytes 786440 | tf_op jit(solution)/shard_map/ppermute | solution.py:561
  73.9 68.6 %collective-permute-start.7 = (f32[1,7]{1,0:T(1,128)S(1)}, f32[1,7]{1,0:T(1,128)S(1)}, u32[]{:S(2)}, u32[]{:S(2)}) collective-permute-start(f32[1,7]{1,0:T(1,128)S(1)} %fusion.44), channel_id=1, source_target_pairs={{0,8},{8,0},{1,9},{9,1},{2,10},{10,2},{3,11},{11,3},{4,12},{12,4},... | collective-permute-start | bytes 92 | tf_op jit(solution)/shard_map/ppermute | solution.py:561
  123.5 17.6 %collective-permute-start.3 = (bf16[1,512,1024]{2,1,0:T(8,128)(2,1)S(1)}, bf16[1,512,1024]{2,1,0:T(8,128)(2,1)S(1)}, u32[]{:S(2)}, u32[]{:S(2)}) collective-permute-start(bf16[1,512,1024]{2,1,0:T(8,128)(2,1)S(1)} %get-tuple-element.153), channel_id=1, source_target_pairs={{0,4},{4,0},{1,5},{5,1},{2,6},{6,2},{3,7},{7,3},{8,12},{12,8},{9,1... | collective-permute-start | bytes 3145736 | tf_op jit(solution)/shard_map/ppermute | solution.py:561
  142.1 4.5 collective-permute-start.4
  226.9 4.2 collective-permute-start.10
  232.2 29.4 %collective-permute-start.11 = (bf16[1,512,1024]{2,1,0:T(8,128)(2,1)S(1)}, bf16[1,512,1024]{2,1,0:T(8,128)(2,1)S(1)}, u32[]{:S(2)}, u32[]{:S(2)}) collective-permute-start(bf16[1,512,1024]{2,1,0:T(8,128)(2,1)S(1)} %constant_dynamic-slice_fusion.12), channel_id=1, source_target_pairs={{0,4},{4,0},{1,5},{5,1},{2,6},{6,2},{3,7},{7,3},{8,12},{12,8},{9,1... | collective-permute-start | bytes 3145736 | tf_op jit(solution)/shard_map/ppermute | solution.py:561
  234.0 12.5 %collective-permute-start.19 = (bf16[1,128,1024]{2,1,0:T(8,128)(2,1)S(1)}, bf16[1,128,1024]{2,1,0:T(8,128)(2,1)S(1)}, u32[]{:S(2)}, u32[]{:S(2)}) collective-permute-start(bf16[1,128,1024]{2,1,0:T(8,128)(2,1)S(1)} %get-tuple-element.186), channel_id=1, source_target_pairs={{0,1},{1,0},{2,3},{3,2},{4,5},{5,4},{6,7},{7,6},{8,9},{9,8},{10,11... | collective-permute-start | bytes 786440 | tf_op jit(solution)/shard_map/ppermute | solution.py:561
  235.8 19.5 %collective-permute-start.20 = (bf16[1,128,1024]{2,1,0:T(8,128)(2,1)S(1)}, bf16[1,128,1024]{2,1,0:T(8,128)(2,1)S(1)}, u32[]{:S(2)}, u32[]{:S(2)}) collective-permute-start(bf16[1,128,1024]{2,1,0:T(8,128)(2,1)S(1)} %get-tuple-element.188), channel_id=1, source_target_pairs={{0,2},{1,3},{2,0},{3,1},{4,6},{5,7},{6,4},{7,5},{8,10},{9,11},{10,... | collective-permute-start | bytes 786440 | tf_op jit(solution)/shard_map/ppermute | solution.py:561
  237.3 23.0 %collective-permute-start.21 = (bf16[1,128,1024]{2,1,0:T(8,128)(2,1)S(1)}, bf16[1,128,1024]{2,1,0:T(8,128)(2,1)S(1)}, u32[]{:S(2)}, u32[]{:S(2)}) collective-permute-start(bf16[1,128,1024]{2,1,0:T(8,128)(2,1)S(1)} %get-tuple-element.185), channel_id=1, source_target_pairs={{0,3},{1,2},{2,1},{3,0},{4,7},{5,6},{6,5},{7,4},{8,11},{9,10},{10,... | collective-permute-start | bytes 786440 | tf_op jit(solution)/shard_map/ppermute | solution.py:561
  260.4 26.2 %collective-permute-start.22 = (bf16[1,512,1024]{2,1,0:T(8,128)(2,1)S(1)}, bf16[1,512,1024]{2,1,0:T(8,128)(2,1)S(1)}, u32[]{:S(2)}, u32[]{:S(2)}) collective-permute-start(bf16[1,512,1024]{2,1,0:T(8,128)(2,1)S(1)} %constant_dynamic-update-slice_fusion.7), channel_id=1, source_target_pairs={{0,4},{4,0},{1,5},{5,1},{2,6},{6,2},{3,7},{7,3},{8,12},{12,8},{9,1... | collective-permute-start | bytes 3145736 | tf_op jit(solution)/shard_map/ppermute | solution.py:561
  262.8 44.0 %collective-permute-start.12 = (bf16[1,512,1024]{2,1,0:T(8,128)(2,1)S(1)}, bf16[1,512,1024]{2,1,0:T(8,128)(2,1)S(1)}, u32[]{:S(2)}, u32[]{:S(2)}) collective-permute-start(bf16[1,512,1024]{2,1,0:T(8,128)(2,1)S(1)} %get-tuple-element.149), channel_id=1, source_target_pairs={{0,4},{4,0},{1,5},{5,1},{2,6},{6,2},{3,7},{7,3},{8,12},{12,8},{9,1... | collective-permute-start | bytes 3145736 | tf_op jit(solution)/shard_map/ppermute | solution.py:561
  286.7 20.4 %collective-permute-start.23 = (bf16[1,1024,1024]{2,1,0:T(8,128)(2,1)S(1)}, bf16[1,1024,1024]{2,1,0:T(8,128)(2,1)S(1)}, u32[]{:S(2)}, u32[]{:S(2)}) collective-permute-start(bf16[1,1024,1024]{2,1,0:T(8,128)(2,1)S(1)} %constant_dynamic-update-slice_fusion.5), channel_id=1, source_target_pairs={{0,8},{8,0},{1,9},{9,1},{2,10},{10,2},{3,11},{11,3},{4,12},{12,4},... | collective-permute-start | bytes 6291464 | tf_op jit(solution)/shard_map/ppermute | solution.py:561
  307.0 4.8 collective-permute-start.13
  346.8 4.3 collective-permute-start.24
  352.2 25.5 %collective-permute-start.25 = (bf16[1,512,1024]{2,1,0:T(8,128)(2,1)S(1)}, bf16[1,512,1024]{2,1,0:T(8,128)(2,1)S(1)}, u32[]{:S(2)}, u32[]{:S(2)}) collective-permute-start(bf16[1,512,1024]{2,1,0:T(8,128)(2,1)S(1)} %constant_dynamic-slice_fusion.4), channel_id=1, source_target_pairs={{0,4},{4,0},{1,5},{5,1},{2,6},{6,2},{3,7},{7,3},{8,12},{12,8},{9,1... | collective-permute-start | bytes 3145736 | tf_op jit(solution)/shard_map/ppermute | solution.py:561
  380.5 34.3 %collective-permute-start.26 = (bf16[1,512,1024]{2,1,0:T(8,128)(2,1)}, bf16[1,512,1024]{2,1,0:T(8,128)(2,1)}, u32[]{:S(2)}, u32[]{:S(2)}) collective-permute-start(bf16[1,512,1024]{2,1,0:T(8,128)(2,1)} %get-tuple-element.147), channel_id=1, source_target_pairs={{0,4},{4,0},{1,5},{5,1},{2,6},{6,2},{3,7},{7,3},{8,12},{12,8},{9,1... | collective-permute-start | bytes 3145736 | tf_op jit(solution)/shard_map/ppermute | solution.py:561
  417.1 32.7 %collective-permute-start.27 = (bf16[1,1024,1024]{2,1,0:T(8,128)(2,1)}, bf16[1,1024,1024]{2,1,0:T(8,128)(2,1)}, u32[]{:S(2)}, u32[]{:S(2)}) collective-permute-start(bf16[1,1024,1024]{2,1,0:T(8,128)(2,1)} %constant_dynamic-update-slice_fusion.3), channel_id=1, source_target_pairs={{0,8},{8,0},{1,9},{9,1},{2,10},{10,2},{3,11},{11,3},{4,12},{12,4},... | collective-permute-start | bytes 6291464 | tf_op jit(solution)/shard_map/ppermute | solution.py:561
  570.2 229.2 %reduce-scatter.5.cloned.1.call-start = ((), (), s32[]{:S(2)}) async-start(), calls=%async_computation.5 | async-start | bytes 5308416 | tf_op jit(solution)/shard_map/reduce_scatter | solution.py:713
  590.8 15.4 %collective-permute-start.28 = (bf16[1,1024,1024]{2,1,0:T(8,128)(2,1)}, bf16[1,1024,1024]{2,1,0:T(8,128)(2,1)S(1)}, u32[]{:S(2)}, u32[]{:S(2)}) collective-permute-start(bf16[1,1024,1024]{2,1,0:T(8,128)(2,1)} %slice_bitcast_fusion), channel_id=1, source_target_pairs={{0,8},{8,0},{1,9},{9,1},{2,10},{10,2},{3,11},{11,3},{4,12},{12,4},... | collective-permute-start | bytes 6291464 | tf_op jit(solution)/shard_map/ppermute | solution.py:561
  592.8 16.7 %collective-permute-start.14 = (bf16[1,1024,1024]{2,1,0:T(8,128)(2,1)}, bf16[1,1024,1024]{2,1,0:T(8,128)(2,1)}, u32[]{:S(2)}, u32[]{:S(2)}) collective-permute-start(bf16[1,1024,1024]{2,1,0:T(8,128)(2,1)} %slice_bitcast_fusion.4), channel_id=1, source_target_pairs={{0,8},{8,0},{1,9},{9,1},{2,10},{10,2},{3,11},{11,3},{4,12},{12,4},... | collective-permute-start | bytes 6291464 | tf_op jit(solution)/shard_map/ppermute | solution.py:561
  595.4 6.3 collective-permute-start.41
  601.7 4.4 collective-permute-start.42
  606.1 7.2 collective-permute-start.43
  609.1 26.2 %collective-permute-start.29 = (bf16[1,512,1024]{2,1,0:T(8,128)(2,1)S(1)}, bf16[1,512,1024]{2,1,0:T(8,128)(2,1)S(1)}, u32[]{:S(2)}, u32[]{:S(2)}) collective-permute-start(bf16[1,512,1024]{2,1,0:T(8,128)(2,1)S(1)} %constant_dynamic-slice_fusion.3), channel_id=1, source_target_pairs={{0,4},{4,0},{1,5},{5,1},{2,6},{6,2},{3,7},{7,3},{8,12},{12,8},{9,1... | collective-permute-start | bytes 3145736 | tf_op jit(solution)/shard_map/ppermute | solution.py:561
  613.4 6.6 collective-permute-start.44
  618.1 38.0 %collective-permute-start.15 = (bf16[1,512,1024]{2,1,0:T(8,128)(2,1)}, bf16[1,512,1024]{2,1,0:T(8,128)(2,1)}, u32[]{:S(2)}, u32[]{:S(2)}) collective-permute-start(bf16[1,512,1024]{2,1,0:T(8,128)(2,1)} %constant_dynamic-slice_fusion.11), channel_id=1, source_target_pairs={{0,4},{4,0},{1,5},{5,1},{2,6},{6,2},{3,7},{7,3},{8,12},{12,8},{9,1... | collective-permute-start | bytes 3145736 | tf_op jit(solution)/shard_map/ppermute | solution.py:561
  636.3 2.5 collective-permute-start.33
  638.7 3.6 collective-permute-start.34
  642.4 17.9 %collective-permute-start.35 = (f32[8,128]{1,0:T(8,128)S(1)}, f32[8,128]{1,0:T(8,128)S(1)}, u32[]{:S(2)}, u32[]{:S(2)}) collective-permute-start(f32[8,128]{1,0:T(8,128)S(1)} %fusion.96), channel_id=1, source_target_pairs={{0,4},{4,0},{1,5},{5,1},{2,6},{6,2},{3,7},{7,3},{8,12},{12,8},{9,1... | collective-permute-start | bytes 12296 | tf_op jit(solution)/shard_map/ppermute | solution.py:561
  660.3 6.0 collective-permute-start.36
  662.8 39.9 %collective-permute-start.30 = (bf16[1,128,1024]{2,1,0:T(8,128)(2,1)S(1)}, bf16[1,128,1024]{2,1,0:T(8,128)(2,1)S(1)}, u32[]{:S(2)}, u32[]{:S(2)}) collective-permute-start(bf16[1,128,1024]{2,1,0:T(8,128)(2,1)S(1)} %get-tuple-element.183), channel_id=1, source_target_pairs={{0,1},{1,0},{2,3},{3,2},{4,5},{5,4},{6,7},{7,6},{8,9},{9,8},{10,11... | collective-permute-start | bytes 786440 | tf_op jit(solution)/shard_map/ppermute | solution.py:561
  663.3 41.0 %collective-permute-start.31 = (bf16[1,128,1024]{2,1,0:T(8,128)(2,1)S(1)}, bf16[1,128,1024]{2,1,0:T(8,128)(2,1)S(1)}, u32[]{:S(2)}, u32[]{:S(2)}) collective-permute-start(bf16[1,128,1024]{2,1,0:T(8,128)(2,1)S(1)} %get-tuple-element.182), channel_id=1, source_target_pairs={{0,2},{1,3},{2,0},{3,1},{4,6},{5,7},{6,4},{7,5},{8,10},{9,11},{10,... | collective-permute-start | bytes 786440 | tf_op jit(solution)/shard_map/ppermute | solution.py:561
  665.5 43.8 %collective-permute-start.32 = (bf16[1,128,1024]{2,1,0:T(8,128)(2,1)}, bf16[1,128,1024]{2,1,0:T(8,128)(2,1)S(1)}, u32[]{:S(2)}, u32[]{:S(2)}) collective-permute-start(bf16[1,128,1024]{2,1,0:T(8,128)(2,1)} %get-tuple-element.181), channel_id=1, source_target_pairs={{0,3},{1,2},{2,1},{3,0},{4,7},{5,6},{6,5},{7,4},{8,11},{9,10},{10,... | collective-permute-start | bytes 786440 | tf_op jit(solution)/shard_map/ppermute | solution.py:561
  666.3 30.4 %collective-permute-start.37 = (f32[8,128]{1,0:T(8,128)S(1)}, f32[8,128]{1,0:T(8,128)S(1)}, u32[]{:S(2)}, u32[]{:S(2)}) collective-permute-start(f32[8,128]{1,0:T(8,128)S(1)} %add.250), channel_id=1, source_target_pairs={{0,2},{1,3},{2,0},{3,1},{4,6},{5,7},{6,4},{7,5},{8,10},{9,11},{10,... | collective-permute-start | bytes 12296 | tf_op jit(solution)/shard_map/ppermute | solution.py:561
  669.4 41.6 %collective-permute-start.16 = (bf16[1,128,1024]{2,1,0:T(8,128)(2,1)}, bf16[1,128,1024]{2,1,0:T(8,128)(2,1)}, u32[]{:S(2)}, u32[]{:S(2)}) collective-permute-start(bf16[1,128,1024]{2,1,0:T(8,128)(2,1)} %get-tuple-element.191), channel_id=1, source_target_pairs={{0,1},{1,0},{2,3},{3,2},{4,5},{5,4},{6,7},{7,6},{8,9},{9,8},{10,11... | collective-permute-start | bytes 786440 | tf_op jit(solution)/shard_map/ppermute | solution.py:561
  696.7 29.1 %collective-permute-start.17 = (bf16[1,128,1024]{2,1,0:T(8,128)(2,1)}, bf16[1,128,1024]{2,1,0:T(8,128)(2,1)}, u32[]{:S(2)}, u32[]{:S(2)}) collective-permute-start(bf16[1,128,1024]{2,1,0:T(8,128)(2,1)} %get-tuple-element.190), channel_id=1, source_target_pairs={{0,2},{1,3},{2,0},{3,1},{4,6},{5,7},{6,4},{7,5},{8,10},{9,11},{10,... | collective-permute-start | bytes 786440 | tf_op jit(solution)/shard_map/ppermute | solution.py:561
  702.7 38.6 %collective-permute-start.18 = (bf16[1,128,1024]{2,1,0:T(8,128)(2,1)}, bf16[1,128,1024]{2,1,0:T(8,128)(2,1)}, u32[]{:S(2)}, u32[]{:S(2)}) collective-permute-start(bf16[1,128,1024]{2,1,0:T(8,128)(2,1)} %get-tuple-element.189), channel_id=1, source_target_pairs={{0,3},{1,2},{2,1},{3,0},{4,7},{5,6},{6,5},{7,4},{8,11},{9,10},{10,... | collective-permute-start | bytes 786440 | tf_op jit(solution)/shard_map/ppermute | solution.py:561
  705.0 97.6 %collective-permute-start.38 = (bf16[256,1152]{0,1:T(8,128)(2,1)}, bf16[256,1152]{0,1:T(8,128)(2,1)S(1)}, u32[]{:S(2)}, u32[]{:S(2)}) collective-permute-start(bf16[256,1152]{0,1:T(8,128)(2,1)} %reduce-scatter.3.cloned.1.call-done), channel_id=1, source_target_pairs={{1,4},{3,6},{4,1},{6,3},{9,12},{11,14},{12,9},{14,11},{17,20},{19,... | collective-permute-start | bytes 1769480 | tf_op jit(solution)/shard_map/ppermute | solution.py:671
  799.4 17.9 %collective-permute-start.45 = (bf16[256,1152]{0,1:T(8,128)(2,1)}, bf16[256,1152]{0,1:T(8,128)(2,1)S(1)}, u32[]{:S(2)}, u32[]{:S(2)}) collective-permute-start(bf16[256,1152]{0,1:T(8,128)(2,1)} %reduce-scatter.5.cloned.1.call-done), channel_id=1, source_target_pairs={{1,4},{3,6},{4,1},{6,3},{9,12},{11,14},{12,9},{14,11},{17,20},{19,... | collective-permute-start | bytes 1769480 | tf_op jit(solution)/shard_map/ppermute | solution.py:671
  802.7 14.7 %collective-permute-start.39 = (bf16[128,1152]{0,1:T(8,128)(2,1)S(1)}, bf16[128,1152]{0,1:T(8,128)(2,1)S(1)}, u32[]{:S(2)}, u32[]{:S(2)}) collective-permute-start(bf16[128,1152]{0,1:T(8,128)(2,1)S(1)} %broadcast_select_fusion.8), channel_id=1, source_target_pairs={{0,8},{8,0},{1,9},{9,1},{2,10},{10,2},{3,11},{11,3},{4,12},{12,4},... | collective-permute-start | bytes 884744 | tf_op jit(solution)/shard_map/ppermute | solution.py:561
  (62 other events, 1334.8 us)
Sparse Core Ops, SparseCore 0:
  29.5 94.7 all-gather.2
  126.5 92.7 all-gather.4
  570.3 99.1 reduce-scatter.2
  673.0 126.3 reduce-scatter.4

commit v3 on v2

--- a/solution.py
+++ b/solution.py
@@ -644,17 +644,23 @@
     return with_partner(both)
 
 
-def sum_in_group(partial_sums):
-    side = lax.axis_index("cl")
+def sum_of_cores(partial_sums):
     half = partial_sums.shape[0] // 2
     received = swapped(partial_sums[half:], "core", 1)
-    both = (partial_sums[:half].astype(jnp.float32) + received.astype(jnp.float32)).astype(
-        partial_sums.dtype
-    )
+    both = partial_sums[:half].astype(jnp.float32) + received.astype(jnp.float32)
+    return both.astype(partial_sums.dtype)
+
+
+def sum_of_sides(both):
+    side = lax.axis_index("cl")
     tokens = both.shape[1] // 2
     mine = lax.dynamic_slice_in_dim(both, side * tokens, tokens, 1)
     other = lax.dynamic_slice_in_dim(both, (1 - side) * tokens, tokens, 1)
     return mine.astype(jnp.float32) + swapped(other, "cl", 1).astype(jnp.float32)
+
+
+def sum_in_group(partial_sums):
+    return sum_of_sides(sum_of_cores(partial_sums))
 
 
 SPREAD = ("tensor", "px", "cg")
@@ -684,28 +690,47 @@
     pair = traded(pair.reshape(2 * rows, cols))
     full = lax.all_gather(pair, SPREAD, axis=0, tiled=True)
     lanes, px, groups = (lax.axis_size(axis) for axis in SPREAD)
-    return full.reshape(lanes // 2, 2, px, groups, 2, rows, cols)
+    return full.reshape(lanes // 2, 4 * px * groups * rows, cols)
 
 
 def whole_rows(gathered, first, width):
-    pieces = [
-        jnp.transpose(part[..., first : first + width], (1, 3, 2, 0, 4, 5)).reshape(-1, width)
-        for part in gathered
-    ]
-    return jnp.concatenate(pieces, 1)
-
-
-def split_rows(grad):
+    return jnp.concatenate([part[:, first : first + width] for part in gathered], 1)
+
+
+def block_order():
     px, groups = lax.axis_size("px"), lax.axis_size("cg")
-    rows = grad.shape[0] // (4 * px * groups)
-    shaped = grad.reshape(px, 2, groups, 2, rows, grad.shape[1])
-    return jnp.transpose(shaped, (3, 0, 2, 1, 4, 5)).reshape(-1, grad.shape[1])
+    return [
+        ((place * 2 + core) * groups + group) * 2 + side
+        for side in range(2)
+        for place in range(px)
+        for group in range(groups)
+        for core in range(2)
+    ]
+
+
+def reordered(array, order):
+    width = array.shape[-1] // len(order)
+    return jnp.concatenate([array[..., n * width : (n + 1) * width] for n in order], -1)
+
+
+def to_gather_order(array):
+    return reordered(array, block_order())
+
+
+def to_model_order(array):
+    order = block_order()
+    return reordered(array, [order.index(n) for n in range(len(order))])
 
 
 def joined_grads(by_k):
-    return jnp.concatenate(
-        [jnp.concatenate([split_rows(part) for part in parts], 1) for parts in by_k], 0
-    )
+    by_k = [list(parts) for parts in by_k]
+    rows = by_k[0][0].shape[0]
+    widths = [part.shape[1] for part in by_k[0]]
+    joined = jnp.zeros((rows * len(by_k), sum(widths)), by_k[0][0].dtype)
+    for n, parts in enumerate(by_k):
+        for place, part in enumerate(parts):
+            joined = lax.dynamic_update_slice(joined, part, (n * rows, sum(widths[:place])))
+    return joined
 
 
 def scatter_grads(joined):
@@ -806,12 +831,18 @@
         return mine.reshape(array.shape[0], heads, width)
 
     mix_parts = gather_weights(mix_half(0), mix_half(1))
-    own = dealt_by_sequence(tokens).astype(jnp.float32)
+    dealt = dealt_by_sequence(tokens)
+    dealt, w_ffn_gate, w_ffn_up, w_ffn_down, w_out = lax.optimization_barrier(
+        (dealt, w_ffn_gate, w_ffn_up, w_ffn_down, w_out)
+    )
+    norm_gain, ffn_gain = to_gather_order(norm_gain), to_gather_order(ffn_gain)
+    own = to_gather_order(dealt).astype(jnp.float32)
     normed_own = (rms_rows(own) * norm_gain).astype(low)
     normed = with_group(normed_own).reshape(flat, model)
     rest_parts = gather_weights(rest_half(0), rest_half(1))
     w_mix = whole_rows(mix_parts, 0, per_quarter * HEAD)
     pre = matmul(normed, w_mix).reshape(seqs, length, heads * HEAD)
+    pre, d_mixed = lax.optimization_barrier((pre, d_mixed))
     rim = jnp.zeros((seqs, RIM, heads * HEAD), jnp.float32)
     if pieces > 1:
         rim = passed_along(pre[:, length - RIM :], "cg", 1)
@@ -835,7 +866,6 @@
     gain_row = out_gain[None]
     front = (pre, rim, taps, par, segs)
     cot_own = dealt_by_sequence(d_mixed)
-    cot = with_group(cot_own).reshape(flat, model)
     if pieces == 1:
         inverse, step, read, states, mixer, gated = run_whole(*front, gain_row)
     else:
@@ -848,6 +878,9 @@
             state_in,
         )
         states, mixer, gated = run_output(state_in, step, push, read, base_out, pre, gain_row)
+    gated, cot_own = lax.optimization_barrier((gated, cot_own))
+    cot_own = to_gather_order(cot_own)
+    cot = with_group(cot_own)
     gated_flat = gated.reshape(flat, heads * VAL)
     w_pair = jnp.concatenate(
         [whole_rows(rest_parts, 0, wide), whole_rows(rest_parts, wide, wide)], 1
@@ -855,6 +888,8 @@
     w_down_t = whole_rows(rest_parts, 2 * wide, wide)
     w_out_t = whole_rows(rest_parts, 3 * wide, val_cols)
     attn_part = matmul_right_t(gated_flat, w_out_t).astype(low)
+    attn_part, cot = lax.optimization_barrier((attn_part, cot))
+    cot = cot.reshape(flat, model)
     middle = own + sum_in_group(attn_part.reshape(seqs, length, model))
     normed_two_own = (rms_rows(middle) * ffn_gain).astype(low)
     normed_two = with_group(normed_two_own).reshape(flat, model)
@@ -882,7 +917,9 @@
         )
     )
     d_branch = with_group(d_middle.astype(low)).reshape(flat, model)
-    d_branch, rest_joined = lax.optimization_barrier((d_branch, rest_joined))
+    ffn_part = matmul_right_t(hidden, w_down_t).astype(low)
+    ffn_both = sum_of_cores(ffn_part.reshape(seqs, length, model))
+    d_branch, rest_joined, ffn_both = lax.optimization_barrier((d_branch, rest_joined, ffn_both))
     rest_first, rest_second = scatter_grads(rest_joined)
     d_gated = matmul(d_branch, w_out_t).reshape(seqs, length, heads * VAL)
     if pieces == 1:
@@ -897,10 +934,10 @@
             d_end,
         )
         ends = (pull, d_end)
-    ffn_part = matmul_right_t(hidden, w_down_t).astype(low)
-    ffn_own = sum_in_group(ffn_part.reshape(seqs, length, model))
-    mixed = dealt_by_tokens((middle + ffn_own).astype(low))
+    ffn_own = sum_of_sides(ffn_both)
     d_all, d_rim, d_small = run_back(*front, inverse, step, states, d_gated, mixer, gain_row, *ends)
+    d_all, ffn_own = lax.optimization_barrier((d_all, ffn_own))
+    mixed = dealt_by_tokens(to_model_order((middle + ffn_own).astype(low)))
     if pieces > 1:
         back_rim = passed_along(d_rim, "cg", -1).reshape(seqs, RIM, heads, GATE_AT)
         back_rim = jnp.pad(back_rim, ((0, 0),) * 3 + ((0, HEAD - GATE_AT),))
@@ -910,12 +947,17 @@
     grad_mix = matmul_left_t(normed, d_all).astype(low)
     grad_out = matmul_left_t(d_branch, gated_flat).astype(low)
     mix_joined = joined_grads(zip(columns_of(grad_mix, groups), columns_of(grad_out, groups)))
+    mix_joined, rest_first, rest_second, d_all = lax.optimization_barrier(
+        (mix_joined, rest_first, rest_second, d_all)
+    )
     mix_first, mix_second = scatter_grads(mix_joined)
     d_normed = matmul_right_t(d_all, w_mix).astype(low)
     own_d_normed = sum_in_group(d_normed.reshape(seqs, length, model))
     _, norm_back = jax.vjp(norm_scaled, own, norm_gain)
     d_own, grad_norm_gain = norm_back(own_d_normed)
-    grad_tokens = dealt_by_tokens((d_middle + d_own).astype(low)).astype(jnp.float32)
+    grad_tokens = dealt_by_tokens(to_model_order((d_middle + d_own).astype(low)))
+    grad_tokens = grad_tokens.astype(jnp.float32)
+    grad_norm_gain, grad_ffn_gain = to_model_order(grad_norm_gain), to_model_order(grad_ffn_gain)
 
     small = jnp.sum(d_small, axis=0)
 

time: 840 us -> 724 us (0.86)
  waiting for transfers between devices: 391 us -> 322 us
  local copies, waits for them, and re-layouts: 112 us -> 71.8 us
  other arithmetic: 60.4 us -> 49.2 us
    ppermute x43, waiting for transfers between devices: 264 us -> 196 us  [swapped(): lax.ppermute(value, axis, [(place, place ^ bits) for place in range(count)])]
    all_gather x2, waiting for transfers between devices: 10.7 us -> 42.9 us  [gather_weights(): full = lax.all_gather(pair, SPREAD, axis=0, tiled=True)]
    reshape x10 -> x0, local copies, waits for them, and re-layouts: 29.8 us -> none  [split_rows(): return jnp.transpose(shaped, (3, 0, 2, 1, 4, 5)).reshape(-1, grad.shape[1])]
    transpose x12 -> x2, local copies, waits for them, and re-layouts: 29.1 us -> 0.11 us  [the longest x1 0.1 us: rest_half(): parts = [w_ffn_gate[:, inner], w_ffn_up[:, inner], w_ffn_down[inner].T]]
    concatenate x2 -> x0, other arithmetic: 28.3 us -> none  [joined_grads(): jnp.concatenate([jnp.concatenate([split_rows(part) for part in parts], 1)...]
    ppermute x4, waiting for transfers between devices: 57.9 us -> 34.3 us  [traded(): received = lax.ppermute(value, ('cl', 'tensor'), pairs)]
    dynamic_update_slice x0 -> x10, local copies, waits for them, and re-layouts: none -> 13.3 us  [joined_grads(): lax.dynamic_update_slice(joined, part, (n * rows, sum(widths[:place])))]
    reduce_scatter x2, waiting for transfers between devices: 57.1 us -> 48 us  [scatter_grads(): lax.psum_scatter(joined, SPREAD, scatter_dimension=0, tiled=True)]
  transfers between devices with their start and end apart: 51 -> 51, of which waited for: 32 -> 27; matrix products, arithmetic and copies ran while one was open for 17% -> 20% of each run, Pallas kernels for 6% -> 15%
where the time goes in v3:
time: 724 us; the launch traced here: 712 us
  waiting for transfers between devices  322 us (44%)
  Pallas kernels  103 us (14%)
  matrix products  102 us (14%)
  local copies, waits for them, and re-layouts  71.8 us (10%)
  other arithmetic  49.2 us (7%)
  starting transfers between devices  46.8 us (6%)
  between operations  16.5 us (2%)
    ppermute x43, waiting for transfers between devices, swapped(): lax.ppermute(value, axis, [(place, place ^ bits) for place in range(count)])  196 us
    pallas_call x2, Pallas kernels, call(): pl.pallas_call(kernel, grid=lead, in_specs=in_specs, out_specs=[spec for...  103 us
    reduce_scatter x2, waiting for transfers between devices, scatter_grads(): lax.psum_scatter(joined, SPREAD, scatter_dimension=0, tiled=True)  48 us
    all_gather x2, waiting for transfers between devices, gather_weights(): full = lax.all_gather(pair, SPREAD, axis=0, tiled=True)  42.9 us
    dot_general x4, matrix products, matmul(): return lax.dot_general(left, right, NN, preferred_element_type=jnp.float32)  42.1 us
    ppermute x4, waiting for transfers between devices, traded(): received = lax.ppermute(value, ('cl', 'tensor'), pairs)  34.3 us
    ppermute x43, starting transfers between devices, swapped(): lax.ppermute(value, axis, [(place, place ^ bits) for place in range(count)])  33.8 us
    dot_general x4, matrix products, matmul_left_t(): return lax.dot_general(left, right, TN, preferred_element_type=jnp.float32)  30.8 us
  transfers between devices with their start and end apart: 51, of which 27 were waited for; matrix products, arithmetic and copies ran while one was open for 20% of the time, Pallas kernels for 15%

profile of v3, /device:TPU:8, one launch (start us, length us, event | category | flops | bytes accessed | tf_op | source)
XLA Modules:
  0.0 711.7 jit_solution(3791701111985640909)
XLA Ops:
  12.5 3.0 collective-permute-start.1
  18.1 4.2 collective-permute-start.6
  22.4 21.1 %collective-permute-done.6 = bf16[256,896]{1,0:T(8,128)(2,1)S(1)} collective-permute-done((bf16[256,896]{1,0:T(8,128)(2,1)S(1)}, bf16[256,896]{1,0:T(8,128)(2,1)S(1)}, u32[]{:S(2)}, u32[]{:S(2)}) %collective-permute-start.6) | collective-permute-done | bytes 458784 | tf_op jit(solution)/shard_map/ppermute | solution.py:677
  53.6 37.6 %collective-permute-done.3 = bf16[1,512,1024]{2,1,0:T(8,128)(2,1)S(1)} collective-permute-done((bf16[1,512,1024]{2,1,0:T(8,128)(2,1)}, bf16[1,512,1024]{2,1,0:T(8,128)(2,1)S(1)}, u32[]{:S(2)}, u32[]{:S(2)}) %collective-permute-start.3) | collective-permute-done | bytes 1048608 | tf_op jit(solution)/shard_map/ppermute | solution.py:561
  95.3 29.6 %all-gather.3.cloned.1.call-done = bf16[2048,896]{1,0:T(8,128)(2,1)} async-done(((bf16[256,896]{1,0:T(8,128)(2,1)}), bf16[2048,896]{1,0:T(8,128)(2,1)}) %all-gather.3.cloned.1.call-update) | async-done | bytes 3670032 | tf_op jit(solution)/shard_map/all_gather | solution.py:691
  127.3 13.7 %fusion.8.pre = f32[2,1024,1792]{2,1,0:T(8,128)} fusion(bf16[1,1024,1024]{2,1,0:T(8,128)(2,1)} %collective-permute-done.4, bf16[1,1024,1024]{2,1,0:T(8,128)(2,1)S(1)} %copy-done.22, bf16[1024,896]{1,0:T(8,128)(2,1)S(1)} %get-tuple-element.206, bf16[1024,896]{1,0:T(8,128)(2,1)S(1)} %get-tuple-element.205), kind=kOutput, calls=%fused_computation.31 | convolution fusion | flops 7525629952 | bytes 22544384 | tf_op jit(solution)/shard_map/dot_general | solution.py:586
  144.9 47.9 %shard_map.356 = (f32[2,2,1024,128]{3,2,1,0:T(8,128)S(1)}, f32[2,2,1024,128]{3,2,1,0:T(8,128)S(1)}, f32[2,2,1024,128]{3,2,1,0:T(8,128)}, f32[2,2,1024,256]{3,2,1...) custom-call(f32[2,1024,1792]{2,1,0:T(8,128)} %fusion.8.pre, ...), custom_call_target="tpu_custom_call" | custom-call | flops 9395240960 | bytes 93952408 | tf_op jit(solution)/shard_map/pallas_call | solution.py:455
  195.3 20.9 %collective-permute-done.13 = bf16[1,512,1024]{2,1,0:T(8,128)(2,1)S(1)} collective-permute-done((bf16[1,512,1024]{2,1,0:T(8,128)(2,1)S(1)}, bf16[1,512,1024]{2,1,0:T(8,128)(2,1)S(1)}, u32[]{:S(2)}, u32[]{:S(2)}) %collective-permute-start.13) | collective-permute-done | bytes 1048608 | tf_op jit(solution)/shard_map/ppermute | solution.py:561
  216.4 4.1 collective-permute-done.14
  222.9 13.3 %all-gather.5.cloned.1.call-done = bf16[2048,1408]{1,0:T(8,128)(2,1)} async-done(((bf16[256,1408]{1,0:T(8,128)(2,1)}), bf16[2048,1408]{1,0:T(8,128)(2,1)}) %all-gather.5.cloned.1.call-update) | async-done | bytes 5767184 | tf_op jit(solution)/shard_map/all_gather | solution.py:691
  237.4 4.3 convolution_convert_fusion.1
  245.3 4.5 collective-permute-done.15
  249.8 3.2 fusion.3
  254.6 23.7 %collective-permute-done.16 = bf16[1,512,1024]{2,1,0:T(8,128)(2,1)S(1)} collective-permute-done((bf16[1,512,1024]{2,1,0:T(8,128)(2,1)S(1)}, bf16[1,512,1024]{2,1,0:T(8,128)(2,1)S(1)}, u32[]{:S(2)}, u32[]{:S(2)}) %collective-permute-start.16) | collective-permute-done | bytes 1048608 | tf_op jit(solution)/shard_map/ppermute | solution.py:561
  281.0 22.9 %collective-permute-done.17 = bf16[1,512,1024]{2,1,0:T(8,128)(2,1)S(1)} collective-permute-done((bf16[1,512,1024]{2,1,0:T(8,128)(2,1)S(1)}, bf16[1,512,1024]{2,1,0:T(8,128)(2,1)S(1)}, u32[]{:S(2)}, u32[]{:S(2)}) %collective-permute-start.17) | collective-permute-done | bytes 1048608 | tf_op jit(solution)/shard_map/ppermute | solution.py:561
  304.6 3.6 collective-permute-done.18
  308.6 10.0 %fusion.29 = f32[2048,1536]{0,1:T(8,128)} fusion(bf16[2048,1024]{1,0:T(8,128)(2,1)S(1)} %bitcast.200, bf16[1024,384]{1,0:T(8,128)(2,1)S(1)} %get-tuple-element.198, bf16[1024,384]{1,0:T(8,128)(2,1)S(1)} %get-tuple-element.199, bf16[1024,384]{1,0:T(8,128)(2,1)S(1)} %get-tuple-element.200, bf16[1024,384]{1,0:T(8,128)(2,1)S(1)} %get-tuple-element.197), kind=kOutput, calls=%fused_computation.89 | convolution fusion | flops 6455033856 | bytes 19922944 | tf_op jit(solution)/shard_map/dot_general | solution.py:586
  318.7 11.9 %multiply_convert_fusion.2 = (bf16[2048,768]{0,1:T(8,128)(2,1)}, bf16[2048,768]{0,1:T(8,128)(2,1)}, bf16[2048,768]{0,1:T(8,128)(2,1)}) fusion(f32[2048,1536]{0,1:T(8,128)} %fusion.29, bf16[2048,1024]{1,0:T(8,128)(2,1)S(1)} %bitcast.196, bf16[1024,384]{1,0:T(8,128)(2,1)S(1)} %get-tuple-element.201, bf16[1024,384]{1,0:T(8,128)(2,1)S(1)} %get-tuple-element.202), kind=kOutput, calls=%fused_computation.4 | convolution fusion | flops 3249537024 | bytes 27787264 | tf_op jit(solution)/shard_map/dot_general | solution.py:586
  330.6 9.8 %fusion.6 = bf16[2048,1024]{1,0:T(8,128)(2,1)S(1)} fusion(bf16[2048,768]{0,1:T(8,128)(2,1)} %get-tuple-element.195, bf16[2048,768]{0,1:T(8,128)(2,1)} %get-tuple-element.194, bf16[1024,384]{1,0:T(8,128)(2,1)S(1)} %copy-done.34, bf16[1024,384]{1,0:T(8,128)(2,1)S(1)} %copy-done.36, bf16[1024,384]{1,0:T(8,128)(2,1)} %copy-done.37, ...), kind=kOutput, calls=%fused_computation.25 | convolution fusion | flops 6469713920 | bytes 13631488 | tf_op jit(solution)/shard_map/dot_general | solution.py:594
  340.8 4.0 collective-permute-done.19
  347.4 4.0 convolution_convert_fusion.2
  354.9 16.2 %collective-permute-done.20 = bf16[1,512,1024]{2,1,0:T(8,128)(2,1)S(1)} collective-permute-done((bf16[1,512,1024]{2,1,0:T(8,128)(2,1)S(1)}, bf16[1,512,1024]{2,1,0:T(8,128)(2,1)S(1)}, u32[]{:S(2)}, u32[]{:S(2)}) %collective-permute-start.20) | collective-permute-done | bytes 1048608 | tf_op jit(solution)/shard_map/ppermute | solution.py:561
  376.8 10.3 %fusion.7 = bf16[1024,1536]{1,0:T(8,128)(2,1)S(1)} fusion(bf16[2048,1024]{1,0:T(8,128)(2,1)S(1)} %bitcast.201, bf16[2048,768]{0,1:T(8,128)(2,1)} %get-tuple-element.195, bf16[2048,768]{0,1:T(8,128)(2,1)} %get-tuple-element.194), kind=kOutput, calls=%fused_computation.26 | convolution fusion | flops 6456606720 | bytes 13631488 | tf_op jit(solution)/shard_map/dot_general | solution.py:590
  390.8 8.9 %collective-permute-done.21 = bf16[1,512,1024]{2,1,0:T(8,128)(2,1)S(1)} collective-permute-done((bf16[1,512,1024]{2,1,0:T(8,128)(2,1)S(1)}, bf16[1,512,1024]{2,1,0:T(8,128)(2,1)S(1)}, u32[]{:S(2)}, u32[]{:S(2)}) %collective-permute-start.21) | collective-permute-done | bytes 1048608 | tf_op jit(solution)/shard_map/ppermute | solution.py:561
  400.7 3.5 convolution_convert_fusion.3
  408.4 4.5 fusion.1
  412.9 4.5 pad_maximum_fusion.4
  421.5 6.5 fusion.26
  427.9 55.6 %shard_map.357 = (bf16[2,1024,1792]{2,1,0:T(8,128)(2,1)}, f32[2,8,1024]{2,1,0:T(8,128)}, f32[2,2,8,512]{3,2,1,0:T(8,128)S(1)}) custom-call(f32[2,1024,1792]{2,1,0:T(8,128)} %fusion.8.pre, f32[2,8,1792]{2,1,0:T(8,128)S(1)} %broadcast_in_dim.116.rim, f32[4,1024]{1,0:T(4,128)S(1)} %bitcast.191, f32[2,8,128]{2,1,0:T(8,128)S(1)} %broadcast_in_dim.117.par, ...), custom_call_target="tpu_custom_call" | custom-call | flops 8053063680 | bytes 80530640 | tf_op jit(solution)/shard_map/pallas_call | solution.py:455
  483.7 5.4 convolution_convert_fusion.4
  489.1 3.1 convert_add_fusion.6
  492.1 20.5 %reduce-scatter.3.cloned.1.call-done = bf16[256,1152]{1,0:T(8,128)(2,1)} async-done(((bf16[2048,1152]{1,0:T(8,128)(2,1)}), bf16[256,1152]{1,0:T(8,128)(2,1)}) %reduce-scatter.3.cloned.1.call-update) | async-done | bytes 589840 | tf_op jit(solution)/shard_map/reduce_scatter | solution.py:738
  512.6 3.2 collective-permute-start.28
  515.9 11.6 %bitcast_convert_fusion = bf16[1024,1792]{1,0:T(8,128)(2,1)S(1)} fusion(bf16[2,1024,1792]{2,1,0:T(8,128)(2,1)} %get-tuple-element.69, bf16[1,1024,1024]{2,1,0:T(8,128)(2,1)} %collective-permute-done.4, bf16[1,1024,1024]{2,1,0:T(8,128)(2,1)S(1)} %copy-done.23), kind=kOutput, calls=%fused_computation | convolution fusion | flops 7520124928 | bytes 15204352 | tf_op jit(solution)/shard_map/dot_general | solution.py:590
  533.6 11.2 %convolution_convert_fusion = bf16[2048,1024]{1,0:T(8,128)(2,1)S(1)} fusion(bf16[2048,1792]{1,0:T(8,128)(2,1)} %bitcast.230, bf16[1024,896]{1,0:T(8,128)(2,1)} %copy-done.25, bf16[1024,896]{1,0:T(8,128)(2,1)} %copy-done.24), kind=kOutput, calls=%fused_computation.27 | convolution fusion | flops 7525629952 | bytes 15204352 | tf_op jit(solution)/shard_map/dot_general | solution.py:594
  549.4 3.3 collective-permute-done.42
  554.3 3.1 collective-permute-done.43
  557.4 4.3 collective-permute-done.44
  562.0 4.2 collective-permute-done.45
  568.5 3.1 collective-permute-done.46
  574.6 3.2 fusion
  586.7 13.8 %collective-permute-done.31 = bf16[1,512,1024]{2,1,0:T(8,128)(2,1)} collective-permute-done((bf16[1,512,1024]{2,1,0:T(8,128)(2,1)}, bf16[1,512,1024]{2,1,0:T(8,128)(2,1)}, u32[]{:S(2)}, u32[]{:S(2)}) %collective-permute-start.31) | collective-permute-done | bytes 1048608 | tf_op jit(solution)/shard_map/ppermute | solution.py:561
  614.0 3.8 fusion.16
  632.4 7.2 %collective-permute-done.38 = f32[8,128]{1,0:T(8,128)S(1)} collective-permute-done((f32[8,128]{1,0:T(8,128)S(1)}, f32[8,128]{1,0:T(8,128)S(1)}, u32[]{:S(2)}, u32[]{:S(2)}) %collective-permute-start.38) | collective-permute-done | bytes 4128 | tf_op jit(solution)/shard_map/ppermute | solution.py:561
  640.2 27.5 %reduce-scatter.5.cloned.1.call-done = bf16[256,1152]{1,0:T(8,128)(2,1)} async-done(((bf16[2048,1152]{1,0:T(8,128)(2,1)}), bf16[256,1152]{1,0:T(8,128)(2,1)}) %reduce-scatter.5.cloned.1.call-update) | async-done | bytes 589840 | tf_op jit(solution)/shard_map/reduce_scatter | solution.py:738
  667.7 3.4 collective-permute-start.40
  677.5 13.2 %collective-permute-done.40 = bf16[256,1152]{1,0:T(8,128)(2,1)S(1)} collective-permute-done((bf16[256,1152]{1,0:T(8,128)(2,1)}, bf16[256,1152]{1,0:T(8,128)(2,1)S(1)}, u32[]{:S(2)}, u32[]{:S(2)}) %collective-permute-start.40) | collective-permute-done | bytes 589856 | tf_op jit(solution)/shard_map/ppermute | solution.py:677
  691.0 4.1 collective-permute-done.25
  (469 shorter events, 138.6 us)
Async XLA Ops:
  7.2 117.6 %all-gather.3.cloned.1.call-start = ((), (), s32[]{:S(2)}) async-start(), calls=%async_computation.2 | async-start | bytes 4128768 | tf_op jit(solution)/shard_map/all_gather | solution.py:691
  11.4 5.5 collective-permute-start.5
  12.5 32.0 %collective-permute-start = (bf16[1,128,1024]{2,1,0:T(8,128)(2,1)}, bf16[1,128,1024]{2,1,0:T(8,128)(2,1)S(1)}, u32[]{:S(2)}, u32[]{:S(2)}) collective-permute-start(bf16[1,128,1024]{2,1,0:T(8,128)(2,1)} %get-tuple-element.224), channel_id=1, source_target_pairs={{0,1},{1,0},{2,3},{3,2},{4,5},{5,4},{6,7},{7,6},{8,9},{9,8},{10,11... | collective-permute-start | bytes 786440 | tf_op jit(solution)/shard_map/ppermute | solution.py:561
  12.5 32.1 %collective-permute-start.1 = (bf16[1,128,1024]{2,1,0:T(8,128)(2,1)}, bf16[1,128,1024]{2,1,0:T(8,128)(2,1)S(1)}, u32[]{:S(2)}, u32[]{:S(2)}) collective-permute-start(bf16[1,128,1024]{2,1,0:T(8,128)(2,1)} %get-tuple-element.226), channel_id=1, source_target_pairs={{0,2},{1,3},{2,0},{3,1},{4,6},{5,7},{6,4},{7,5},{8,10},{9,11},{10,... | collective-permute-start | bytes 786440 | tf_op jit(solution)/shard_map/ppermute | solution.py:561
  15.6 29.1 %collective-permute-start.2 = (bf16[1,128,1024]{2,1,0:T(8,128)(2,1)S(1)}, bf16[1,128,1024]{2,1,0:T(8,128)(2,1)S(1)}, u32[]{:S(2)}, u32[]{:S(2)}) collective-permute-start(bf16[1,128,1024]{2,1,0:T(8,128)(2,1)S(1)} %get-tuple-element.223), channel_id=1, source_target_pairs={{0,3},{1,2},{2,1},{3,0},{4,7},{5,6},{6,5},{7,4},{8,11},{9,10},{10,... | collective-permute-start | bytes 786440 | tf_op jit(solution)/shard_map/ppermute | solution.py:561
  16.7 78.0 %collective-permute-start.7 = (f32[1,7]{1,0:T(1,128)S(1)}, f32[1,7]{1,0:T(1,128)S(1)}, u32[]{:S(2)}, u32[]{:S(2)}) collective-permute-start(f32[1,7]{1,0:T(1,128)S(1)} %fusion.44), channel_id=1, source_target_pairs={{0,8},{8,0},{1,9},{9,1},{2,10},{10,2},{3,11},{11,3},{4,12},{12,4},... | collective-permute-start | bytes 92 | tf_op jit(solution)/shard_map/ppermute | solution.py:561
  18.1 25.5 %collective-permute-start.6 = (bf16[256,896]{1,0:T(8,128)(2,1)S(1)}, bf16[256,896]{1,0:T(8,128)(2,1)S(1)}, u32[]{:S(2)}, u32[]{:S(2)}) collective-permute-start(bf16[256,896]{1,0:T(8,128)(2,1)S(1)} %bitcast.204), channel_id=1, source_target_pairs={{1,4},{3,6},{4,1},{6,3},{9,12},{11,14},{12,9},{14,11},{17,20},{19,... | collective-permute-start | bytes 1376264 | tf_op jit(solution)/shard_map/ppermute | solution.py:677
  44.4 191.7 %all-gather.5.cloned.1.call-start = ((), (), s32[]{:S(2)}) async-start(), calls=%async_computation.3 | async-start | bytes 6488064 | tf_op jit(solution)/shard_map/all_gather | solution.py:691
  50.0 41.2 %collective-permute-start.3 = (bf16[1,512,1024]{2,1,0:T(8,128)(2,1)}, bf16[1,512,1024]{2,1,0:T(8,128)(2,1)S(1)}, u32[]{:S(2)}, u32[]{:S(2)}) collective-permute-start(bf16[1,512,1024]{2,1,0:T(8,128)(2,1)} %get-tuple-element.193), channel_id=1, source_target_pairs={{0,4},{4,0},{1,5},{5,1},{2,6},{6,2},{3,7},{7,3},{8,12},{12,8},{9,1... | collective-permute-start | bytes 3145736 | tf_op jit(solution)/shard_map/ppermute | solution.py:561
  51.3 40.9 %collective-permute-start.12 = (bf16[256,1408]{1,0:T(8,128)(2,1)S(1)}, bf16[256,1408]{1,0:T(8,128)(2,1)}, u32[]{:S(2)}, u32[]{:S(2)}) collective-permute-start(bf16[256,1408]{1,0:T(8,128)(2,1)S(1)} %bitcast.203), channel_id=1, source_target_pairs={{1,4},{3,6},{4,1},{6,3},{9,12},{11,14},{12,9},{14,11},{17,20},{19,... | collective-permute-start | bytes 2162696 | tf_op jit(solution)/shard_map/ppermute | solution.py:677
  92.3 35.0 %collective-permute-start.4 = (bf16[1,1024,1024]{2,1,0:T(8,128)(2,1)}, bf16[1,1024,1024]{2,1,0:T(8,128)(2,1)}, u32[]{:S(2)}, u32[]{:S(2)}) collective-permute-start(bf16[1,1024,1024]{2,1,0:T(8,128)(2,1)} %constant_dynamic-update-slice_fusion.39), channel_id=1, source_target_pairs={{0,8},{8,0},{1,9},{9,1},{2,10},{10,2},{3,11},{11,3},{4,12},{12,4},... | collective-permute-start | bytes 6291464 | tf_op jit(solution)/shard_map/ppermute | solution.py:561
  94.3 418.3 %reduce-scatter.3.cloned.1.call-start = ((), (), s32[]{:S(2)}) async-start(), calls=%async_computation.4 | async-start | bytes 5308416 | tf_op jit(solution)/shard_map/reduce_scatter | solution.py:738
  141.2 51.6 %collective-permute-start.8 = (bf16[1,128,1024]{2,1,0:T(8,128)(2,1)S(1)}, bf16[1,128,1024]{2,1,0:T(8,128)(2,1)S(1)}, u32[]{:S(2)}, u32[]{:S(2)}) collective-permute-start(bf16[1,128,1024]{2,1,0:T(8,128)(2,1)S(1)} %get-tuple-element.221), channel_id=1, source_target_pairs={{0,1},{1,0},{2,3},{3,2},{4,5},{5,4},{6,7},{7,6},{8,9},{9,8},{10,11... | collective-permute-start | bytes 786440 | tf_op jit(solution)/shard_map/ppermute | solution.py:561
  142.1 50.7 %collective-permute-start.9 = (bf16[1,128,1024]{2,1,0:T(8,128)(2,1)S(1)}, bf16[1,128,1024]{2,1,0:T(8,128)(2,1)S(1)}, u32[]{:S(2)}, u32[]{:S(2)}) collective-permute-start(bf16[1,128,1024]{2,1,0:T(8,128)(2,1)S(1)} %get-tuple-element.220), channel_id=1, source_target_pairs={{0,2},{1,3},{2,0},{3,1},{4,6},{5,7},{6,4},{7,5},{8,10},{9,11},{10,... | collective-permute-start | bytes 786440 | tf_op jit(solution)/shard_map/ppermute | solution.py:561
  143.9 49.0 %collective-permute-start.10 = (bf16[1,128,1024]{2,1,0:T(8,128)(2,1)S(1)}, bf16[1,128,1024]{2,1,0:T(8,128)(2,1)S(1)}, u32[]{:S(2)}, u32[]{:S(2)}) collective-permute-start(bf16[1,128,1024]{2,1,0:T(8,128)(2,1)S(1)} %get-tuple-element.219), channel_id=1, source_target_pairs={{0,3},{1,2},{2,1},{3,0},{4,7},{5,6},{6,5},{7,4},{8,11},{9,10},{10,... | collective-permute-start | bytes 786440 | tf_op jit(solution)/shard_map/ppermute | solution.py:561
  193.3 22.9 %collective-permute-start.13 = (bf16[1,512,1024]{2,1,0:T(8,128)(2,1)S(1)}, bf16[1,512,1024]{2,1,0:T(8,128)(2,1)S(1)}, u32[]{:S(2)}, u32[]{:S(2)}) collective-permute-start(bf16[1,512,1024]{2,1,0:T(8,128)(2,1)S(1)} %slice_dynamic-update-slice_fusion.24), channel_id=1, source_target_pairs={{0,4},{4,0},{1,5},{5,1},{2,6},{6,2},{3,7},{7,3},{8,12},{12,8},{9,1... | collective-permute-start | bytes 3145736 | tf_op jit(solution)/shard_map/ppermute | solution.py:561
  216.3 4.2 collective-permute-start.14
  245.3 4.5 collective-permute-start.15
  253.0 25.3 %collective-permute-start.16 = (bf16[1,512,1024]{2,1,0:T(8,128)(2,1)S(1)}, bf16[1,512,1024]{2,1,0:T(8,128)(2,1)S(1)}, u32[]{:S(2)}, u32[]{:S(2)}) collective-permute-start(bf16[1,512,1024]{2,1,0:T(8,128)(2,1)S(1)} %constant_dynamic-slice_fusion.9), channel_id=1, source_target_pairs={{0,4},{4,0},{1,5},{5,1},{2,6},{6,2},{3,7},{7,3},{8,12},{12,8},{9,1... | collective-permute-start | bytes 3145736 | tf_op jit(solution)/shard_map/ppermute | solution.py:561
  279.4 24.4 %collective-permute-start.17 = (bf16[1,512,1024]{2,1,0:T(8,128)(2,1)S(1)}, bf16[1,512,1024]{2,1,0:T(8,128)(2,1)S(1)}, u32[]{:S(2)}, u32[]{:S(2)}) collective-permute-start(bf16[1,512,1024]{2,1,0:T(8,128)(2,1)S(1)} %get-tuple-element.189), channel_id=1, source_target_pairs={{0,4},{4,0},{1,5},{5,1},{2,6},{6,2},{3,7},{7,3},{8,12},{12,8},{9,1... | collective-permute-start | bytes 3145736 | tf_op jit(solution)/shard_map/ppermute | solution.py:561
  304.0 4.2 collective-permute-start.18
  340.6 4.2 collective-permute-start.19
  345.9 25.3 %collective-permute-start.20 = (bf16[1,512,1024]{2,1,0:T(8,128)(2,1)S(1)}, bf16[1,512,1024]{2,1,0:T(8,128)(2,1)S(1)}, u32[]{:S(2)}, u32[]{:S(2)}) collective-permute-start(bf16[1,512,1024]{2,1,0:T(8,128)(2,1)S(1)} %constant_dynamic-slice_fusion.8), channel_id=1, source_target_pairs={{0,4},{4,0},{1,5},{5,1},{2,6},{6,2},{3,7},{7,3},{8,12},{12,8},{9,1... | collective-permute-start | bytes 3145736 | tf_op jit(solution)/shard_map/ppermute | solution.py:561
  354.9 53.5 %collective-permute-start.23 = (bf16[1,1024,1024]{2,1,0:T(8,128)(2,1)}, bf16[1,1024,1024]{2,1,0:T(8,128)(2,1)}, u32[]{:S(2)}, u32[]{:S(2)}) collective-permute-start(bf16[1,1024,1024]{2,1,0:T(8,128)(2,1)} %slice_bitcast_fusion.2), channel_id=1, source_target_pairs={{0,8},{8,0},{1,9},{9,1},{2,10},{10,2},{3,11},{11,3},{4,12},{12,4},... | collective-permute-start | bytes 6291464 | tf_op jit(solution)/shard_map/ppermute | solution.py:561
  375.3 24.4 %collective-permute-start.21 = (bf16[1,512,1024]{2,1,0:T(8,128)(2,1)S(1)}, bf16[1,512,1024]{2,1,0:T(8,128)(2,1)S(1)}, u32[]{:S(2)}, u32[]{:S(2)}) collective-permute-start(bf16[1,512,1024]{2,1,0:T(8,128)(2,1)S(1)} %get-tuple-element.187), channel_id=1, source_target_pairs={{0,4},{4,0},{1,5},{5,1},{2,6},{6,2},{3,7},{7,3},{8,12},{12,8},{9,1... | collective-permute-start | bytes 3145736 | tf_op jit(solution)/shard_map/ppermute | solution.py:561
  400.7 12.2 %collective-permute-start.22 = (bf16[1,1024,1024]{2,1,0:T(8,128)(2,1)}, bf16[1,1024,1024]{2,1,0:T(8,128)(2,1)}, u32[]{:S(2)}, u32[]{:S(2)}) collective-permute-start(bf16[1,1024,1024]{2,1,0:T(8,128)(2,1)} %constant_dynamic-update-slice_fusion.30), channel_id=1, source_target_pairs={{0,8},{8,0},{1,9},{9,1},{2,10},{10,2},{3,11},{11,3},{4,12},{12,4},... | collective-permute-start | bytes 6291464 | tf_op jit(solution)/shard_map/ppermute | solution.py:561
  417.5 250.2 %reduce-scatter.5.cloned.1.call-start = ((), (), s32[]{:S(2)}) async-start(), calls=%async_computation.5 | async-start | bytes 5308416 | tf_op jit(solution)/shard_map/reduce_scatter | solution.py:738
  420.0 69.1 %collective-permute-start.24 = (bf16[1,512,1024]{2,1,0:T(8,128)(2,1)}, bf16[1,512,1024]{2,1,0:T(8,128)(2,1)}, u32[]{:S(2)}, u32[]{:S(2)}) collective-permute-start(bf16[1,512,1024]{2,1,0:T(8,128)(2,1)} %constant_dynamic-slice_fusion.7), channel_id=1, source_target_pairs={{0,4},{4,0},{1,5},{5,1},{2,6},{6,2},{3,7},{7,3},{8,12},{12,8},{9,1... | collective-permute-start | bytes 3145736 | tf_op jit(solution)/shard_map/ppermute | solution.py:561
  512.6 18.4 %collective-permute-start.28 = (bf16[256,1152]{1,0:T(8,128)(2,1)}, bf16[256,1152]{1,0:T(8,128)(2,1)S(1)}, u32[]{:S(2)}, u32[]{:S(2)}) collective-permute-start(bf16[256,1152]{1,0:T(8,128)(2,1)} %reduce-scatter.3.cloned.1.call-done), channel_id=1, source_target_pairs={{1,4},{3,6},{4,1},{6,3},{9,12},{11,14},{12,9},{14,11},{17,20},{19,... | collective-permute-start | bytes 1769480 | tf_op jit(solution)/shard_map/ppermute | solution.py:677
  548.3 26.3 %collective-permute-start.30 = (bf16[1,1024,1024]{2,1,0:T(8,128)(2,1)}, bf16[1,1024,1024]{2,1,0:T(8,128)(2,1)}, u32[]{:S(2)}, u32[]{:S(2)}) collective-permute-start(bf16[1,1024,1024]{2,1,0:T(8,128)(2,1)} %slice_bitcast_fusion), channel_id=1, source_target_pairs={{0,8},{8,0},{1,9},{9,1},{2,10},{10,2},{3,11},{11,3},{4,12},{12,4},... | collective-permute-start | bytes 6291464 | tf_op jit(solution)/shard_map/ppermute | solution.py:561
  552.7 4.6 collective-permute-start.43
  557.4 4.4 collective-permute-start.44
  561.8 4.4 collective-permute-start.45
  566.2 5.3 collective-permute-start.46
  579.0 21.5 %collective-permute-start.31 = (bf16[1,512,1024]{2,1,0:T(8,128)(2,1)}, bf16[1,512,1024]{2,1,0:T(8,128)(2,1)}, u32[]{:S(2)}, u32[]{:S(2)}) collective-permute-start(bf16[1,512,1024]{2,1,0:T(8,128)(2,1)} %constant_dynamic-slice_fusion.3), channel_id=1, source_target_pairs={{0,4},{4,0},{1,5},{5,1},{2,6},{6,2},{3,7},{7,3},{8,12},{12,8},{9,1... | collective-permute-start | bytes 3145736 | tf_op jit(solution)/shard_map/ppermute | solution.py:561
  613.3 9.8 %collective-permute-start.35 = (f32[8,128]{1,0:T(8,128)}, f32[8,128]{1,0:T(8,128)S(1)}, u32[]{:S(2)}, u32[]{:S(2)}) collective-permute-start(f32[8,128]{1,0:T(8,128)} %bitcast.211), channel_id=1, source_target_pairs={{0,8},{8,0},{1,9},{9,1},{2,10},{10,2},{3,11},{11,3},{4,12},{12,4},... | collective-permute-start | bytes 12296 | tf_op jit(solution)/shard_map/ppermute | solution.py:561
  619.3 52.7 %collective-permute-start.32 = (bf16[1,128,1024]{2,1,0:T(8,128)(2,1)}, bf16[1,128,1024]{2,1,0:T(8,128)(2,1)}, u32[]{:S(2)}, u32[]{:S(2)}) collective-permute-start(bf16[1,128,1024]{2,1,0:T(8,128)(2,1)} %get-tuple-element.213), channel_id=1, source_target_pairs={{0,1},{1,0},{2,3},{3,2},{4,5},{5,4},{6,7},{7,6},{8,9},{9,8},{10,11... | collective-permute-start | bytes 786440 | tf_op jit(solution)/shard_map/ppermute | solution.py:561
  620.4 54.7 %collective-permute-start.33 = (bf16[1,128,1024]{2,1,0:T(8,128)(2,1)}, bf16[1,128,1024]{2,1,0:T(8,128)(2,1)}, u32[]{:S(2)}, u32[]{:S(2)}) collective-permute-start(bf16[1,128,1024]{2,1,0:T(8,128)(2,1)} %get-tuple-element.212), channel_id=1, source_target_pairs={{0,2},{1,3},{2,0},{3,1},{4,6},{5,7},{6,4},{7,5},{8,10},{9,11},{10,... | collective-permute-start | bytes 786440 | tf_op jit(solution)/shard_map/ppermute | solution.py:561
  622.1 55.4 %collective-permute-start.34 = (bf16[1,128,1024]{2,1,0:T(8,128)(2,1)}, bf16[1,128,1024]{2,1,0:T(8,128)(2,1)S(1)}, u32[]{:S(2)}, u32[]{:S(2)}) collective-permute-start(bf16[1,128,1024]{2,1,0:T(8,128)(2,1)} %get-tuple-element.211), channel_id=1, source_target_pairs={{0,3},{1,2},{2,1},{3,0},{4,7},{5,6},{6,5},{7,4},{8,11},{9,10},{10,... | collective-permute-start | bytes 786440 | tf_op jit(solution)/shard_map/ppermute | solution.py:561
  623.1 3.7 collective-permute-start.36
  626.8 3.6 collective-permute-start.37
  630.4 9.3 %collective-permute-start.38 = (f32[8,128]{1,0:T(8,128)S(1)}, f32[8,128]{1,0:T(8,128)S(1)}, u32[]{:S(2)}, u32[]{:S(2)}) collective-permute-start(f32[8,128]{1,0:T(8,128)S(1)} %add.253), channel_id=1, source_target_pairs={{0,1},{1,0},{2,3},{3,2},{4,5},{5,4},{6,7},{7,6},{8,9},{9,8},{10,11... | collective-permute-start | bytes 12296 | tf_op jit(solution)/shard_map/ppermute | solution.py:561
  639.7 31.7 %collective-permute-start.39 = (f32[8,128]{1,0:T(8,128)S(1)}, f32[8,128]{1,0:T(8,128)S(1)}, u32[]{:S(2)}, u32[]{:S(2)}) collective-permute-start(f32[8,128]{1,0:T(8,128)S(1)} %add.254), channel_id=1, source_target_pairs={{0,2},{1,3},{2,0},{3,1},{4,6},{5,7},{6,4},{7,5},{8,10},{9,11},{10,... | collective-permute-start | bytes 12296 | tf_op jit(solution)/shard_map/ppermute | solution.py:561
  667.7 23.0 %collective-permute-start.40 = (bf16[256,1152]{1,0:T(8,128)(2,1)}, bf16[256,1152]{1,0:T(8,128)(2,1)S(1)}, u32[]{:S(2)}, u32[]{:S(2)}) collective-permute-start(bf16[256,1152]{1,0:T(8,128)(2,1)} %reduce-scatter.5.cloned.1.call-done), channel_id=1, source_target_pairs={{1,4},{3,6},{4,1},{6,3},{9,12},{11,14},{12,9},{14,11},{17,20},{19,... | collective-permute-start | bytes 1769480 | tf_op jit(solution)/shard_map/ppermute | solution.py:677
  671.3 23.8 %collective-permute-start.25 = (bf16[1,128,1024]{2,1,0:T(8,128)(2,1)S(1)}, bf16[1,128,1024]{2,1,0:T(8,128)(2,1)S(1)}, u32[]{:S(2)}, u32[]{:S(2)}) collective-permute-start(bf16[1,128,1024]{2,1,0:T(8,128)(2,1)S(1)} %get-tuple-element.217), channel_id=1, source_target_pairs={{0,1},{1,0},{2,3},{3,2},{4,5},{5,4},{6,7},{7,6},{8,9},{9,8},{10,11... | collective-permute-start | bytes 786440 | tf_op jit(solution)/shard_map/ppermute | solution.py:561
  672.0 26.9 %collective-permute-start.26 = (bf16[1,128,1024]{2,1,0:T(8,128)(2,1)S(1)}, bf16[1,128,1024]{2,1,0:T(8,128)(2,1)S(1)}, u32[]{:S(2)}, u32[]{:S(2)}) collective-permute-start(bf16[1,128,1024]{2,1,0:T(8,128)(2,1)S(1)} %get-tuple-element.216), channel_id=1, source_target_pairs={{0,2},{1,3},{2,0},{3,1},{4,6},{5,7},{6,4},{7,5},{8,10},{9,11},{10,... | collective-permute-start | bytes 786440 | tf_op jit(solution)/shard_map/ppermute | solution.py:561
  675.2 23.8 %collective-permute-start.27 = (bf16[1,128,1024]{2,1,0:T(8,128)(2,1)S(1)}, bf16[1,128,1024]{2,1,0:T(8,128)(2,1)S(1)}, u32[]{:S(2)}, u32[]{:S(2)}) collective-permute-start(bf16[1,128,1024]{2,1,0:T(8,128)(2,1)S(1)} %get-tuple-element.215), channel_id=1, source_target_pairs={{0,3},{1,2},{2,1},{3,0},{4,7},{5,6},{6,5},{7,4},{8,11},{9,10},{10,... | collective-permute-start | bytes 786440 | tf_op jit(solution)/shard_map/ppermute | solution.py:561
  690.9 8.1 %collective-permute-start.41 = (bf16[128,1152]{1,0:T(8,128)(2,1)S(1)}, bf16[128,1152]{1,0:T(8,128)(2,1)S(1)}, u32[]{:S(2)}, u32[]{:S(2)}) collective-permute-start(bf16[128,1152]{1,0:T(8,128)(2,1)S(1)} %broadcast_select_fusion.6), channel_id=1, source_target_pairs={{0,8},{8,0},{1,9},{9,1},{2,10},{10,2},{3,11},{11,3},{4,12},{12,4},... | collective-permute-start | bytes 884744 | tf_op jit(solution)/shard_map/ppermute | solution.py:561
  (68 other events, 1055.3 us)
Sparse Core Ops, SparseCore 0:
  44.5 80.2 all-gather.2
  127.0 109.0 all-gather.4
  417.6 94.9 reduce-scatter.2
  572.3 95.3 reduce-scatter.4

commit v4 on v3

--- a/solution.py
+++ b/solution.py
@@ -49,20 +49,35 @@
     return row, col
 
 
+def dot_wide(left, right):
+    left_high, left_low = halves(left)
+    right_high, right_low = halves(right)
+    lefts = jnp.concatenate([left_high, left_low], axis=1)
+    rights = jnp.concatenate(
+        [
+            jnp.concatenate([right_high, right_low], axis=1),
+            jnp.concatenate([right_high, jnp.zeros_like(right_low)], axis=1),
+        ],
+        axis=0,
+    )
+    both = lax.dot_general(lefts, rights, NN, preferred_element_type=jnp.float32)
+    return both[:, :CHUNK] + both[:, CHUNK:]
+
+
 def unit_lower_inverses(lowers):
     row, col = positions()
     eye = (row == col).astype(jnp.float32)
     diag = [jnp.where(row // 8 == col // 8, low, 0.0) for low in lowers]
     result = [eye - d for d in diag]
-    power = [dot_split(d, d, NN) for d in diag]
-    result = [x + dot_split(x, p, NN) for x, p in zip(result, power)]
-    power = [dot_split(p, p, NN) for p in power]
-    result = [x + dot_split(x, p, NN) for x, p in zip(result, power)]
+    power = [dot_wide(d, d) for d in diag]
+    result = [x + dot_wide(x, p) for x, p in zip(result, power)]
+    power = [dot_wide(p, p) for p in power]
+    result = [x + dot_wide(x, p) for x, p in zip(result, power)]
     size = 8
     while size < CHUNK:
         across = (row // (2 * size) == col // (2 * size)) & (row // size != col // size)
-        mixed = [dot_split(jnp.where(across, low, 0.0), x, NN) for low, x in zip(lowers, result)]
-        result = [x - dot_split(x, m, NN) for x, m in zip(result, mixed)]
+        mixed = [dot_wide(jnp.where(across, low, 0.0), x) for low, x in zip(lowers, result)]
+        result = [x - dot_wide(x, m) for x, m in zip(result, mixed)]
         size *= 2
     return result
 
@@ -633,7 +648,7 @@
     return jnp.concatenate([own, swapped(own, "core", 1)], 0)
 
 
-def with_group(own):
+def with_sides(own):
     side = lax.axis_index("cl")
     tokens = own.shape[1]
     both = jnp.zeros((own.shape[0], 2 * tokens) + own.shape[2:], own.dtype)
@@ -641,7 +656,11 @@
     both = lax.dynamic_update_slice_in_dim(
         both, swapped(own, "cl", 1), (1 - side) * tokens, 1
     )
-    return with_partner(both)
+    return both
+
+
+def with_group(own):
+    return with_partner(with_sides(own))
 
 
 def sum_of_cores(partial_sums):
@@ -679,18 +698,19 @@
     return jnp.where(stays, value, received)
 
 
-def gather_weights(first, second):
+def rank_weights(first, second):
     core = lax.axis_index("core")
     mine = jnp.where(core == 0, first, second)
     received = swapped(jnp.where(core == 0, second, first), "core", 1)
-    rows, cols = mine.shape
     pair = jnp.stack(
         [jnp.where(core == 0, mine, received), jnp.where(core == 0, received, mine)]
     )
-    pair = traded(pair.reshape(2 * rows, cols))
+    return traded(pair.reshape(-1, mine.shape[1]))
+
+
+def gather_weights(pair):
     full = lax.all_gather(pair, SPREAD, axis=0, tiled=True)
-    lanes, px, groups = (lax.axis_size(axis) for axis in SPREAD)
-    return full.reshape(lanes // 2, 4 * px * groups * rows, cols)
+    return full.reshape(lax.axis_size("tensor") // 2, -1, pair.shape[1])
 
 
 def whole_rows(gathered, first, width):
@@ -734,8 +754,12 @@
 
 
 def scatter_grads(joined):
+    return lax.psum_scatter(joined, SPREAD, scatter_dimension=0, tiled=True)
+
+
+def own_rows_of(summed):
     core = lax.axis_index("core")
-    summed = traded(lax.psum_scatter(joined, SPREAD, scatter_dimension=0, tiled=True))
+    summed = traded(summed)
     rows = summed.shape[0] // 2
     top, bottom = summed[:rows], summed[rows:]
     mine = jnp.where(core == 0, top, bottom)
@@ -830,19 +854,23 @@
         mine = jnp.where(core == 0, mine[:, :, 0], mine[:, :, 1])
         return mine.reshape(array.shape[0], heads, width)
 
-    mix_parts = gather_weights(mix_half(0), mix_half(1))
+    mix_pair = rank_weights(mix_half(0), mix_half(1))
+    mix_pair, tokens = lax.optimization_barrier((mix_pair, tokens))
+    mix_parts = gather_weights(mix_pair)
     dealt = dealt_by_sequence(tokens)
-    dealt, w_ffn_gate, w_ffn_up, w_ffn_down, w_out = lax.optimization_barrier(
-        (dealt, w_ffn_gate, w_ffn_up, w_ffn_down, w_out)
-    )
     norm_gain, ffn_gain = to_gather_order(norm_gain), to_gather_order(ffn_gain)
     own = to_gather_order(dealt).astype(jnp.float32)
     normed_own = (rms_rows(own) * norm_gain).astype(low)
-    normed = with_group(normed_own).reshape(flat, model)
-    rest_parts = gather_weights(rest_half(0), rest_half(1))
+    normed_both = with_sides(normed_own)
+    mix_parts, normed_both, w_ffn_gate, w_ffn_up, w_ffn_down, w_out = lax.optimization_barrier(
+        (mix_parts, normed_both, w_ffn_gate, w_ffn_up, w_ffn_down, w_out)
+    )
+    rest_pair = rank_weights(rest_half(0), rest_half(1))
+    normed = with_partner(normed_both).reshape(flat, model)
     w_mix = whole_rows(mix_parts, 0, per_quarter * HEAD)
     pre = matmul(normed, w_mix).reshape(seqs, length, heads * HEAD)
-    pre, d_mixed = lax.optimization_barrier((pre, d_mixed))
+    pre, d_mixed, rest_pair = lax.optimization_barrier((pre, d_mixed, rest_pair))
+    rest_parts = gather_weights(rest_pair)
     rim = jnp.zeros((seqs, RIM, heads * HEAD), jnp.float32)
     if pieces > 1:
         rim = passed_along(pre[:, length - RIM :], "cg", 1)
@@ -919,8 +947,8 @@
     d_branch = with_group(d_middle.astype(low)).reshape(flat, model)
     ffn_part = matmul_right_t(hidden, w_down_t).astype(low)
     ffn_both = sum_of_cores(ffn_part.reshape(seqs, length, model))
-    d_branch, rest_joined, ffn_both = lax.optimization_barrier((d_branch, rest_joined, ffn_both))
-    rest_first, rest_second = scatter_grads(rest_joined)
+    rest_summed = scatter_grads(rest_joined)
+    d_branch, ffn_both, _ = lax.optimization_barrier((d_branch, ffn_both, rest_joined))
     d_gated = matmul(d_branch, w_out_t).reshape(seqs, length, heads * VAL)
     if pieces == 1:
         ends = (read,)
@@ -946,18 +974,25 @@
     d_all = d_all.reshape(flat, heads * HEAD)
     grad_mix = matmul_left_t(normed, d_all).astype(low)
     grad_out = matmul_left_t(d_branch, gated_flat).astype(low)
-    mix_joined = joined_grads(zip(columns_of(grad_mix, groups), columns_of(grad_out, groups)))
-    mix_joined, rest_first, rest_second, d_all = lax.optimization_barrier(
-        (mix_joined, rest_first, rest_second, d_all)
-    )
-    mix_first, mix_second = scatter_grads(mix_joined)
+    grad_heads = [
+        part.reshape(model, per_quarter, HEAD) for part in columns_of(grad_mix, groups)
+    ]
+    mix_joined = joined_grads(
+        [part[:, n, :AB_AT] for n in range(per_quarter)] + [out]
+        for part, out in zip(grad_heads, columns_of(grad_out, groups))
+    )
+    grad_ab = jnp.concatenate([part[..., AB_AT : AB_AT + 2] for part in grad_heads], 1)
+    mix_joined, rest_summed, d_all = lax.optimization_barrier((mix_joined, rest_summed, d_all))
+    rest_first, rest_second = own_rows_of(rest_summed)
+    mix_first, mix_second = own_rows_of(scatter_grads(mix_joined))
     d_normed = matmul_right_t(d_all, w_mix).astype(low)
-    own_d_normed = sum_in_group(d_normed.reshape(seqs, length, model))
+    d_normed = sum_of_cores(d_normed.reshape(seqs, length, model))
+    d_normed, mixed = lax.optimization_barrier((d_normed, mixed))
+    own_d_normed = sum_of_sides(d_normed)
     _, norm_back = jax.vjp(norm_scaled, own, norm_gain)
     d_own, grad_norm_gain = norm_back(own_d_normed)
     grad_tokens = dealt_by_tokens(to_model_order((d_middle + d_own).astype(low)))
     grad_tokens = grad_tokens.astype(jnp.float32)
-    grad_norm_gain, grad_ffn_gain = to_model_order(grad_norm_gain), to_model_order(grad_ffn_gain)
 
     small = jnp.sum(d_small, axis=0)
 
@@ -976,6 +1011,7 @@
         jnp.sum(small[:, 4, :VAL], axis=0),
         placed(small[None, :, 5, :1]),
         placed(small[None, :, 6, :1]),
+        placed(jnp.transpose(grad_ab, (2, 0, 1)).reshape(-1, heads, 1).astype(jnp.float32)),
     ]
     sizes = [item.shape[0] for item in items]
     total = up_to(sum(sizes), 1024)
@@ -984,10 +1020,17 @@
     norm_sum = summed_everywhere(grad_norm_gain.reshape(8, -1)).reshape(-1)
     ends = [sum(sizes[: n + 1]) for n in range(len(sizes))]
     sums = [joined[end - size : end] for size, end in zip(sizes, ends)]
+    blocks = 4 * lax.axis_size("px") * pieces
+    block = ((side * lax.axis_size("px") + lax.axis_index("px")) * pieces + place) * 2 + core
+    ab_sums = lax.dynamic_slice(
+        sums[7].reshape(2, model, lanes * quarter_heads),
+        (0, block * (model // blocks), lane * quarter_heads),
+        (2, model // blocks, quarter_heads),
+    )
 
     def mix_cols(first, width):
         halves_of = [
-            half[:, : per_quarter * HEAD].reshape(half.shape[0], per_quarter, HEAD)[:, :, first : first + width].reshape(
+            half[:, : per_quarter * AB_AT].reshape(half.shape[0], per_quarter, AB_AT)[:, :, first : first + width].reshape(
                 half.shape[0], -1
             )
             for half in (mix_first, mix_second)
@@ -1000,21 +1043,21 @@
     return (
         mixed,
         grad_tokens,
-        norm_sum,
+        to_model_order(norm_sum),
         mix_cols(0, KEY),
         mix_cols(KEY, KEY),
         mix_cols(2 * KEY, VAL),
         mix_cols(GATE_AT, VAL),
-        mix_cols(AB_AT, 1),
-        mix_cols(AB_AT + 1, 1),
+        ab_sums[0],
+        ab_sums[1],
         sums[1].reshape(4, -1),
         sums[2].reshape(4, -1),
         sums[3].reshape(4, -1),
         sums[5],
         sums[6],
         sums[4],
-        rest_cols(per_quarter * HEAD, val_cols, (mix_first, mix_second)).T,
-        sums[0],
+        rest_cols(per_quarter * AB_AT, val_cols, (mix_first, mix_second)).T,
+        to_model_order(sums[0]),
         rest_cols(0, half_units),
         rest_cols(wide, half_units),
         rest_cols(2 * wide, half_units).T,

time: 724 us -> 795 us (1.098)
  waiting for transfers between devices: 322 us -> 358 us
  local copies, waits for them, and re-layouts: 71.8 us -> 97.8 us
  other arithmetic: 49.2 us -> 60.5 us
    reduce_scatter x2, waiting for transfers between devices: 48 us -> 0.21 us  [scatter_grads(): return lax.psum_scatter(joined, SPREAD, scatter_dimension=0, tiled=True)]
    ppermute x4, waiting for transfers between devices: 34.3 us -> 81.4 us  [traded(): received = lax.ppermute(value, ('cl', 'tensor'), pairs)]
    ppermute x43, waiting for transfers between devices: 196 us -> 234 us  [swapped(): lax.ppermute(value, axis, [(place, place ^ bits) for place in range(count)])]
    select_n x3 -> x4, other arithmetic: 0.23 us -> 8.84 us  [placed(): return jnp.where(spots == 2 * side + core, shaped, 0.0).reshape(-1)]
    unnamed x186 -> x210, local copies, waits for them, and re-layouts: 21.5 us -> 22.1 us
  transfers between devices with their start and end apart: 51 -> 51, of which waited for: 27 -> 31; matrix products, arithmetic and copies ran while one was open for 20% -> 20% of each run, Pallas kernels for 15% -> 13%
where the time goes in v4:
time: 795 us; the launch traced here: 786 us
  waiting for transfers between devices  358 us (45%)
  Pallas kernels  102 us (13%)
  local copies, waits for them, and re-layouts  97.8 us (12%)
  matrix products  96.8 us (12%)
  other arithmetic  60.5 us (8%)
  starting transfers between devices  54.6 us (7%)
  between operations  16.4 us (2%)
    ppermute x43, waiting for transfers between devices, swapped(): lax.ppermute(value, axis, [(place, place ^ bits) for place in range(count)])  234 us
    pallas_call x2, Pallas kernels, call(): pl.pallas_call(kernel, grid=lead, in_specs=in_specs, out_specs=[spec for...  102 us
    ppermute x4, waiting for transfers between devices, traded(): received = lax.ppermute(value, ('cl', 'tensor'), pairs)  81.4 us
    all_gather x2, waiting for transfers between devices, gather_weights(): full = lax.all_gather(pair, SPREAD, axis=0, tiled=True)  42.4 us
    ppermute x43, starting transfers between devices, swapped(): lax.ppermute(value, axis, [(place, place ^ bits) for place in range(count)])  40.8 us
    dot_general x4, matrix products, matmul(): return lax.dot_general(left, right, NN, preferred_element_type=jnp.float32)  38.1 us
    dot_general x4, matrix products, matmul_right_t(): return lax.dot_general(left, right, NT, preferred_element_type=jnp.float32)  29.5 us
    dot_general x4, matrix products, matmul_left_t(): return lax.dot_general(left, right, TN, preferred_element_type=jnp.float32)  29.2 us
  transfers between devices with their start and end apart: 51, of which 31 were waited for; matrix products, arithmetic and copies ran while one was open for 20% of the time, Pallas kernels for 13%

profile of v4, /device:TPU:8, one launch (start us, length us, event | category | flops | bytes accessed | tf_op | source)
XLA Modules:
  0.0 786.2 jit_solution(12340942514068507721)
XLA Ops:
  13.1 3.3 collective-permute-start.1
  16.4 12.0 %collective-permute-done.1 = bf16[256,896]{1,0:T(8,128)(2,1)S(1)} collective-permute-done((bf16[256,896]{1,0:T(8,128)(2,1)S(1)}, bf16[256,896]{1,0:T(8,128)(2,1)S(1)}, u32[]{:S(2)}, u32[]{:S(2)}) %collective-permute-start.1) | collective-permute-done | bytes 458784 | tf_op jit(solution)/shard_map/ppermute | solution.py:696
  34.0 9.6 %collective-permute-done.2 = bf16[1,128,1024]{2,1,0:T(8,128)(2,1)S(1)} collective-permute-done((bf16[1,128,1024]{2,1,0:T(8,128)(2,1)}, bf16[1,128,1024]{2,1,0:T(8,128)(2,1)S(1)}, u32[]{:S(2)}, u32[]{:S(2)}) %collective-permute-start.2) | collective-permute-done | bytes 262176 | tf_op jit(solution)/shard_map/ppermute | solution.py:576
  43.6 14.4 %collective-permute-done.3 = bf16[1,128,1024]{2,1,0:T(8,128)(2,1)S(1)} collective-permute-done((bf16[1,128,1024]{2,1,0:T(8,128)(2,1)S(1)}, bf16[1,128,1024]{2,1,0:T(8,128)(2,1)S(1)}, u32[]{:S(2)}, u32[]{:S(2)}) %collective-permute-start.3) | collective-permute-done | bytes 262176 | tf_op jit(solution)/shard_map/ppermute | solution.py:576
  58.1 12.7 %collective-permute-done.4 = bf16[1,128,1024]{2,1,0:T(8,128)(2,1)S(1)} collective-permute-done((bf16[1,128,1024]{2,1,0:T(8,128)(2,1)S(1)}, bf16[1,128,1024]{2,1,0:T(8,128)(2,1)S(1)}, u32[]{:S(2)}, u32[]{:S(2)}) %collective-permute-start.4) | collective-permute-done | bytes 262176 | tf_op jit(solution)/shard_map/ppermute | solution.py:576
  73.8 18.7 %collective-permute-done.5 = bf16[1,512,1024]{2,1,0:T(8,128)(2,1)} collective-permute-done((bf16[1,512,1024]{2,1,0:T(8,128)(2,1)}, bf16[1,512,1024]{2,1,0:T(8,128)(2,1)}, u32[]{:S(2)}, u32[]{:S(2)}) %collective-permute-start.5) | collective-permute-done | bytes 1048608 | tf_op jit(solution)/shard_map/ppermute | solution.py:576
  93.8 17.6 %all-gather.3.cloned.1.call-done = bf16[2048,896]{1,0:T(8,128)(2,1)} async-done(((bf16[256,896]{1,0:T(8,128)(2,1)}), bf16[2048,896]{1,0:T(8,128)(2,1)}) %all-gather.3.cloned.1.call-update) | async-done | bytes 3670032 | tf_op jit(solution)/shard_map/all_gather | solution.py:712
  130.9 3.9 collective-permute-start.8
  138.5 14.0 %collective-permute-done.8 = bf16[256,1408]{1,0:T(8,128)(2,1)S(1)} collective-permute-done((bf16[256,1408]{1,0:T(8,128)(2,1)S(1)}, bf16[256,1408]{1,0:T(8,128)(2,1)S(1)}, u32[]{:S(2)}, u32[]{:S(2)}) %collective-permute-start.8) | collective-permute-done | bytes 720928 | tf_op jit(solution)/shard_map/ppermute | solution.py:696
  156.8 12.5 %fusion.8.pre = f32[2,1024,1792]{2,1,0:T(8,128)} fusion(bf16[2,1024,1024]{2,1,0:T(8,128)(2,1)} %constant_dynamic-update-slice_fusion.1, bf16[1024,896]{1,0:T(8,128)(2,1)S(1)} %copy-done.33, bf16[1024,896]{1,0:T(8,128)(2,1)S(1)} %copy-done.32), kind=kOutput, calls=%fused_computation.31 | convolution fusion | flops 7523532800 | bytes 22544384 | tf_op jit(solution)/shard_map/dot_general | solution.py:601
  174.7 46.5 %shard_map.356 = (f32[2,2,1024,128]{3,2,1,0:T(8,128)S(1)}, f32[2,2,1024,128]{3,2,1,0:T(8,128)S(1)}, f32[2,2,1024,128]{3,2,1,0:T(8,128)}, f32[2,2,1024,256]{3,2,1...) custom-call(f32[2,1024,1792]{2,1,0:T(8,128)} %fusion.8.pre, ...), custom_call_target="tpu_custom_call" | custom-call | flops 9395240960 | bytes 93952408 | tf_op jit(solution)/shard_map/pallas_call | solution.py:470
  222.6 22.8 %collective-permute-done.13 = bf16[1,512,1024]{2,1,0:T(8,128)(2,1)S(1)} collective-permute-done((bf16[1,512,1024]{2,1,0:T(8,128)(2,1)S(1)}, bf16[1,512,1024]{2,1,0:T(8,128)(2,1)S(1)}, u32[]{:S(2)}, u32[]{:S(2)}) %collective-permute-start.13) | collective-permute-done | bytes 1048608 | tf_op jit(solution)/shard_map/ppermute | solution.py:576
  245.6 4.1 collective-permute-done.14
  252.1 24.8 %all-gather.5.cloned.1.call-done = bf16[2048,1408]{1,0:T(8,128)(2,1)} async-done(((bf16[256,1408]{1,0:T(8,128)(2,1)}), bf16[2048,1408]{1,0:T(8,128)(2,1)}) %all-gather.5.cloned.1.call-update) | async-done | bytes 5767184 | tf_op jit(solution)/shard_map/all_gather | solution.py:712
  278.2 4.3 convolution_convert_fusion.1
  286.0 4.5 collective-permute-done.15
  295.4 23.7 %collective-permute-done.16 = bf16[1,512,1024]{2,1,0:T(8,128)(2,1)S(1)} collective-permute-done((bf16[1,512,1024]{2,1,0:T(8,128)(2,1)S(1)}, bf16[1,512,1024]{2,1,0:T(8,128)(2,1)S(1)}, u32[]{:S(2)}, u32[]{:S(2)}) %collective-permute-start.16) | collective-permute-done | bytes 1048608 | tf_op jit(solution)/shard_map/ppermute | solution.py:576
  322.4 22.9 %collective-permute-done.17 = bf16[1,512,1024]{2,1,0:T(8,128)(2,1)S(1)} collective-permute-done((bf16[1,512,1024]{2,1,0:T(8,128)(2,1)S(1)}, bf16[1,512,1024]{2,1,0:T(8,128)(2,1)S(1)}, u32[]{:S(2)}, u32[]{:S(2)}) %collective-permute-start.17) | collective-permute-done | bytes 1048608 | tf_op jit(solution)/shard_map/ppermute | solution.py:576
  346.0 3.6 collective-permute-done.18
  350.0 10.0 %fusion.30 = f32[2048,1536]{0,1:T(8,128)} fusion(bf16[2048,1024]{1,0:T(8,128)(2,1)S(1)} %bitcast.210, bf16[1024,384]{1,0:T(8,128)(2,1)S(1)} %get-tuple-element.202, bf16[1024,384]{1,0:T(8,128)(2,1)S(1)} %get-tuple-element.203, bf16[1024,384]{1,0:T(8,128)(2,1)S(1)} %get-tuple-element.204, bf16[1024,384]{1,0:T(8,128)(2,1)S(1)} %get-tuple-element.201), kind=kOutput, calls=%fused_computation.94 | convolution fusion | flops 6455033856 | bytes 19922944 | tf_op jit(solution)/shard_map/dot_general | solution.py:601
  360.0 11.3 %multiply_convert_fusion.2 = (bf16[2048,768]{0,1:T(8,128)(2,1)S(1)}, bf16[2048,768]{0,1:T(8,128)(2,1)}, bf16[2048,768]{0,1:T(8,128)(2,1)}) fusion(f32[2048,1536]{0,1:T(8,128)} %fusion.30, bf16[2048,1024]{1,0:T(8,128)(2,1)S(1)} %bitcast.208, bf16[1024,384]{1,0:T(8,128)(2,1)S(1)} %get-tuple-element.205, bf16[1024,384]{1,0:T(8,128)(2,1)S(1)} %get-tuple-element.206), kind=kOutput, calls=%fused_computation.4 | convolution fusion | flops 3249537024 | bytes 27787264 | tf_op jit(solution)/shard_map/dot_general | solution.py:601
  371.3 9.9 %fusion.6 = bf16[2048,1024]{1,0:T(8,128)(2,1)S(1)} fusion(bf16[2048,768]{0,1:T(8,128)(2,1)} %get-tuple-element.199, bf16[2048,768]{0,1:T(8,128)(2,1)S(1)} %get-tuple-element.198, bf16[1024,384]{1,0:T(8,128)(2,1)S(1)} %get-tuple-element.202, bf16[1024,384]{1,0:T(8,128)(2,1)S(1)} %get-tuple-element.203, bf16[1024,384]{1,0:T(8,128)(2,1)S(1)} %copy-done.43, ...), kind=kOutput, calls=%fused_computation.25 | convolution fusion | flops 6469713920 | bytes 13631488 | tf_op jit(solution)/shard_map/dot_general | solution.py:609
  384.9 4.3 collective-permute-done.19
  394.0 7.7 fusion.7
  401.7 16.0 %collective-permute-done.20 = bf16[1,512,1024]{2,1,0:T(8,128)(2,1)S(1)} collective-permute-done((bf16[1,512,1024]{2,1,0:T(8,128)(2,1)S(1)}, bf16[1,512,1024]{2,1,0:T(8,128)(2,1)S(1)}, u32[]{:S(2)}, u32[]{:S(2)}) %collective-permute-start.20) | collective-permute-done | bytes 1048608 | tf_op jit(solution)/shard_map/ppermute | solution.py:576
  423.5 4.1 convolution_convert_fusion.2
  434.4 12.0 %collective-permute-done.21 = bf16[1,512,1024]{2,1,0:T(8,128)(2,1)S(1)} collective-permute-done((bf16[1,512,1024]{2,1,0:T(8,128)(2,1)S(1)}, bf16[1,512,1024]{2,1,0:T(8,128)(2,1)S(1)}, u32[]{:S(2)}, u32[]{:S(2)}) %collective-permute-start.21) | collective-permute-done | bytes 1048608 | tf_op jit(solution)/shard_map/ppermute | solution.py:576
  447.5 3.5 convolution_convert_fusion.3
  455.2 4.5 fusion.1
  462.5 4.4 fusion.27
  466.9 55.8 %shard_map.357 = (bf16[2,1024,1792]{2,1,0:T(8,128)(2,1)}, f32[2,8,1024]{2,1,0:T(8,128)}, f32[2,2,8,512]{3,2,1,0:T(8,128)S(1)}) custom-call(f32[2,1024,1792]{2,1,0:T(8,128)} %fusion.8.pre, f32[2,8,1792]{2,1,0:T(8,128)S(1)} %broadcast_in_dim.138.rim, f32[4,1024]{1,0:T(4,128)S(1)} %bitcast.203, f32[2,8,128]{2,1,0:T(8,128)S(1)} %broadcast_in_dim.139.par, ...), custom_call_target="tpu_custom_call" | custom-call | flops 8053063680 | bytes 80530640 | tf_op jit(solution)/shard_map/pallas_call | solution.py:470
  526.1 6.7 convolution_convert_fusion.4
  532.8 16.9 %collective-permute-done.24 = bf16[1,512,1024]{2,1,0:T(8,128)(2,1)S(1)} collective-permute-done((bf16[1,512,1024]{2,1,0:T(8,128)(2,1)S(1)}, bf16[1,512,1024]{2,1,0:T(8,128)(2,1)S(1)}, u32[]{:S(2)}, u32[]{:S(2)}) %collective-permute-start.24) | collective-permute-done | bytes 1048608 | tf_op jit(solution)/shard_map/ppermute | solution.py:576
  551.4 11.3 %bitcast_convert_fusion = bf16[1024,1792]{1,0:T(8,128)(2,1)S(1)} fusion(bf16[2,1024,1024]{2,1,0:T(8,128)(2,1)S(1)} %copy-done.34, bf16[2,1024,1792]{2,1,0:T(8,128)(2,1)} %get-tuple-element.76), kind=kOutput, calls=%fused_computation | convolution fusion | flops 7518027776 | bytes 15204352 | tf_op jit(solution)/shard_map/dot_general | solution.py:605
  565.0 8.6 %broadcast_select_fusion = f32[2048,2,2,2]{3,2,1,0:T(2,128)} fusion(pred[2,2]{1,0:T(4,128)(4,1)S(1)} %add_compare_fusion, f32[2048,2]{1,0:T(8,128)S(1)} %bitcast.214), kind=kLoop, calls=%fused_computation.22 | loop fusion | flops 16384 | bytes 81924 | tf_op jit(solution)/shard_map/jit(_where)/select_n | solution.py:1003
  573.6 7.4 select_n.449
  592.2 4.3 collective-permute-done.41
  606.5 8.8 %collective-permute-done.43 = f32[272,128]{1,0:T(8,128)S(1)} collective-permute-done((f32[272,128]{1,0:T(8,128)S(1)}, f32[272,128]{1,0:T(8,128)S(1)}, u32[]{:S(2)}, u32[]{:S(2)}) %collective-permute-start.43) | collective-permute-done | bytes 139296 | tf_op jit(solution)/shard_map/ppermute | solution.py:576
  620.2 7.6 collective-permute-done.28
  633.6 11.2 %convolution_convert_fusion = bf16[2048,1024]{1,0:T(8,128)(2,1)S(1)} fusion(bf16[2048,1792]{1,0:T(8,128)(2,1)} %bitcast.231, bf16[1024,896]{1,0:T(8,128)(2,1)} %get-tuple-element.212, bf16[1024,896]{1,0:T(8,128)(2,1)} %get-tuple-element.211), kind=kOutput, calls=%fused_computation.27 | convolution fusion | flops 7525629952 | bytes 15204352 | tf_op jit(solution)/shard_map/dot_general | solution.py:609
  649.3 3.6 collective-permute-start.45
  654.1 32.6 %collective-permute-done.45 = bf16[256,1152]{1,0:T(8,128)(2,1)S(1)} collective-permute-done((bf16[256,1152]{1,0:T(8,128)(2,1)S(1)}, bf16[256,1152]{1,0:T(8,128)(2,1)S(1)}, u32[]{:S(2)}, u32[]{:S(2)}) %collective-permute-start.45) | collective-permute-done | bytes 589856 | tf_op jit(solution)/shard_map/ppermute | solution.py:696
  703.2 13.9 %collective-permute-done.29 = bf16[1,512,1024]{2,1,0:T(8,128)(2,1)} collective-permute-done((bf16[1,512,1024]{2,1,0:T(8,128)(2,1)}, bf16[1,512,1024]{2,1,0:T(8,128)(2,1)}, u32[]{:S(2)}, u32[]{:S(2)}) %collective-permute-start.29) | collective-permute-done | bytes 1048608 | tf_op jit(solution)/shard_map/ppermute | solution.py:576
  723.5 3.5 collective-permute-done.34
  727.3 3.3 collective-permute-done.35
  735.4 7.8 collective-permute-start.37
  744.1 3.5 collective-permute-start.32
  750.5 22.8 %collective-permute-done.38 = bf16[256,1024]{1,0:T(8,128)(2,1)S(1)} collective-permute-done((bf16[256,1024]{1,0:T(8,128)(2,1)}, bf16[256,1024]{1,0:T(8,128)(2,1)S(1)}, u32[]{:S(2)}, u32[]{:S(2)}) %collective-permute-start.38) | collective-permute-done | bytes 524320 | tf_op jit(solution)/shard_map/ppermute | solution.py:696
  (503 shorter events, 176.5 us)
Async XLA Ops:
  7.2 104.2 %all-gather.3.cloned.1.call-start = ((), (), s32[]{:S(2)}) async-start(), calls=%async_computation.2 | async-start | bytes 4128768 | tf_op jit(solution)/shard_map/all_gather | solution.py:712
  13.1 15.4 %collective-permute-start.1 = (bf16[256,896]{1,0:T(8,128)(2,1)S(1)}, bf16[256,896]{1,0:T(8,128)(2,1)S(1)}, u32[]{:S(2)}, u32[]{:S(2)}) collective-permute-start(bf16[256,896]{1,0:T(8,128)(2,1)S(1)} %bitcast.218), channel_id=1, source_target_pairs={{1,4},{3,6},{4,1},{6,3},{9,12},{11,14},{12,9},{14,11},{17,20},{19,... | collective-permute-start | bytes 1376264 | tf_op jit(solution)/shard_map/ppermute | solution.py:696
  29.3 247.6 %all-gather.5.cloned.1.call-start = ((), (), s32[]{:S(2)}) async-start(), calls=%async_computation.3 | async-start | bytes 6488064 | tf_op jit(solution)/shard_map/all_gather | solution.py:712
  30.5 13.1 %collective-permute-start.2 = (bf16[1,128,1024]{2,1,0:T(8,128)(2,1)}, bf16[1,128,1024]{2,1,0:T(8,128)(2,1)S(1)}, u32[]{:S(2)}, u32[]{:S(2)}) collective-permute-start(bf16[1,128,1024]{2,1,0:T(8,128)(2,1)} %get-tuple-element.231), channel_id=1, source_target_pairs={{0,1},{1,0},{2,3},{3,2},{4,5},{5,4},{6,7},{7,6},{8,9},{9,8},{10,11... | collective-permute-start | bytes 786440 | tf_op jit(solution)/shard_map/ppermute | solution.py:576
  30.5 27.6 %collective-permute-start.3 = (bf16[1,128,1024]{2,1,0:T(8,128)(2,1)S(1)}, bf16[1,128,1024]{2,1,0:T(8,128)(2,1)S(1)}, u32[]{:S(2)}, u32[]{:S(2)}) collective-permute-start(bf16[1,128,1024]{2,1,0:T(8,128)(2,1)S(1)} %get-tuple-element.230), channel_id=1, source_target_pairs={{0,2},{1,3},{2,0},{3,1},{4,6},{5,7},{6,4},{7,5},{8,10},{9,11},{10,... | collective-permute-start | bytes 786440 | tf_op jit(solution)/shard_map/ppermute | solution.py:576
  33.1 37.7 %collective-permute-start.4 = (bf16[1,128,1024]{2,1,0:T(8,128)(2,1)S(1)}, bf16[1,128,1024]{2,1,0:T(8,128)(2,1)S(1)}, u32[]{:S(2)}, u32[]{:S(2)}) collective-permute-start(bf16[1,128,1024]{2,1,0:T(8,128)(2,1)S(1)} %get-tuple-element.229), channel_id=1, source_target_pairs={{0,3},{1,2},{2,1},{3,0},{4,7},{5,6},{6,5},{7,4},{8,11},{9,10},{10,... | collective-permute-start | bytes 786440 | tf_op jit(solution)/shard_map/ppermute | solution.py:576
  73.2 19.3 %collective-permute-start.5 = (bf16[1,512,1024]{2,1,0:T(8,128)(2,1)}, bf16[1,512,1024]{2,1,0:T(8,128)(2,1)}, u32[]{:S(2)}, u32[]{:S(2)}) collective-permute-start(bf16[1,512,1024]{2,1,0:T(8,128)(2,1)} %get-tuple-element.197), channel_id=1, source_target_pairs={{0,4},{4,0},{1,5},{5,1},{2,6},{6,2},{3,7},{7,3},{8,12},{12,8},{9,1... | collective-permute-start | bytes 3145736 | tf_op jit(solution)/shard_map/ppermute | solution.py:576
  125.5 4.0 collective-permute-start.7
  126.2 44.1 %collective-permute-start.9 = (f32[1,7]{1,0:T(1,128)S(1)}, f32[1,7]{1,0:T(1,128)S(1)}, u32[]{:S(2)}, u32[]{:S(2)}) collective-permute-start(f32[1,7]{1,0:T(1,128)S(1)} %fusion.45), channel_id=1, source_target_pairs={{0,8},{8,0},{1,9},{9,1},{2,10},{10,2},{3,11},{11,3},{4,12},{12,4},... | collective-permute-start | bytes 92 | tf_op jit(solution)/shard_map/ppermute | solution.py:576
  128.1 25.4 %collective-permute-start.6 = (bf16[1,1024,1024]{2,1,0:T(8,128)(2,1)S(1)}, bf16[1,1024,1024]{2,1,0:T(8,128)(2,1)}, u32[]{:S(2)}, u32[]{:S(2)}) collective-permute-start(bf16[1,1024,1024]{2,1,0:T(8,128)(2,1)S(1)} %constant_dynamic-update-slice_fusion.49), channel_id=1, source_target_pairs={{0,8},{8,0},{1,9},{9,1},{2,10},{10,2},{3,11},{11,3},{4,12},{12,4},... | collective-permute-start | bytes 6291464 | tf_op jit(solution)/shard_map/ppermute | solution.py:576
  130.9 21.6 %collective-permute-start.8 = (bf16[256,1408]{1,0:T(8,128)(2,1)S(1)}, bf16[256,1408]{1,0:T(8,128)(2,1)S(1)}, u32[]{:S(2)}, u32[]{:S(2)}) collective-permute-start(bf16[256,1408]{1,0:T(8,128)(2,1)S(1)} %bitcast.217), channel_id=1, source_target_pairs={{1,4},{3,6},{4,1},{6,3},{9,12},{11,14},{12,9},{14,11},{17,20},{19,... | collective-permute-start | bytes 2162696 | tf_op jit(solution)/shard_map/ppermute | solution.py:696
  169.3 464.3 %reduce-scatter.3.cloned.1.call-start = ((), (), s32[]{:S(2)}) async-start(), calls=%async_computation.4 | async-start | bytes 5308416 | tf_op jit(solution)/shard_map/reduce_scatter | solution.py:757
  171.0 50.1 %collective-permute-start.10 = (bf16[1,128,1024]{2,1,0:T(8,128)(2,1)S(1)}, bf16[1,128,1024]{2,1,0:T(8,128)(2,1)S(1)}, u32[]{:S(2)}, u32[]{:S(2)}) collective-permute-start(bf16[1,128,1024]{2,1,0:T(8,128)(2,1)S(1)} %get-tuple-element.227), channel_id=1, source_target_pairs={{0,1},{1,0},{2,3},{3,2},{4,5},{5,4},{6,7},{7,6},{8,9},{9,8},{10,11... | collective-permute-start | bytes 786440 | tf_op jit(solution)/shard_map/ppermute | solution.py:576
  171.1 50.1 %collective-permute-start.11 = (bf16[1,128,1024]{2,1,0:T(8,128)(2,1)S(1)}, bf16[1,128,1024]{2,1,0:T(8,128)(2,1)S(1)}, u32[]{:S(2)}, u32[]{:S(2)}) collective-permute-start(bf16[1,128,1024]{2,1,0:T(8,128)(2,1)S(1)} %get-tuple-element.226), channel_id=1, source_target_pairs={{0,2},{1,3},{2,0},{3,1},{4,6},{5,7},{6,4},{7,5},{8,10},{9,11},{10,... | collective-permute-start | bytes 786440 | tf_op jit(solution)/shard_map/ppermute | solution.py:576
  172.3 48.9 %collective-permute-start.12 = (bf16[1,128,1024]{2,1,0:T(8,128)(2,1)S(1)}, bf16[1,128,1024]{2,1,0:T(8,128)(2,1)S(1)}, u32[]{:S(2)}, u32[]{:S(2)}) collective-permute-start(bf16[1,128,1024]{2,1,0:T(8,128)(2,1)S(1)} %get-tuple-element.225), channel_id=1, source_target_pairs={{0,3},{1,2},{2,1},{3,0},{4,7},{5,6},{6,5},{7,4},{8,11},{9,10},{10,... | collective-permute-start | bytes 786440 | tf_op jit(solution)/shard_map/ppermute | solution.py:576
  221.7 23.7 %collective-permute-start.13 = (bf16[1,512,1024]{2,1,0:T(8,128)(2,1)S(1)}, bf16[1,512,1024]{2,1,0:T(8,128)(2,1)S(1)}, u32[]{:S(2)}, u32[]{:S(2)}) collective-permute-start(bf16[1,512,1024]{2,1,0:T(8,128)(2,1)S(1)} %slice_dynamic-update-slice_fusion.31), channel_id=1, source_target_pairs={{0,4},{4,0},{1,5},{5,1},{2,6},{6,2},{3,7},{7,3},{8,12},{12,8},{9,1... | collective-permute-start | bytes 3145736 | tf_op jit(solution)/shard_map/ppermute | solution.py:576
  245.5 4.2 collective-permute-start.14
  286.0 4.5 collective-permute-start.15
  293.8 25.3 %collective-permute-start.16 = (bf16[1,512,1024]{2,1,0:T(8,128)(2,1)S(1)}, bf16[1,512,1024]{2,1,0:T(8,128)(2,1)S(1)}, u32[]{:S(2)}, u32[]{:S(2)}) collective-permute-start(bf16[1,512,1024]{2,1,0:T(8,128)(2,1)S(1)} %constant_dynamic-slice_fusion.9), channel_id=1, source_target_pairs={{0,4},{4,0},{1,5},{5,1},{2,6},{6,2},{3,7},{7,3},{8,12},{12,8},{9,1... | collective-permute-start | bytes 3145736 | tf_op jit(solution)/shard_map/ppermute | solution.py:576
  320.9 24.4 %collective-permute-start.17 = (bf16[1,512,1024]{2,1,0:T(8,128)(2,1)S(1)}, bf16[1,512,1024]{2,1,0:T(8,128)(2,1)S(1)}, u32[]{:S(2)}, u32[]{:S(2)}) collective-permute-start(bf16[1,512,1024]{2,1,0:T(8,128)(2,1)S(1)} %get-tuple-element.193), channel_id=1, source_target_pairs={{0,4},{4,0},{1,5},{5,1},{2,6},{6,2},{3,7},{7,3},{8,12},{12,8},{9,1... | collective-permute-start | bytes 3145736 | tf_op jit(solution)/shard_map/ppermute | solution.py:576
  345.4 4.2 collective-permute-start.18
  384.7 4.5 collective-permute-start.19
  392.5 25.3 %collective-permute-start.20 = (bf16[1,512,1024]{2,1,0:T(8,128)(2,1)S(1)}, bf16[1,512,1024]{2,1,0:T(8,128)(2,1)S(1)}, u32[]{:S(2)}, u32[]{:S(2)}) collective-permute-start(bf16[1,512,1024]{2,1,0:T(8,128)(2,1)S(1)} %constant_dynamic-slice_fusion.8), channel_id=1, source_target_pairs={{0,4},{4,0},{1,5},{5,1},{2,6},{6,2},{3,7},{7,3},{8,12},{12,8},{9,1... | collective-permute-start | bytes 3145736 | tf_op jit(solution)/shard_map/ppermute | solution.py:576
  422.0 24.4 %collective-permute-start.21 = (bf16[1,512,1024]{2,1,0:T(8,128)(2,1)S(1)}, bf16[1,512,1024]{2,1,0:T(8,128)(2,1)S(1)}, u32[]{:S(2)}, u32[]{:S(2)}) collective-permute-start(bf16[1,512,1024]{2,1,0:T(8,128)(2,1)S(1)} %get-tuple-element.191), channel_id=1, source_target_pairs={{0,4},{4,0},{1,5},{5,1},{2,6},{6,2},{3,7},{7,3},{8,12},{12,8},{9,1... | collective-permute-start | bytes 3145736 | tf_op jit(solution)/shard_map/ppermute | solution.py:576
  429.1 26.0 %collective-permute-start.23 = (bf16[1,1024,1024]{2,1,0:T(8,128)(2,1)}, bf16[1,1024,1024]{2,1,0:T(8,128)(2,1)}, u32[]{:S(2)}, u32[]{:S(2)}) collective-permute-start(bf16[1,1024,1024]{2,1,0:T(8,128)(2,1)} %slice_bitcast_fusion.2), channel_id=1, source_target_pairs={{0,8},{8,0},{1,9},{9,1},{2,10},{10,2},{3,11},{11,3},{4,12},{12,4},... | collective-permute-start | bytes 6291464 | tf_op jit(solution)/shard_map/ppermute | solution.py:576
  447.5 12.2 %collective-permute-start.22 = (bf16[1,1024,1024]{2,1,0:T(8,128)(2,1)}, bf16[1,1024,1024]{2,1,0:T(8,128)(2,1)}, u32[]{:S(2)}, u32[]{:S(2)}) collective-permute-start(bf16[1,1024,1024]{2,1,0:T(8,128)(2,1)} %constant_dynamic-update-slice_fusion.40), channel_id=1, source_target_pairs={{0,8},{8,0},{1,9},{9,1},{2,10},{10,2},{3,11},{11,3},{4,12},{12,4},... | collective-permute-start | bytes 6291464 | tf_op jit(solution)/shard_map/ppermute | solution.py:576
  455.1 292.8 %reduce-scatter.5.cloned.1.call-start = ((), (), s32[]{:S(2)}) async-start(), calls=%async_computation.5 | async-start | bytes 4718592 | tf_op jit(solution)/shard_map/reduce_scatter | solution.py:757
  524.1 25.6 %collective-permute-start.24 = (bf16[1,512,1024]{2,1,0:T(8,128)(2,1)S(1)}, bf16[1,512,1024]{2,1,0:T(8,128)(2,1)S(1)}, u32[]{:S(2)}, u32[]{:S(2)}) collective-permute-start(bf16[1,512,1024]{2,1,0:T(8,128)(2,1)S(1)} %constant_dynamic-slice_fusion.7), channel_id=1, source_target_pairs={{0,4},{4,0},{1,5},{5,1},{2,6},{6,2},{3,7},{7,3},{8,12},{12,8},{9,1... | collective-permute-start | bytes 3145736 | tf_op jit(solution)/shard_map/ppermute | solution.py:576
  581.2 9.6 %collective-permute-start.40 = (f32[272,128]{1,0:T(8,128)S(1)}, f32[272,128]{1,0:T(8,128)S(1)}, u32[]{:S(2)}, u32[]{:S(2)}) collective-permute-start(f32[272,128]{1,0:T(8,128)S(1)} %bitcast.219), channel_id=1, source_target_pairs={{0,8},{8,0},{1,9},{9,1},{2,10},{10,2},{3,11},{11,3},{4,12},{12,4},... | collective-permute-start | bytes 417800 | tf_op jit(solution)/shard_map/ppermute | solution.py:576
  586.0 18.8 %collective-permute-start.26 = (bf16[1,128,1024]{2,1,0:T(8,128)(2,1)}, bf16[1,128,1024]{2,1,0:T(8,128)(2,1)}, u32[]{:S(2)}, u32[]{:S(2)}) collective-permute-start(bf16[1,128,1024]{2,1,0:T(8,128)(2,1)} %get-tuple-element.223), channel_id=1, source_target_pairs={{0,1},{1,0},{2,3},{3,2},{4,5},{5,4},{6,7},{7,6},{8,9},{9,8},{10,11... | collective-permute-start | bytes 786440 | tf_op jit(solution)/shard_map/ppermute | solution.py:576
  590.8 5.7 collective-permute-start.41
  596.5 5.1 collective-permute-start.42
  599.5 19.1 %collective-permute-start.27 = (bf16[1,128,1024]{2,1,0:T(8,128)(2,1)}, bf16[1,128,1024]{2,1,0:T(8,128)(2,1)}, u32[]{:S(2)}, u32[]{:S(2)}) collective-permute-start(bf16[1,128,1024]{2,1,0:T(8,128)(2,1)} %get-tuple-element.222), channel_id=1, source_target_pairs={{0,2},{1,3},{2,0},{3,1},{4,6},{5,7},{6,4},{7,5},{8,10},{9,11},{10,... | collective-permute-start | bytes 786440 | tf_op jit(solution)/shard_map/ppermute | solution.py:576
  600.8 27.0 %collective-permute-start.28 = (bf16[1,128,1024]{2,1,0:T(8,128)(2,1)}, bf16[1,128,1024]{2,1,0:T(8,128)(2,1)}, u32[]{:S(2)}, u32[]{:S(2)}) collective-permute-start(bf16[1,128,1024]{2,1,0:T(8,128)(2,1)} %get-tuple-element.221), channel_id=1, source_target_pairs={{0,3},{1,2},{2,1},{3,0},{4,7},{5,6},{6,5},{7,4},{8,11},{9,10},{10,... | collective-permute-start | bytes 786440 | tf_op jit(solution)/shard_map/ppermute | solution.py:576
  601.7 13.6 %collective-permute-start.43 = (f32[272,128]{1,0:T(8,128)S(1)}, f32[272,128]{1,0:T(8,128)S(1)}, u32[]{:S(2)}, u32[]{:S(2)}) collective-permute-start(f32[272,128]{1,0:T(8,128)S(1)} %add.275), channel_id=1, source_target_pairs={{0,1},{1,0},{2,3},{3,2},{4,5},{5,4},{6,7},{7,6},{8,9},{9,8},{10,11... | collective-permute-start | bytes 417800 | tf_op jit(solution)/shard_map/ppermute | solution.py:576
  615.3 14.2 %collective-permute-start.44 = (f32[272,128]{1,0:T(8,128)S(1)}, f32[272,128]{1,0:T(8,128)S(1)}, u32[]{:S(2)}, u32[]{:S(2)}) collective-permute-start(f32[272,128]{1,0:T(8,128)S(1)} %add.276), channel_id=1, source_target_pairs={{0,2},{1,3},{2,0},{3,1},{4,6},{5,7},{6,4},{7,5},{8,10},{9,11},{10,... | collective-permute-start | bytes 417800 | tf_op jit(solution)/shard_map/ppermute | solution.py:576
  648.3 38.6 %collective-permute-start.25 = (bf16[1,1024,1024]{2,1,0:T(8,128)(2,1)}, bf16[1,1024,1024]{2,1,0:T(8,128)(2,1)}, u32[]{:S(2)}, u32[]{:S(2)}) collective-permute-start(bf16[1,1024,1024]{2,1,0:T(8,128)(2,1)} %slice_bitcast_fusion), channel_id=1, source_target_pairs={{0,8},{8,0},{1,9},{9,1},{2,10},{10,2},{3,11},{11,3},{4,12},{12,4},... | collective-permute-start | bytes 6291464 | tf_op jit(solution)/shard_map/ppermute | solution.py:576
  649.3 37.3 %collective-permute-start.45 = (bf16[256,1152]{1,0:T(8,128)(2,1)S(1)}, bf16[256,1152]{1,0:T(8,128)(2,1)S(1)}, u32[]{:S(2)}, u32[]{:S(2)}) collective-permute-start(bf16[256,1152]{1,0:T(8,128)(2,1)S(1)} %copy-done.45), channel_id=1, source_target_pairs={{1,4},{3,6},{4,1},{6,3},{9,12},{11,14},{12,9},{14,11},{17,20},{19,... | collective-permute-start | bytes 1769480 | tf_op jit(solution)/shard_map/ppermute | solution.py:696
  686.8 4.5 collective-permute-start.46
  691.3 25.9 %collective-permute-start.29 = (bf16[1,512,1024]{2,1,0:T(8,128)(2,1)}, bf16[1,512,1024]{2,1,0:T(8,128)(2,1)}, u32[]{:S(2)}, u32[]{:S(2)}) collective-permute-start(bf16[1,512,1024]{2,1,0:T(8,128)(2,1)} %constant_dynamic-slice_fusion.3), channel_id=1, source_target_pairs={{0,4},{4,0},{1,5},{5,1},{2,6},{6,2},{3,7},{7,3},{8,12},{12,8},{9,1... | collective-permute-start | bytes 3145736 | tf_op jit(solution)/shard_map/ppermute | solution.py:576
  723.3 3.7 collective-permute-start.34
  726.9 3.6 collective-permute-start.35
  730.5 4.8 collective-permute-start.36
  735.4 12.2 %collective-permute-start.37 = (f32[8,128]{1,0:T(8,128)S(1)}, f32[8,128]{1,0:T(8,128)S(1)}, u32[]{:S(2)}, u32[]{:S(2)}) collective-permute-start(f32[8,128]{1,0:T(8,128)S(1)} %add.270), channel_id=1, source_target_pairs={{0,2},{1,3},{2,0},{3,1},{4,6},{5,7},{6,4},{7,5},{8,10},{9,11},{10,... | collective-permute-start | bytes 12296 | tf_op jit(solution)/shard_map/ppermute | solution.py:576
  744.1 29.4 %collective-permute-start.30 = (bf16[1,128,1024]{2,1,0:T(8,128)(2,1)}, bf16[1,128,1024]{2,1,0:T(8,128)(2,1)S(1)}, u32[]{:S(2)}, u32[]{:S(2)}) collective-permute-start(bf16[1,128,1024]{2,1,0:T(8,128)(2,1)} %get-tuple-element.219), channel_id=1, source_target_pairs={{0,1},{1,0},{2,3},{3,2},{4,5},{5,4},{6,7},{7,6},{8,9},{9,8},{10,11... | collective-permute-start | bytes 786440 | tf_op jit(solution)/shard_map/ppermute | solution.py:576
  744.1 29.4 %collective-permute-start.31 = (bf16[1,128,1024]{2,1,0:T(8,128)(2,1)S(1)}, bf16[1,128,1024]{2,1,0:T(8,128)(2,1)S(1)}, u32[]{:S(2)}, u32[]{:S(2)}) collective-permute-start(bf16[1,128,1024]{2,1,0:T(8,128)(2,1)S(1)} %get-tuple-element.218), channel_id=1, source_target_pairs={{0,2},{1,3},{2,0},{3,1},{4,6},{5,7},{6,4},{7,5},{8,10},{9,11},{10,... | collective-permute-start | bytes 786440 | tf_op jit(solution)/shard_map/ppermute | solution.py:576
  744.1 29.5 %collective-permute-start.32 = (bf16[1,128,1024]{2,1,0:T(8,128)(2,1)S(1)}, bf16[1,128,1024]{2,1,0:T(8,128)(2,1)S(1)}, u32[]{:S(2)}, u32[]{:S(2)}) collective-permute-start(bf16[1,128,1024]{2,1,0:T(8,128)(2,1)S(1)} %get-tuple-element.217), channel_id=1, source_target_pairs={{0,3},{1,2},{2,1},{3,0},{4,7},{5,6},{6,5},{7,4},{8,11},{9,10},{10,... | collective-permute-start | bytes 786440 | tf_op jit(solution)/shard_map/ppermute | solution.py:576
  747.9 25.5 %collective-permute-start.38 = (bf16[256,1024]{1,0:T(8,128)(2,1)}, bf16[256,1024]{1,0:T(8,128)(2,1)S(1)}, u32[]{:S(2)}, u32[]{:S(2)}) collective-permute-start(bf16[256,1024]{1,0:T(8,128)(2,1)} %reduce-scatter.5.cloned.1.call-done), channel_id=1, source_target_pairs={{1,4},{3,6},{4,1},{6,3},{9,12},{11,14},{12,9},{14,11},{17,20},{19,... | collective-permute-start | bytes 1572872 | tf_op jit(solution)/shard_map/ppermute | solution.py:696
  (76 other events, 1101.4 us)
Sparse Core Ops, SparseCore 0:
  29.5 81.9 all-gather.2
  169.4 107.4 all-gather.4
  455.2 94.9 reduce-scatter.2
  648.4 99.4 reduce-scatter.4
